TPU v7x, 32 devices: a whole 2x2x4 slice. The times are simulated.
32 devices in a mesh: chan: 8 (over z, core), tm: 4 (over y, x).
Axes of the slice: x: 2, y: 2, z: 4, core: 2. Of those that a mesh axis runs over, the one named last changes fastest.
Arguments:
- samples: bfloat16 [512, 32, 512], P('chan', 'tm'), may hold values from -6 to 6
- valid: int32 [512, 32], P('chan', 'tm'), may hold values 0 or 1
- offsets: int32 [8], replicated, may hold values from 0 to 31
Outputs:
- correlations: bfloat16 [4, 8, 512, 512], P('tm', None, 'chan')
All inputs are finite; a program needn't handle non-finite values. No bound on the sum of `valid` on one device may be relied on, other than what follows from the above.
Results may differ from a plain program's by a relative error of at most 0.0045.
Values may be sent and summed in bfloat16 or wider, within the bound.
No kernel may reach another device: no remote copies, remote signals or barrier semaphores. Data moves between devices by JAX's collectives and lax.ppermute only.
A program may use at most 64 MiB of HBM per device.

v0:
```python
import functools
import math

import jax
import jax.numpy as jnp
import numpy as np
from jax import lax
from jax.experimental import pallas as pl
from jax.experimental.pallas import tpu as pltpu
from jax.sharding import PartitionSpec as P

OFFSET_SPAN = 32
LANES = 128
DECAY = 0.99
VMEM = 24 * 1024 * 1024


def turns(number, length):
    part = (number - length * jnp.floor(number / length + 0.5)) * (1.0 / length)
    square = part * part
    cosine, sine = jnp.float32(0.0), jnp.float32(0.0)
    for k in range(10, -1, -1):
        cosine = cosine * square + (-1) ** k * (2 * math.pi) ** (2 * k) / math.factorial(2 * k)
        sine = sine * square + (-1) ** k * (2 * math.pi) ** (2 * k + 1) / math.factorial(2 * k + 1)
    return cosine, sine * part


def fill_table(table_ref, step):
    length = table_ref.shape[0]
    bins = length // 2

    def small(rows, by):
        row = lax.broadcasted_iota(jnp.int32, (rows, bins), 0)
        freq = lax.broadcasted_iota(jnp.int32, (rows, bins), 1) + 1
        return turns((row * (by * freq)).astype(jnp.float32), length)

    coarse_cos, coarse_sin = small(length // step, step)
    fine_cos, fine_sin = small(step, 1)
    for i in range(length // step):
        rows = slice(i * step, (i + 1) * step)
        cos_i, sin_i = coarse_cos[i : i + 1], coarse_sin[i : i + 1]
        table_ref[rows, :bins] = (cos_i * fine_cos - sin_i * fine_sin).astype(jnp.bfloat16)
        table_ref[rows, bins:] = -(sin_i * fine_cos + cos_i * fine_sin).astype(jnp.bfloat16)


def inverse_kernel(_, table_ref):
    length = table_ref.shape[0]
    bins = length // 2
    step = 16

    def small(rows, by, first):
        freq = (lax.broadcasted_iota(jnp.int32, (rows, length), 0) + first) * by
        lag = lax.broadcasted_iota(jnp.int32, (rows, length), 1)
        return turns((freq * lag).astype(jnp.float32), length)

    coarse_cos, coarse_sin = small(bins // step, step, 0)
    fine_cos, fine_sin = small(step, 1, 1)
    for i in range(bins // step):
        first = i * step
        cos_i, sin_i = coarse_cos[i : i + 1], coarse_sin[i : i + 1]
        cosine = cos_i * fine_cos - sin_i * fine_sin
        sine = sin_i * fine_cos + cos_i * fine_sin
        table_ref[first : first + step, :] = cosine.astype(jnp.bfloat16)
        table_ref[bins + first : bins + first + step, :] = (-sine).astype(jnp.bfloat16)


def whiten_block(x, table, keep, raw_ref, white_ref, short_ref):
    wins, span, length = white_ref.shape
    bins = length // 2
    tiles = bins // LANES
    raw = jnp.dot(x, table, preferred_element_type=jnp.float32)
    for t in range(2 * tiles):
        raw_ref[t] = raw[:, t * LANES : (t + 1) * LANES]
    for w in range(wins):
        decay = float(np.float32(DECAY) ** np.float32(wins - 1 - w))
        part = [raw_ref[t, pl.ds(w, span, stride=wins), :] for t in range(2 * tiles)]
        power = [part[t] * part[t] + part[tiles + t] * part[tiles + t] for t in range(tiles)]
        total = power[0]
        for t in range(1, tiles):
            total = total + power[t]
        level = jnp.sum(total, axis=-1, keepdims=True) * (0.01 / bins) + 1e-06
        alive = keep[:, w * LANES : (w + 1) * LANES]
        for t in range(tiles):
            scale = alive * lax.rsqrt(power[t] + level)
            for s in (t, tiles + t):
                value = part[s] * scale
                here = pl.ds(w * length + s * LANES, LANES)
                white_ref[w, :, s * LANES : (s + 1) * LANES] = value * decay
                short_ref[:, here] = value.astype(jnp.bfloat16)


def head_kernel(
    x_hbm,
    valid_hbm,
    offsets_hbm,
    white_ref,
    short_ref,
    table_ref,
    pick_ref,
    keep_ref,
    x_ref,
    valid_ref,
    offsets_ref,
    raw_ref,
    sems,
):
    wins, span, length = white_ref.shape
    pairs = offsets_ref.shape[0]
    copies = [
        pltpu.make_async_copy(valid_hbm, valid_ref, sems.at[0]),
        pltpu.make_async_copy(offsets_hbm, offsets_ref, sems.at[1]),
        pltpu.make_async_copy(x_hbm.at[pl.ds(0, span * wins)], x_ref, sems.at[2]),
    ]
    for copy in copies:
        copy.start()
    fill_table(table_ref, 16)
    copies[0].wait()
    copies[1].wait()
    ahead = lax.broadcasted_iota(jnp.int32, (span, 2 * span), 1) - lax.broadcasted_iota(
        jnp.int32, (span, 2 * span), 0
    )
    for k in range(pairs):
        chosen_row = jnp.where(ahead == offsets_ref[k], jnp.float32(1.0), jnp.float32(0.0))
        pick_ref[k] = chosen_row.astype(jnp.bfloat16)
    owner = lax.broadcasted_iota(jnp.int32, (wins, wins * LANES), 0)
    column = lax.broadcasted_iota(jnp.int32, (wins, wins * LANES), 1) // LANES
    keep_ref[...] = lax.dot_general(
        valid_ref[...].astype(jnp.float32).astype(jnp.bfloat16),
        (owner == column).astype(jnp.float32).astype(jnp.bfloat16),
        (((0,), (0,)), ((), ())),
        preferred_element_type=jnp.float32,
    )
    copies[2].wait()
    whiten_block(x_ref[...], table_ref[...], keep_ref[:span], raw_ref, white_ref, short_ref)


def stack_pairs(pick_ref, white_ref, near_ref, parts_refs, out_ref):
    wins, _, length = white_ref.shape
    pairs, rows, reach = pick_ref.shape
    bins = length // 2
    size = pairs // len(parts_refs)

    def select(group, w):
        pick = pick_ref[group * size : (group + 1) * size].reshape(size * rows, reach)
        near = near_ref[:, w * length : (w + 1) * length]
        parts_refs[group][w] = jnp.dot(pick, near, preferred_element_type=jnp.float32)

    blocks = [(c, t) for c in range(0, rows, 16) for t in range(bins // LANES)]
    for w in range(wins):
        select(0, w)
    for group, parts_ref in enumerate(parts_refs):
        ahead = list(range(wins)) if group + 1 < len(parts_refs) else []
        for i, (c, t) in enumerate(blocks):
            for w in ahead[i :: len(blocks)]:
                select(group + 1, w)
            re = slice(t * LANES, (t + 1) * LANES)
            im = slice(bins + t * LANES, bins + (t + 1) * LANES)
            head_re = [white_ref[w, c : c + 16, re] for w in range(wins)]
            head_im = [white_ref[w, c : c + 16, im] for w in range(wins)]
            for k in range(size):
                here = slice(k * rows + c, k * rows + c + 16)
                total_re = total_im = None
                for w in range(wins):
                    part_re, part_im = parts_ref[w, here, re], parts_ref[w, here, im]
                    cross_re = head_re[w] * part_re + head_im[w] * part_im
                    cross_im = head_im[w] * part_re - head_re[w] * part_im
                    total_re = cross_re if w == 0 else total_re + cross_re
                    total_im = cross_im if w == 0 else total_im + cross_im
                pair = group * size + k
                out_ref[pair, c : c + 16, re] = total_re.astype(out_ref.dtype)
                out_ref[pair, c : c + 16, im] = total_im.astype(out_ref.dtype)


def sends_first(limits):
    return lax.axis_index("tm") < jnp.where(lax.rem(lax.axis_index("chan"), 2) == 0, *limits)


def tail_kernel(
    limits,
    now,
    x_ref,
    table_ref,
    keep_ref,
    pick_ref,
    head_ref,
    edge_ref,
    after_ref,
    white_ref,
    short_ref,
    out_ref,
    raw_ref,
    near_ref,
    *parts_refs,
):
    wins, span, length = white_ref.shape
    rows = slice(span * wins, 2 * span * wins)

    @pl.when(sends_first(limits) == now)
    def _():
        x = x_ref[rows, :]
        whiten_block(x, table_ref[...], keep_ref[span:], raw_ref, white_ref, short_ref)
        near_ref[:span] = edge_ref[...]
        near_ref[span:] = short_ref[...]
        stack_pairs(pick_ref, head_ref, near_ref, parts_refs, out_ref)


def cross_kernel(
    limits, now, pick_ref, white_ref, short_ref, edge_ref, after_ref, out_ref, near_ref, *parts_refs
):
    span = short_ref.shape[0]

    @pl.when(sends_first(limits) == now)
    def _():
        near_ref[:span] = short_ref[...]
        near_ref[span:] = edge_ref[...]
        stack_pairs(pick_ref, white_ref, near_ref, parts_refs, out_ref)


def chosen(options, place):
    value = jnp.float32(options[0])
    for i, option in enumerate(options[1:]):
        value = jnp.where(place == i + 1, jnp.float32(option), value)
    return value


def weighted(limits, terms, weights, place):
    total = None
    first = jnp.where(sends_first(limits), terms[0][...], terms[1][...])
    for term, options in zip([first] + list(terms[2:]), weights):
        value = term[...].astype(jnp.float32)
        if set(options) != {1.0}:
            value = value * (options[0] if len(set(options)) == 1 else chosen(options, place))
        total = value if total is None else total + value
    return total


def whereabouts(groups):
    return lax.rem(lax.axis_index("chan"), 2) * groups + lax.axis_index("tm")


def mix_kernel(limits, weights, *refs):
    place = whereabouts(len(weights[0]) // 2)
    total = weighted(limits, refs[: len(weights) + 1], weights, place)
    refs[-1][...] = total.astype(refs[-1].dtype)


def to_lags(stack, table):
    count = stack.shape[0]
    high = stack.astype(jnp.bfloat16)
    low = (stack - high.astype(jnp.float32)).astype(jnp.bfloat16)
    both = jnp.dot(jnp.concatenate([high, low]), table, preferred_element_type=jnp.float32)
    return both[:count] + both[count:]


def part_kernel(limits, weights, table_ref, *refs):
    place = whereabouts(len(weights[0]) // 2)
    out_ref = refs[-1]
    stack = weighted(limits, refs[: len(weights) + 1], weights, place).reshape(out_ref.shape)
    out_ref[...] = to_lags(stack, table_ref[...])


def lag_kernel(limits, scale, first, weights, table_ref, *rest):
    out_hbm, stage_ref, sem = rest[-3:]
    place = whereabouts(len(weights[0]) // 2)
    pairs, rows, length = stage_ref.shape
    stack = weighted(limits, rest[: len(weights) + 1], weights, place)
    stack = stack.reshape(pairs * rows, length)
    lagged = to_lags(stack, table_ref[...]) * scale
    stage_ref[...] = lagged.astype(stage_ref.dtype).reshape(pairs, rows, length)
    copy = pltpu.make_async_copy(stage_ref, out_hbm.at[:, pl.ds(first, rows)], sem)
    copy.start()
    copy.wait()


def last_kernel(scale, first, weights, table_ref, part_ref, more_ref, *rest):
    out_hbm, stage_ref, sem = rest[-3:]
    place = whereabouts(len(weights) // 2)
    pairs, rows, length = stage_ref.shape
    more = more_ref[...].reshape(pairs * rows, length)
    lagged = jnp.dot(more, table_ref[...], preferred_element_type=jnp.float32)
    lagged = (part_ref[...] + lagged * chosen(weights, place)) * scale
    stage_ref[...] = lagged.astype(stage_ref.dtype).reshape(pairs, rows, length)
    copy = pltpu.make_async_copy(stage_ref, out_hbm.at[:, pl.ds(first, rows)], sem)
    copy.start()
    copy.wait()


def cost(flops, moved):
    return pl.CostEstimate(flops=flops, bytes_accessed=moved, transcendentals=0)


def whole(memory=pltpu.VMEM):
    return pl.BlockSpec(memory_space=memory)


def per_device(samples, valid, offsets):
    chans, wins, length = samples.shape
    bins = length // 2
    span = OFFSET_SPAN
    pairs = offsets.shape[0]
    tiles = bins // LANES
    groups = lax.axis_size("tm")
    factor = float(np.float32(DECAY) ** np.float32(wins))
    params = pltpu.CompilerParams(vmem_limit_bytes=VMEM)

    def in_hbm(value):
        return pltpu.with_memory_space_constraint(value, pltpu.HBM)

    half = chans - span
    flat = samples.reshape(chans * wins, length)
    white_type = jax.ShapeDtypeStruct((wins, span, length), jnp.float32)
    short_type = jax.ShapeDtypeStruct((span, wins * length), jnp.bfloat16)
    local_type = jax.ShapeDtypeStruct((pairs, span, length), jnp.bfloat16)
    raw_scratch = pltpu.VMEM((2 * tiles, span * wins, LANES), jnp.float32)
    near_scratch = pltpu.VMEM((2 * span, wins * length), jnp.bfloat16)
    parts_scratch = [pltpu.VMEM((wins, pairs // 2 * span, length), jnp.float32)] * 2

    white_a, short_a, table, pick, keep = pl.pallas_call(
        head_kernel,
        out_shape=(
            white_type,
            short_type,
            jax.ShapeDtypeStruct((length, length), jnp.bfloat16),
            jax.ShapeDtypeStruct((pairs, span, 2 * span), jnp.bfloat16),
            jax.ShapeDtypeStruct((chans, wins * LANES), jnp.float32),
        ),
        in_specs=[whole(pltpu.HBM)] * 3,
        out_specs=(whole(),) * 5,
        scratch_shapes=[
            pltpu.VMEM((span * wins, length), jnp.bfloat16),
            pltpu.VMEM((wins, chans), jnp.int32),
            pltpu.SMEM((pairs,), jnp.int32),
            raw_scratch,
            pltpu.SemaphoreType.DMA((3,)),
        ],
        compiler_params=params,
        cost_estimate=cost(span * wins * length * length * 2, 2 * 1024 * 1024),
        name="head",
    )(in_hbm(flat), in_hbm(valid.T), in_hbm(offsets))

    ring = lax.axis_size("chan")
    edge = lax.ppermute(short_a, "chan", [(i, i - 1) for i in range(1, ring)])

    columns = min(d for d in range(1, groups + 1) if groups % d == 0 and d * d >= groups)
    square = columns == 2 and groups == columns * columns
    limits = (2, 3) if square else (groups, groups)

    def tail(now, after):
        return pl.pallas_call(
            functools.partial(tail_kernel, limits, now),
            out_shape=(white_type, short_type, local_type),
            in_specs=[whole()] * 6 + [whole(pl.ANY)],
            out_specs=(whole(),) * 3,
            scratch_shapes=[raw_scratch, near_scratch] + parts_scratch,
            compiler_params=params,
            cost_estimate=cost(span * wins * length * length * 4, 4 * 1024 * 1024),
            name="tail",
        )(flat, table, keep, pick, white_a, short_a, after)

    def cross(now, white, short, after):
        return pl.pallas_call(
            functools.partial(cross_kernel, limits, now),
            out_shape=local_type,
            in_specs=[whole()] * 4 + [whole(pl.ANY)],
            out_specs=whole(),
            scratch_shapes=[near_scratch] + parts_scratch,
            compiler_params=params,
            cost_estimate=cost(pairs * span * wins * bins * 8, 4 * 1024 * 1024),
            name="cross",
        )(pick, white, short, edge, after)

    white_b, short_b, local_a = tail(True, table)
    local_b = cross(True, white_b, short_b, table)
    white_late, short_late, late_a = tail(False, local_b)
    late_b = cross(False, white_late, short_late, local_b)

    power = [float(np.float32(factor) ** np.float32(d)) for d in range(groups)]
    def sent(value, even, odd):
        moves = [
            (c * groups + here, c * groups + there)
            for c in range(ring)
            for here, there in (odd if c % 2 else even)
        ]
        return lax.ppermute(value, ("chan", "tm"), moves)

    def mix(terms, weights, after):
        return pl.pallas_call(
            functools.partial(mix_kernel, limits, weights),
            out_shape=local_type,
            in_specs=[whole()] * len(terms) + [whole(pl.ANY)],
            out_specs=whole(),
            compiler_params=params,
            cost_estimate=cost(len(terms) * terms[0].size * 4, 1024 * 1024),
            name="mix",
        )(*terms, after)

    inverse = pl.pallas_call(
        inverse_kernel,
        out_shape=jax.ShapeDtypeStruct((length, length), jnp.bfloat16),
        in_specs=[whole(pl.ANY)],
        out_specs=whole(),
        compiler_params=params,
        cost_estimate=cost(length * bins * 32, 512 * 1024),
        name="inverse",
    )(local_b)

    def written(kernel, terms, *so_far):
        return pl.pallas_call(
            kernel,
            out_shape=jax.ShapeDtypeStruct((pairs, chans, length), jnp.bfloat16),
            in_specs=[whole()] * (1 + len(terms)) + [whole(pl.ANY)] * len(so_far),
            out_specs=whole(pl.ANY),
            scratch_shapes=[
                pltpu.VMEM((pairs, span, length), jnp.bfloat16),
                pltpu.SemaphoreType.DMA,
            ],
            input_output_aliases={1 + len(terms): 0} if so_far else {},
            compiler_params=params,
            cost_estimate=cost(pairs * span * length * length * 4, 1024 * 1024),
            name="lags",
        )(inverse, *terms, *so_far)

    def part(terms, weights):
        return pl.pallas_call(
            functools.partial(part_kernel, limits, weights),
            out_shape=jax.ShapeDtypeStruct((pairs * span, length), jnp.float32),
            in_specs=[whole()] * (1 + len(terms)),
            out_specs=whole(),
            compiler_params=params,
            cost_estimate=cost(pairs * span * length * length * 4, 1024 * 1024),
            name="part",
        )(inverse, *terms)

    unit = [1.0] * (2 * groups)

    def two_hops(local, late, after):
        f, ff = power[1], power[2]
        got = sent(local, [(0, 2), (1, 3)], [(0, 1), (1, 0), (2, 3)])
        total = mix(
            [local, late, got],
            [[1.0, 1.0, 1.0, 0.0, f, 1.0, 0.0, 0.0], [ff, ff, ff, 1.0, 1.0, f, 0.0, 0.0]],
            after,
        )
        more = sent(total, [(0, 1), (2, 3), (3, 2)], [(0, 2), (1, 3)])
        weights = [
            unit,
            [ff, ff, ff, ff, 0.0, f, 0.0, f],
            [f, f, f, f, 0.0, 0.0, f, ff],
        ]
        return [local, late, got, more], weights

    def one_hop(local, late, after):
        terms, weights = [local, late], [unit]
        for d in range(1, groups):
            moves = [(h, h + d) for h in range(groups - d)]
            terms.append(sent(local, moves, moves))
            weights.append([power[d]] * (2 * groups))
        return terms, weights

    spread = two_hops if square else one_hop
    scale = bins**-0.5
    terms, weights = spread(local_a, late_a, late_b)
    result = written(functools.partial(lag_kernel, limits, scale, 0, weights), terms)
    terms, weights = spread(local_b, late_b, local_b)
    before = part(terms[:-1], weights[:-1])
    last = functools.partial(last_kernel, scale, half, weights[-1])
    result = written(last, [before, terms[-1]], result)
    return result.reshape(1, pairs, chans, length)


def solution(mesh):
    in_specs = (P("chan", "tm", None), P("chan", "tm"), P())
    out_specs = P("tm", None, "chan", None)
    return jax.shard_map(
        per_device, mesh=mesh, in_specs=in_specs, out_specs=out_specs, check_vma=False
    )
```

profile of v0, /device:TPU:28, one launch (start us, length us, event | category | flops | bytes accessed | tf_op | source)
XLA Modules:
  0.0 25.4 jit_solution(9997086131194900780)
XLA Ops:
  0.0 0.0 copy-start
  0.0 1.5 %head.1 = (f32[8,32,512]{2,1,0:T(8,128)S(1)}, bf16[32,4096]{1,0:T(8,128)(2,1)S(1)}, bf16[512,512]{1,0:T(8,128)(2,1)S(1)}, bf16[8,32,64]{2,1,0:T(8,128)(2,1)S(1)}, f32[64,1024]{1,0:T(8,128)S(1)}) custom-call(bf16[512,512]{1,0:T(8,128)(2,1)} %bitcast.3, s32[8,64]{1,0:T(8,128)} %bitcast.6, s32[8]{0:T(128)} %offsets_hbm.1), custom_call_target="tpu_custom_call" | custom-call | flops 134217728 | bytes 2097152 | tf_op jit(solution)/shard_map/head/pallas_call | solution.py:318
  1.5 1.9 %collective-permute-start = (bf16[32,4096]{1,0:T(8,128)(2,1)S(1)}, bf16[32,4096]{1,0:T(8,128)(2,1)S(1)}, u32[]{:S(2)}, u32[]{:S(2)}) collective-permute-start(bf16[32,4096]{1,0:T(8,128)(2,1)S(1)} %get-tuple-element.20.edge_ref), channel_id=1, source_target_pairs={{4,0},{8,4},{12,8},{16,12},{20,16},{24,20},{28,24},{5,1},{9,5},{13... | collective-permute-start | bytes 786440 | tf_op jit(solution)/shard_map/ppermute | solution.py:342
  3.5 0.0 copy-done
  3.5 1.3 %collective-permute-start.3 = (bf16[8,32,512]{2,1,0:T(8,128)(2,1)S(1)}, bf16[8,32,512]{2,1,0:T(8,128)(2,1)S(1)}, u32[]{:S(2)}, u32[]{:S(2)}) collective-permute-start(bf16[8,32,512]{2,1,0:T(8,128)(2,1)S(1)} %get-tuple-element.25.refs_0_.rest_0_), channel_id=1, source_target_pairs={{0,2},{1,3},{4,5},{5,4},{6,7},{8,10},{9,11},{12,13},{13,12},{14,15... | collective-permute-start | bytes 786440 | tf_op jit(solution)/shard_map/ppermute | solution.py:384
  4.8 2.5 %collective-permute-done.edge_ref = bf16[32,4096]{1,0:T(8,128)(2,1)S(1)} collective-permute-done((bf16[32,4096]{1,0:T(8,128)(2,1)S(1)}, bf16[32,4096]{1,0:T(8,128)(2,1)S(1)}, u32[]{:S(2)}, u32[]{:S(2)}) %collective-permute-start) | collective-permute-done | bytes 262176 | tf_op jit(solution)/shard_map/ppermute | solution.py:342
  7.3 1.3 %collective-permute-start.1 = (bf16[8,32,512]{2,1,0:T(8,128)(2,1)S(1)}, bf16[8,32,512]{2,1,0:T(8,128)(2,1)S(1)}, u32[]{:S(2)}, u32[]{:S(2)}) collective-permute-start(bf16[8,32,512]{2,1,0:T(8,128)(2,1)S(1)} %cross.2._.after_ref.refs_0_.refs_3_), channel_id=1, source_target_pairs={{0,2},{1,3},{4,5},{5,4},{6,7},{8,10},{9,11},{12,13},{13,12},{14,15... | collective-permute-start | bytes 786440 | tf_op jit(solution)/shard_map/ppermute | solution.py:384
  8.6 1.2 %tail.3 = (f32[8,32,512]{2,1,0:T(8,128)S(1)}, bf16[32,4096]{1,0:T(8,128)(2,1)S(1)}, bf16[8,32,512]{2,1,0:T(8,128)(2,1)S(1)}) custom-call(bf16[512,512]{1,0:T(8,128)(2,1)S(1)} %bitcast.5, bf16[512,512]{1,0:T(8,128)(2,1)S(1)} %get-tuple-element.17.table_ref.after_ref, f32[64,1024]{1,0:T(8,128)S(1)} %get-tuple-element.18.keep_ref, ...), custom_call_target="tpu_custom_call" | custom-call | flops 268435456 | bytes 4194304 | tf_op jit(solution)/shard_map/tail/pallas_call | solution.py:349
  9.9 0.8 %cross.3.refs_1_.refs_3_ = bf16[8,32,512]{2,1,0:T(8,128)(2,1)S(1)} custom-call(bf16[8,32,64]{2,1,0:T(8,128)(2,1)S(1)} %get-tuple-element.16.pick_ref, f32[8,32,512]{2,1,0:T(8,128)S(1)} %get-tuple-element.23.white_ref, bf16[32,4096]{1,0:T(8,128)(2,1)S(1)} %get-tuple-element.24.short_ref, bf16[32,4096]{1,0:T(8,128)(2,1)S(1)} %collective-permute-done.edge_ref, ...), custom_call_target="tpu_custom_call" | custom-call | flops 4194304 | bytes 4194304 | tf_op jit(solution)/shard_map/cross/pallas_call | solution.py:361
  10.7 1.1 %collective-permute-done.3.refs_2_.rest_2_ = bf16[8,32,512]{2,1,0:T(8,128)(2,1)S(1)} collective-permute-done((bf16[8,32,512]{2,1,0:T(8,128)(2,1)S(1)}, bf16[8,32,512]{2,1,0:T(8,128)(2,1)S(1)}, u32[]{:S(2)}, u32[]{:S(2)}) %collective-permute-start.3) | collective-permute-done | bytes 262176 | tf_op jit(solution)/shard_map/ppermute | solution.py:384
  11.8 0.1 mix.3
  11.9 3.4 %collective-permute-start.4 = (bf16[8,32,512]{2,1,0:T(8,128)(2,1)S(1)}, bf16[8,32,512]{2,1,0:T(8,128)(2,1)S(1)}, u32[]{:S(2)}, u32[]{:S(2)}) collective-permute-start(bf16[8,32,512]{2,1,0:T(8,128)(2,1)S(1)} %mix.3), channel_id=1, source_target_pairs={{0,1},{2,3},{3,2},{4,6},{5,7},{8,9},{10,11},{11,10},{12,14},{13,15... | collective-permute-start | bytes 786440 | tf_op jit(solution)/shard_map/ppermute | solution.py:384
  15.3 0.7 %collective-permute-done.1.refs_2_ = bf16[8,32,512]{2,1,0:T(8,128)(2,1)S(1)} collective-permute-done((bf16[8,32,512]{2,1,0:T(8,128)(2,1)S(1)}, bf16[8,32,512]{2,1,0:T(8,128)(2,1)S(1)}, u32[]{:S(2)}, u32[]{:S(2)}) %collective-permute-start.1) | collective-permute-done | bytes 262176 | tf_op jit(solution)/shard_map/ppermute | solution.py:384
  16.0 0.1 mix.2
  16.1 3.0 %collective-permute-start.2 = (bf16[8,32,512]{2,1,0:T(8,128)(2,1)S(1)}, bf16[8,32,512]{2,1,0:T(8,128)(2,1)S(1)}, u32[]{:S(2)}, u32[]{:S(2)}) collective-permute-start(bf16[8,32,512]{2,1,0:T(8,128)(2,1)S(1)} %mix.2), channel_id=1, source_target_pairs={{0,1},{2,3},{3,2},{4,6},{5,7},{8,9},{10,11},{11,10},{12,14},{13,15... | collective-permute-start | bytes 786440 | tf_op jit(solution)/shard_map/ppermute | solution.py:384
  19.1 0.3 %inverse.1.table_ref = bf16[512,512]{1,0:T(8,128)(2,1)S(1)} custom-call(bf16[8,32,512]{2,1,0:T(8,128)(2,1)S(1)} %cross.2._.after_ref.refs_0_.refs_3_), custom_call_target="tpu_custom_call" | custom-call | flops 4194304 | bytes 524288 | tf_op jit(solution)/shard_map/inverse/pallas_call | solution.py:397
  19.4 0.4 %part.1.part_ref = f32[256,512]{1,0:T(8,128)S(1)} custom-call(bf16[512,512]{1,0:T(8,128)(2,1)S(1)} %inverse.1.table_ref, bf16[8,32,512]{2,1,0:T(8,128)(2,1)S(1)} %cross.2._.after_ref.refs_0_.refs_3_, bf16[8,32,512]{2,1,0:T(8,128)(2,1)S(1)} %cross.3.refs_1_.refs_3_, bf16[8,32,512]{2,1,0:T(8,128)(2,1)S(1)} %collective-permute-done.1.refs_2_), custom_call_target="tpu_custom_call" | custom-call | flops 268435456 | bytes 1048576 | tf_op jit(solution)/shard_map/part/pallas_call | solution.py:424
  19.9 0.3 %collective-permute-done.4.rest_3_ = bf16[8,32,512]{2,1,0:T(8,128)(2,1)S(1)} collective-permute-done((bf16[8,32,512]{2,1,0:T(8,128)(2,1)S(1)}, bf16[8,32,512]{2,1,0:T(8,128)(2,1)S(1)}, u32[]{:S(2)}, u32[]{:S(2)}) %collective-permute-start.4) | collective-permute-done | bytes 262176 | tf_op jit(solution)/shard_map/ppermute | solution.py:384
  20.1 1.2 %lags.2.rest_0_ = bf16[8,64,512]{2,1,0:T(8,128)(2,1)} custom-call(bf16[512,512]{1,0:T(8,128)(2,1)S(1)} %inverse.1.table_ref, bf16[8,32,512]{2,1,0:T(8,128)(2,1)S(1)} %get-tuple-element.25.refs_0_.rest_0_, bf16[8,32,512]{2,1,0:T(8,128)(2,1)S(1)} %get-tuple-element.26.refs_1_.rest_1_, bf16[8,32,512]{2,1,0:T(8,128)(2,1)S(1)} %collective-permute-done.3.refs_2_.rest_2_, ...), custom_call_target="tpu_custom_call" | custom-call | flops 268435456 | bytes 1048576 | tf_op jit(solution)/shard_map/lags/pallas_call | solution.py:408
  21.3 3.1 %collective-permute-done.2.more_ref = bf16[8,32,512]{2,1,0:T(8,128)(2,1)S(1)} collective-permute-done((bf16[8,32,512]{2,1,0:T(8,128)(2,1)S(1)}, bf16[8,32,512]{2,1,0:T(8,128)(2,1)S(1)}, u32[]{:S(2)}, u32[]{:S(2)}) %collective-permute-start.2) | collective-permute-done | bytes 262176 | tf_op jit(solution)/shard_map/ppermute | solution.py:384
  24.4 1.0 %lags.3 = bf16[8,64,512]{2,1,0:T(8,128)(2,1)} custom-call(bf16[512,512]{1,0:T(8,128)(2,1)S(1)} %inverse.1.table_ref, f32[256,512]{1,0:T(8,128)S(1)} %part.1.part_ref, bf16[8,32,512]{2,1,0:T(8,128)(2,1)S(1)} %collective-permute-done.2.more_ref, bf16[8,64,512]{2,1,0:T(8,128)(2,1)} %lags.2.rest_0_), custom_call_target="tpu_custom_call", output_to_operand_aliasing={{}: (3, {})} | custom-call | flops 268435456 | bytes 1048576 | tf_op jit(solution)/shard_map/lags/pallas_call | solution.py:408
  (2 shorter events, 0.0 us)
Async XLA Ops:
  0.0 3.5 %copy-start = (bf16[64,8,512]{2,1,0:T(8,128)(2,1)S(1)}, bf16[64,8,512]{2,1,0:T(8,128)(2,1)}, u32[]{:S(2)}) copy-start(bf16[64,8,512]{2,1,0:T(8,128)(2,1)} %param.3) | copy-start | bytes 1572868
  1.5 5.8 %collective-permute-start = (bf16[32,4096]{1,0:T(8,128)(2,1)S(1)}, bf16[32,4096]{1,0:T(8,128)(2,1)S(1)}, u32[]{:S(2)}, u32[]{:S(2)}) collective-permute-start(bf16[32,4096]{1,0:T(8,128)(2,1)S(1)} %get-tuple-element.20.edge_ref), channel_id=1, source_target_pairs={{4,0},{8,4},{12,8},{16,12},{20,16},{24,20},{28,24},{5,1},{9,5},{13... | collective-permute-start | bytes 786440 | tf_op jit(solution)/shard_map/ppermute | solution.py:342
  3.5 8.3 %collective-permute-start.3 = (bf16[8,32,512]{2,1,0:T(8,128)(2,1)S(1)}, bf16[8,32,512]{2,1,0:T(8,128)(2,1)S(1)}, u32[]{:S(2)}, u32[]{:S(2)}) collective-permute-start(bf16[8,32,512]{2,1,0:T(8,128)(2,1)S(1)} %get-tuple-element.25.refs_0_.rest_0_), channel_id=1, source_target_pairs={{0,2},{1,3},{4,5},{5,4},{6,7},{8,10},{9,11},{12,13},{13,12},{14,15... | collective-permute-start | bytes 786440 | tf_op jit(solution)/shard_map/ppermute | solution.py:384
  7.3 8.7 %collective-permute-start.1 = (bf16[8,32,512]{2,1,0:T(8,128)(2,1)S(1)}, bf16[8,32,512]{2,1,0:T(8,128)(2,1)S(1)}, u32[]{:S(2)}, u32[]{:S(2)}) collective-permute-start(bf16[8,32,512]{2,1,0:T(8,128)(2,1)S(1)} %cross.2._.after_ref.refs_0_.refs_3_), channel_id=1, source_target_pairs={{0,2},{1,3},{4,5},{5,4},{6,7},{8,10},{9,11},{12,13},{13,12},{14,15... | collective-permute-start | bytes 786440 | tf_op jit(solution)/shard_map/ppermute | solution.py:384
  11.9 8.3 %collective-permute-start.4 = (bf16[8,32,512]{2,1,0:T(8,128)(2,1)S(1)}, bf16[8,32,512]{2,1,0:T(8,128)(2,1)S(1)}, u32[]{:S(2)}, u32[]{:S(2)}) collective-permute-start(bf16[8,32,512]{2,1,0:T(8,128)(2,1)S(1)} %mix.3), channel_id=1, source_target_pairs={{0,1},{2,3},{3,2},{4,6},{5,7},{8,9},{10,11},{11,10},{12,14},{13,15... | collective-permute-start | bytes 786440 | tf_op jit(solution)/shard_map/ppermute | solution.py:384
  16.1 8.3 %collective-permute-start.2 = (bf16[8,32,512]{2,1,0:T(8,128)(2,1)S(1)}, bf16[8,32,512]{2,1,0:T(8,128)(2,1)S(1)}, u32[]{:S(2)}, u32[]{:S(2)}) collective-permute-start(bf16[8,32,512]{2,1,0:T(8,128)(2,1)S(1)} %mix.2), channel_id=1, source_target_pairs={{0,1},{2,3},{3,2},{4,6},{5,7},{8,9},{10,11},{11,10},{12,14},{13,15... | collective-permute-start | bytes 786440 | tf_op jit(solution)/shard_map/ppermute | solution.py:384
where the time goes:
time: 25.6 us; the launch traced here: 25.4 us
  starting transfers between devices  10.9 us (43%)
  waiting for transfers between devices  7.68 us (30%)
  Pallas kernels  6.71 us (26%)
    ppermute x4, starting transfers between devices, sent(): return lax.ppermute(value, ('chan', 'tm'), moves)  8.96 us
    ppermute x4, waiting for transfers between devices, sent(): return lax.ppermute(value, ('chan', 'tm'), moves)  5.15 us
    ppermute x1, waiting for transfers between devices, per_device(): edge = lax.ppermute(short_a, 'chan', [(i, i - 1) for i in range(1, ring)])  2.53 us
    pallas_call x2, Pallas kernels, written(): pl.pallas_call(kernel, out_shape=jax.ShapeDtypeStruct((pairs, chans, leng...  2.17 us
    ppermute x1, starting transfers between devices, per_device(): edge = lax.ppermute(short_a, 'chan', [(i, i - 1) for i in range(1, ring)])  1.92 us
    pallas_call x1, Pallas kernels, per_device(): pl.pallas_call(head_kernel, out_shape=(white_type, short_type, jax.ShapeD...  1.51 us
    pallas_call x2, Pallas kernels, tail(): pl.pallas_call(functools.partial(tail_kernel, limits, now), out_shape=(wh...  1.27 us
    pallas_call x2, Pallas kernels, cross(): pl.pallas_call(functools.partial(cross_kernel, limits, now), out_shape=lo...  0.78 us
  transfers between devices with their start and end apart: 5, of which 5 were waited for; matrix products, arithmetic and copies ran while one was open for 0% of the time, Pallas kernels for 16%

commit v1 on v0

--- a/solution.py
+++ b/solution.py
@@ -404,21 +404,21 @@
         name="inverse",
     )(local_b)
 
-    def written(kernel, terms, *so_far):
+    def written(kernel, terms, later, *so_far):
         return pl.pallas_call(
             kernel,
             out_shape=jax.ShapeDtypeStruct((pairs, chans, length), jnp.bfloat16),
-            in_specs=[whole()] * (1 + len(terms)) + [whole(pl.ANY)] * len(so_far),
+            in_specs=[whole()] * (1 + len(terms)) + [whole(pl.ANY)] * (len(later) + len(so_far)),
             out_specs=whole(pl.ANY),
             scratch_shapes=[
                 pltpu.VMEM((pairs, span, length), jnp.bfloat16),
                 pltpu.SemaphoreType.DMA,
             ],
-            input_output_aliases={1 + len(terms): 0} if so_far else {},
+            input_output_aliases={1 + len(terms) + len(later): 0} if so_far else {},
             compiler_params=params,
             cost_estimate=cost(pairs * span * length * length * 4, 1024 * 1024),
             name="lags",
-        )(inverse, *terms, *so_far)
+        )(inverse, *terms, *later, *so_far)
 
     def part(terms, weights):
         return pl.pallas_call(
@@ -433,9 +433,11 @@
 
     unit = [1.0] * (2 * groups)
 
-    def two_hops(local, late, after):
+    def two_hops(local, late, after, apart):
         f, ff = power[1], power[2]
-        got = sent(local, [(0, 2), (1, 3)], [(0, 1), (1, 0), (2, 3)])
+        last = [(2, 3)]
+        got = sent(local, [(0, 2), (1, 3)], [(0, 1), (1, 0)] + ([] if apart else last))
+        alone = [sent(local, [], last)] if apart else []
         total = mix(
             [local, late, got],
             [[1.0, 1.0, 1.0, 0.0, f, 1.0, 0.0, 0.0], [ff, ff, ff, 1.0, 1.0, f, 0.0, 0.0]],
@@ -445,11 +447,11 @@
         weights = [
             unit,
             [ff, ff, ff, ff, 0.0, f, 0.0, f],
-            [f, f, f, f, 0.0, 0.0, f, ff],
         ]
-        return [local, late, got, more], weights
-
-    def one_hop(local, late, after):
+        weights += [[f] * (2 * groups)] * len(alone) + [[f, f, f, f, 0.0, 0.0, f, ff]]
+        return [local, late, got] + alone + [more], weights
+
+    def one_hop(local, late, after, apart):
         terms, weights = [local, late], [unit]
         for d in range(1, groups):
             moves = [(h, h + d) for h in range(groups - d)]
@@ -459,12 +461,13 @@
 
     spread = two_hops if square else one_hop
     scale = bins**-0.5
-    terms, weights = spread(local_a, late_a, late_b)
-    result = written(functools.partial(lag_kernel, limits, scale, 0, weights), terms)
-    terms, weights = spread(local_b, late_b, local_b)
-    before = part(terms[:-1], weights[:-1])
-    last = functools.partial(last_kernel, scale, half, weights[-1])
-    result = written(last, [before, terms[-1]], result)
+    terms_a, weights_a = spread(local_a, late_a, late_b, False)
+    terms_b, weights_b = spread(local_b, late_b, local_b, True)
+    before = part(terms_b[:-1], weights_b[:-1])
+    first = functools.partial(lag_kernel, limits, scale, 0, weights_a)
+    result = written(first, terms_a, [before])
+    last = functools.partial(last_kernel, scale, half, weights_b[-1])
+    result = written(last, [before, terms_b[-1]], [], result)
     return result.reshape(1, pairs, chans, length)
 
 

time: 25.6 us -> 25.6 us (level)
  starting transfers between devices: 10.9 us -> 11.6 us
  waiting for transfers between devices: 7.68 us -> 6.98 us
    ppermute x4 -> x5, waiting for transfers between devices: 5.15 us -> 4.45 us  [sent(): return lax.ppermute(value, ('chan', 'tm'), moves)]
    ppermute x4 -> x5, starting transfers between devices: 8.96 us -> 9.64 us  [sent(): return lax.ppermute(value, ('chan', 'tm'), moves)]
  transfers between devices with their start and end apart: 5 -> 6, of which waited for: 5 -> 5; matrix products, arithmetic and copies ran while one was open for 0% -> 0% of each run, Pallas kernels for 16% -> 16%
where the time goes in v1:
time: 25.6 us; the launch traced here: 25.4 us
  starting transfers between devices  11.6 us (45%)
  waiting for transfers between devices  6.98 us (27%)
  Pallas kernels  6.71 us (26%)
    ppermute x5, starting transfers between devices, sent(): return lax.ppermute(value, ('chan', 'tm'), moves)  9.64 us
    ppermute x5, waiting for transfers between devices, sent(): return lax.ppermute(value, ('chan', 'tm'), moves)  4.45 us
    ppermute x1, waiting for transfers between devices, per_device(): edge = lax.ppermute(short_a, 'chan', [(i, i - 1) for i in range(1, ring)])  2.53 us
    pallas_call x2, Pallas kernels, written(): pl.pallas_call(kernel, out_shape=jax.ShapeDtypeStruct((pairs, chans, leng...  2.17 us
    ppermute x1, starting transfers between devices, per_device(): edge = lax.ppermute(short_a, 'chan', [(i, i - 1) for i in range(1, ring)])  1.92 us
    pallas_call x1, Pallas kernels, per_device(): pl.pallas_call(head_kernel, out_shape=(white_type, short_type, jax.ShapeD...  1.51 us
    pallas_call x2, Pallas kernels, tail(): pl.pallas_call(functools.partial(tail_kernel, limits, now), out_shape=(wh...  1.27 us
    pallas_call x2, Pallas kernels, cross(): pl.pallas_call(functools.partial(cross_kernel, limits, now), out_shape=lo...  0.78 us
  transfers between devices with their start and end apart: 6, of which 5 were waited for; matrix products, arithmetic and copies ran while one was open for 0% of the time, Pallas kernels for 16%

profile of v1, /device:TPU:28, one launch (start us, length us, event | category | flops | bytes accessed | tf_op | source)
XLA Modules:
  0.0 25.4 jit_solution(9700016816536561405)
XLA Ops:
  0.0 0.0 copy-start
  0.0 1.5 %head.1 = (f32[8,32,512]{2,1,0:T(8,128)S(1)}, bf16[32,4096]{1,0:T(8,128)(2,1)S(1)}, bf16[512,512]{1,0:T(8,128)(2,1)S(1)}, bf16[8,32,64]{2,1,0:T(8,128)(2,1)S(1)}, f32[64,1024]{1,0:T(8,128)S(1)}) custom-call(bf16[512,512]{1,0:T(8,128)(2,1)} %bitcast.3, s32[8,64]{1,0:T(8,128)} %bitcast.6, s32[8]{0:T(128)} %offsets_hbm.1), custom_call_target="tpu_custom_call" | custom-call | flops 134217728 | bytes 2097152 | tf_op jit(solution)/shard_map/head/pallas_call | solution.py:318
  1.5 1.9 %collective-permute-start = (bf16[32,4096]{1,0:T(8,128)(2,1)S(1)}, bf16[32,4096]{1,0:T(8,128)(2,1)S(1)}, u32[]{:S(2)}, u32[]{:S(2)}) collective-permute-start(bf16[32,4096]{1,0:T(8,128)(2,1)S(1)} %get-tuple-element.20.edge_ref), channel_id=1, source_target_pairs={{4,0},{8,4},{12,8},{16,12},{20,16},{24,20},{28,24},{5,1},{9,5},{13... | collective-permute-start | bytes 786440 | tf_op jit(solution)/shard_map/ppermute | solution.py:342
  3.5 0.0 copy-done
  3.5 1.3 %collective-permute-start.4 = (bf16[8,32,512]{2,1,0:T(8,128)(2,1)S(1)}, bf16[8,32,512]{2,1,0:T(8,128)(2,1)S(1)}, u32[]{:S(2)}, u32[]{:S(2)}) collective-permute-start(bf16[8,32,512]{2,1,0:T(8,128)(2,1)S(1)} %get-tuple-element.25.refs_0_.rest_0_), channel_id=1, source_target_pairs={{0,2},{1,3},{4,5},{5,4},{6,7},{8,10},{9,11},{12,13},{13,12},{14,15... | collective-permute-start | bytes 786440 | tf_op jit(solution)/shard_map/ppermute | solution.py:384
  4.8 2.5 %collective-permute-done.edge_ref = bf16[32,4096]{1,0:T(8,128)(2,1)S(1)} collective-permute-done((bf16[32,4096]{1,0:T(8,128)(2,1)S(1)}, bf16[32,4096]{1,0:T(8,128)(2,1)S(1)}, u32[]{:S(2)}, u32[]{:S(2)}) %collective-permute-start) | collective-permute-done | bytes 262176 | tf_op jit(solution)/shard_map/ppermute | solution.py:342
  7.3 1.3 %collective-permute-start.1 = (bf16[8,32,512]{2,1,0:T(8,128)(2,1)S(1)}, bf16[8,32,512]{2,1,0:T(8,128)(2,1)S(1)}, u32[]{:S(2)}, u32[]{:S(2)}) collective-permute-start(bf16[8,32,512]{2,1,0:T(8,128)(2,1)S(1)} %cross.2._.after_ref.refs_0_.refs_3_), channel_id=1, source_target_pairs={{0,2},{1,3},{4,5},{5,4},{8,10},{9,11},{12,13},{13,12},{16,18},{17,... | collective-permute-start | bytes 786440 | tf_op jit(solution)/shard_map/ppermute | solution.py:384
  8.6 0.7 %collective-permute-start.2 = (bf16[8,32,512]{2,1,0:T(8,128)(2,1)S(1)}, bf16[8,32,512]{2,1,0:T(8,128)(2,1)S(1)}, u32[]{:S(2)}, u32[]{:S(2)}) collective-permute-start(bf16[8,32,512]{2,1,0:T(8,128)(2,1)S(1)} %cross.2._.after_ref.refs_0_.refs_3_), channel_id=1, source_target_pairs={{6,7},{14,15},{22,23},{30,31}} | collective-permute-start | bytes 786440 | tf_op jit(solution)/shard_map/ppermute | solution.py:384
  9.3 1.2 %tail.3 = (f32[8,32,512]{2,1,0:T(8,128)S(1)}, bf16[32,4096]{1,0:T(8,128)(2,1)S(1)}, bf16[8,32,512]{2,1,0:T(8,128)(2,1)S(1)}) custom-call(bf16[512,512]{1,0:T(8,128)(2,1)S(1)} %bitcast.5, bf16[512,512]{1,0:T(8,128)(2,1)S(1)} %get-tuple-element.17.table_ref.after_ref, f32[64,1024]{1,0:T(8,128)S(1)} %get-tuple-element.18.keep_ref, ...), custom_call_target="tpu_custom_call" | custom-call | flops 268435456 | bytes 4194304 | tf_op jit(solution)/shard_map/tail/pallas_call | solution.py:349
  10.6 0.8 %cross.3.refs_1_.refs_3_ = bf16[8,32,512]{2,1,0:T(8,128)(2,1)S(1)} custom-call(bf16[8,32,64]{2,1,0:T(8,128)(2,1)S(1)} %get-tuple-element.16.pick_ref, f32[8,32,512]{2,1,0:T(8,128)S(1)} %get-tuple-element.23.white_ref, bf16[32,4096]{1,0:T(8,128)(2,1)S(1)} %get-tuple-element.24.short_ref, bf16[32,4096]{1,0:T(8,128)(2,1)S(1)} %collective-permute-done.edge_ref, ...), custom_call_target="tpu_custom_call" | custom-call | flops 4194304 | bytes 4194304 | tf_op jit(solution)/shard_map/cross/pallas_call | solution.py:361
  11.3 0.4 %collective-permute-done.4.refs_2_.rest_2_ = bf16[8,32,512]{2,1,0:T(8,128)(2,1)S(1)} collective-permute-done((bf16[8,32,512]{2,1,0:T(8,128)(2,1)S(1)}, bf16[8,32,512]{2,1,0:T(8,128)(2,1)S(1)}, u32[]{:S(2)}, u32[]{:S(2)}) %collective-permute-start.4) | collective-permute-done | bytes 262176 | tf_op jit(solution)/shard_map/ppermute | solution.py:384
  11.8 0.1 mix.3
  11.9 3.4 %collective-permute-start.5 = (bf16[8,32,512]{2,1,0:T(8,128)(2,1)S(1)}, bf16[8,32,512]{2,1,0:T(8,128)(2,1)S(1)}, u32[]{:S(2)}, u32[]{:S(2)}) collective-permute-start(bf16[8,32,512]{2,1,0:T(8,128)(2,1)S(1)} %mix.3), channel_id=1, source_target_pairs={{0,1},{2,3},{3,2},{4,6},{5,7},{8,9},{10,11},{11,10},{12,14},{13,15... | collective-permute-start | bytes 786440 | tf_op jit(solution)/shard_map/ppermute | solution.py:384
  15.3 0.7 %collective-permute-done.1.refs_2_ = bf16[8,32,512]{2,1,0:T(8,128)(2,1)S(1)} collective-permute-done((bf16[8,32,512]{2,1,0:T(8,128)(2,1)S(1)}, bf16[8,32,512]{2,1,0:T(8,128)(2,1)S(1)}, u32[]{:S(2)}, u32[]{:S(2)}) %collective-permute-start.1) | collective-permute-done | bytes 262176 | tf_op jit(solution)/shard_map/ppermute | solution.py:384
  16.0 0.1 mix.2
  16.1 3.0 %collective-permute-start.3 = (bf16[8,32,512]{2,1,0:T(8,128)(2,1)S(1)}, bf16[8,32,512]{2,1,0:T(8,128)(2,1)S(1)}, u32[]{:S(2)}, u32[]{:S(2)}) collective-permute-start(bf16[8,32,512]{2,1,0:T(8,128)(2,1)S(1)} %mix.2), channel_id=1, source_target_pairs={{0,1},{2,3},{3,2},{4,6},{5,7},{8,9},{10,11},{11,10},{12,14},{13,15... | collective-permute-start | bytes 786440 | tf_op jit(solution)/shard_map/ppermute | solution.py:384
  19.1 0.3 %inverse.1.table_ref = bf16[512,512]{1,0:T(8,128)(2,1)S(1)} custom-call(bf16[8,32,512]{2,1,0:T(8,128)(2,1)S(1)} %cross.2._.after_ref.refs_0_.refs_3_), custom_call_target="tpu_custom_call" | custom-call | flops 4194304 | bytes 524288 | tf_op jit(solution)/shard_map/inverse/pallas_call | solution.py:397
  19.4 0.0 collective-permute-done.2.refs_3_
  19.4 0.4 %part.1.rest_4_.part_ref = f32[256,512]{1,0:T(8,128)S(1)} custom-call(bf16[512,512]{1,0:T(8,128)(2,1)S(1)} %inverse.1.table_ref, bf16[8,32,512]{2,1,0:T(8,128)(2,1)S(1)} %cross.2._.after_ref.refs_0_.refs_3_, bf16[8,32,512]{2,1,0:T(8,128)(2,1)S(1)} %cross.3.refs_1_.refs_3_, bf16[8,32,512]{2,1,0:T(8,128)(2,1)S(1)} %collective-permute-done.1.refs_2_, ...), custom_call_target="tpu_custom_call" | custom-call | flops 268435456 | bytes 1048576 | tf_op jit(solution)/shard_map/part/pallas_call | solution.py:424
  19.9 0.3 %collective-permute-done.5.rest_3_ = bf16[8,32,512]{2,1,0:T(8,128)(2,1)S(1)} collective-permute-done((bf16[8,32,512]{2,1,0:T(8,128)(2,1)S(1)}, bf16[8,32,512]{2,1,0:T(8,128)(2,1)S(1)}, u32[]{:S(2)}, u32[]{:S(2)}) %collective-permute-start.5) | collective-permute-done | bytes 262176 | tf_op jit(solution)/shard_map/ppermute | solution.py:384
  20.1 1.2 %lags.2.rest_0_ = bf16[8,64,512]{2,1,0:T(8,128)(2,1)} custom-call(bf16[512,512]{1,0:T(8,128)(2,1)S(1)} %inverse.1.table_ref, bf16[8,32,512]{2,1,0:T(8,128)(2,1)S(1)} %get-tuple-element.25.refs_0_.rest_0_, bf16[8,32,512]{2,1,0:T(8,128)(2,1)S(1)} %get-tuple-element.26.refs_1_.rest_1_, bf16[8,32,512]{2,1,0:T(8,128)(2,1)S(1)} %collective-permute-done.4.refs_2_.rest_2_, ...), custom_call_target="tpu_custom_call" | custom-call | flops 268435456 | bytes 1048576 | tf_op jit(solution)/shard_map/lags/pallas_call | solution.py:408
  21.3 3.1 %collective-permute-done.3.more_ref = bf16[8,32,512]{2,1,0:T(8,128)(2,1)S(1)} collective-permute-done((bf16[8,32,512]{2,1,0:T(8,128)(2,1)S(1)}, bf16[8,32,512]{2,1,0:T(8,128)(2,1)S(1)}, u32[]{:S(2)}, u32[]{:S(2)}) %collective-permute-start.3) | collective-permute-done | bytes 262176 | tf_op jit(solution)/shard_map/ppermute | solution.py:384
  24.4 1.0 %lags.3 = bf16[8,64,512]{2,1,0:T(8,128)(2,1)} custom-call(bf16[512,512]{1,0:T(8,128)(2,1)S(1)} %inverse.1.table_ref, f32[256,512]{1,0:T(8,128)S(1)} %part.1.rest_4_.part_ref, bf16[8,32,512]{2,1,0:T(8,128)(2,1)S(1)} %collective-permute-done.3.more_ref, bf16[8,64,512]{2,1,0:T(8,128)(2,1)} %lags.2.rest_0_), custom_call_target="tpu_custom_call", output_to_operand_aliasing={{}: (3, {})} | custom-call | flops 268435456 | bytes 1048576 | tf_op jit(solution)/shard_map/lags/pallas_call | solution.py:408
  (2 shorter events, 0.0 us)
Async XLA Ops:
  0.0 3.5 %copy-start = (bf16[64,8,512]{2,1,0:T(8,128)(2,1)S(1)}, bf16[64,8,512]{2,1,0:T(8,128)(2,1)}, u32[]{:S(2)}) copy-start(bf16[64,8,512]{2,1,0:T(8,128)(2,1)} %param.3) | copy-start | bytes 1572868
  1.5 5.8 %collective-permute-start = (bf16[32,4096]{1,0:T(8,128)(2,1)S(1)}, bf16[32,4096]{1,0:T(8,128)(2,1)S(1)}, u32[]{:S(2)}, u32[]{:S(2)}) collective-permute-start(bf16[32,4096]{1,0:T(8,128)(2,1)S(1)} %get-tuple-element.20.edge_ref), channel_id=1, source_target_pairs={{4,0},{8,4},{12,8},{16,12},{20,16},{24,20},{28,24},{5,1},{9,5},{13... | collective-permute-start | bytes 786440 | tf_op jit(solution)/shard_map/ppermute | solution.py:342
  3.5 8.3 %collective-permute-start.4 = (bf16[8,32,512]{2,1,0:T(8,128)(2,1)S(1)}, bf16[8,32,512]{2,1,0:T(8,128)(2,1)S(1)}, u32[]{:S(2)}, u32[]{:S(2)}) collective-permute-start(bf16[8,32,512]{2,1,0:T(8,128)(2,1)S(1)} %get-tuple-element.25.refs_0_.rest_0_), channel_id=1, source_target_pairs={{0,2},{1,3},{4,5},{5,4},{6,7},{8,10},{9,11},{12,13},{13,12},{14,15... | collective-permute-start | bytes 786440 | tf_op jit(solution)/shard_map/ppermute | solution.py:384
  7.3 8.7 %collective-permute-start.1 = (bf16[8,32,512]{2,1,0:T(8,128)(2,1)S(1)}, bf16[8,32,512]{2,1,0:T(8,128)(2,1)S(1)}, u32[]{:S(2)}, u32[]{:S(2)}) collective-permute-start(bf16[8,32,512]{2,1,0:T(8,128)(2,1)S(1)} %cross.2._.after_ref.refs_0_.refs_3_), channel_id=1, source_target_pairs={{0,2},{1,3},{4,5},{5,4},{8,10},{9,11},{12,13},{13,12},{16,18},{17,... | collective-permute-start | bytes 786440 | tf_op jit(solution)/shard_map/ppermute | solution.py:384
  8.6 10.8 %collective-permute-start.2 = (bf16[8,32,512]{2,1,0:T(8,128)(2,1)S(1)}, bf16[8,32,512]{2,1,0:T(8,128)(2,1)S(1)}, u32[]{:S(2)}, u32[]{:S(2)}) collective-permute-start(bf16[8,32,512]{2,1,0:T(8,128)(2,1)S(1)} %cross.2._.after_ref.refs_0_.refs_3_), channel_id=1, source_target_pairs={{6,7},{14,15},{22,23},{30,31}} | collective-permute-start | bytes 786440 | tf_op jit(solution)/shard_map/ppermute | solution.py:384
  11.9 8.3 %collective-permute-start.5 = (bf16[8,32,512]{2,1,0:T(8,128)(2,1)S(1)}, bf16[8,32,512]{2,1,0:T(8,128)(2,1)S(1)}, u32[]{:S(2)}, u32[]{:S(2)}) collective-permute-start(bf16[8,32,512]{2,1,0:T(8,128)(2,1)S(1)} %mix.3), channel_id=1, source_target_pairs={{0,1},{2,3},{3,2},{4,6},{5,7},{8,9},{10,11},{11,10},{12,14},{13,15... | collective-permute-start | bytes 786440 | tf_op jit(solution)/shard_map/ppermute | solution.py:384
  16.1 8.3 %collective-permute-start.3 = (bf16[8,32,512]{2,1,0:T(8,128)(2,1)S(1)}, bf16[8,32,512]{2,1,0:T(8,128)(2,1)S(1)}, u32[]{:S(2)}, u32[]{:S(2)}) collective-permute-start(bf16[8,32,512]{2,1,0:T(8,128)(2,1)S(1)} %mix.2), channel_id=1, source_target_pairs={{0,1},{2,3},{3,2},{4,6},{5,7},{8,9},{10,11},{11,10},{12,14},{13,15... | collective-permute-start | bytes 786440 | tf_op jit(solution)/shard_map/ppermute | solution.py:384

commit v2 on v1

--- a/solution.py
+++ b/solution.py
@@ -39,8 +39,12 @@
     for i in range(length // step):
         rows = slice(i * step, (i + 1) * step)
         cos_i, sin_i = coarse_cos[i : i + 1], coarse_sin[i : i + 1]
-        table_ref[rows, :bins] = (cos_i * fine_cos - sin_i * fine_sin).astype(jnp.bfloat16)
-        table_ref[rows, bins:] = -(sin_i * fine_cos + cos_i * fine_sin).astype(jnp.bfloat16)
+        cosine = (cos_i * fine_cos - sin_i * fine_sin).astype(jnp.bfloat16)
+        sine = (sin_i * fine_cos + cos_i * fine_sin).astype(jnp.bfloat16)
+        for t in range(bins // LANES):
+            here = slice(t * LANES, (t + 1) * LANES)
+            table_ref[rows, 2 * t * LANES : (2 * t + 1) * LANES] = cosine[:, here]
+            table_ref[rows, (2 * t + 1) * LANES : (2 * t + 2) * LANES] = -sine[:, here]
 
 
 def inverse_kernel(_, table_ref):
@@ -64,26 +68,35 @@
         table_ref[bins + first : bins + first + step, :] = (-sine).astype(jnp.bfloat16)
 
 
-def whiten_block(x, table, keep, raw_ref, white_ref, short_ref):
+def whiten_block(x, table_ref, keep, raw_ref, white_ref, short_ref):
     wins, span, length = white_ref.shape
     bins = length // 2
     tiles = bins // LANES
-    raw = jnp.dot(x, table, preferred_element_type=jnp.float32)
-    for t in range(2 * tiles):
-        raw_ref[t] = raw[:, t * LANES : (t + 1) * LANES]
+
+    def strided(t, w):
+        return raw_ref[t, pl.ds(w, span, stride=wins), :]
+
+    total = [None] * wins
+    for t in range(tiles):
+        lanes = slice(2 * t * LANES, (2 * t + 2) * LANES)
+        raw = jnp.dot(x, table_ref[:, lanes], preferred_element_type=jnp.float32)
+        raw_ref[2 * t] = raw[:, :LANES]
+        raw_ref[2 * t + 1] = raw[:, LANES:]
+    for t in range(tiles):
+        for w in range(wins):
+            real_part, imag_part = strided(2 * t, w), strided(2 * t + 1, w)
+            power = real_part * real_part + imag_part * imag_part
+            total[w] = power if t == 0 else total[w] + power
     for w in range(wins):
         decay = float(np.float32(DECAY) ** np.float32(wins - 1 - w))
-        part = [raw_ref[t, pl.ds(w, span, stride=wins), :] for t in range(2 * tiles)]
-        power = [part[t] * part[t] + part[tiles + t] * part[tiles + t] for t in range(tiles)]
-        total = power[0]
-        for t in range(1, tiles):
-            total = total + power[t]
-        level = jnp.sum(total, axis=-1, keepdims=True) * (0.01 / bins) + 1e-06
+        level = jnp.sum(total[w], axis=-1, keepdims=True) * (0.01 / bins) + 1e-06
         alive = keep[:, w * LANES : (w + 1) * LANES]
         for t in range(tiles):
-            scale = alive * lax.rsqrt(power[t] + level)
-            for s in (t, tiles + t):
-                value = part[s] * scale
+            part = [strided(2 * t, w), strided(2 * t + 1, w)]
+            power = part[0] * part[0] + part[1] * part[1]
+            scale = alive * lax.rsqrt(power + level)
+            for i, s in enumerate((t, tiles + t)):
+                value = part[i] * scale
                 here = pl.ds(w * length + s * LANES, LANES)
                 white_ref[w, :, s * LANES : (s + 1) * LANES] = value * decay
                 short_ref[:, here] = value.astype(jnp.bfloat16)
@@ -131,7 +144,7 @@
         preferred_element_type=jnp.float32,
     )
     copies[2].wait()
-    whiten_block(x_ref[...], table_ref[...], keep_ref[:span], raw_ref, white_ref, short_ref)
+    whiten_block(x_ref[...], table_ref, keep_ref[:span], raw_ref, white_ref, short_ref)
 
 
 def stack_pairs(pick_ref, white_ref, near_ref, parts_refs, out_ref):
@@ -171,8 +184,10 @@
                 out_ref[pair, c : c + 16, im] = total_im.astype(out_ref.dtype)
 
 
-def sends_first(limits):
-    return lax.axis_index("tm") < jnp.where(lax.rem(lax.axis_index("chan"), 2) == 0, *limits)
+def role(limits):
+    odd = lax.rem(lax.axis_index("chan"), 2)
+    first = lax.axis_index("tm") < jnp.where(odd == 0, *limits)
+    return jnp.where(first, 0, 1 + odd)
 
 
 def tail_kernel(
@@ -195,10 +210,10 @@
     wins, span, length = white_ref.shape
     rows = slice(span * wins, 2 * span * wins)
 
-    @pl.when(sends_first(limits) == now)
+    @pl.when(role(limits) == now)
     def _():
         x = x_ref[rows, :]
-        whiten_block(x, table_ref[...], keep_ref[span:], raw_ref, white_ref, short_ref)
+        whiten_block(x, table_ref, keep_ref[span:], raw_ref, white_ref, short_ref)
         near_ref[:span] = edge_ref[...]
         near_ref[span:] = short_ref[...]
         stack_pairs(pick_ref, head_ref, near_ref, parts_refs, out_ref)
@@ -209,7 +224,7 @@
 ):
     span = short_ref.shape[0]
 
-    @pl.when(sends_first(limits) == now)
+    @pl.when(role(limits) == now)
     def _():
         near_ref[:span] = short_ref[...]
         near_ref[span:] = edge_ref[...]
@@ -225,8 +240,12 @@
 
 def weighted(limits, terms, weights, place):
     total = None
-    first = jnp.where(sends_first(limits), terms[0][...], terms[1][...])
-    for term, options in zip([first] + list(terms[2:]), weights):
+    mine = role(limits)
+    late = len(terms) - len(weights)
+    first = terms[late][...]
+    for i in range(late - 1, -1, -1):
+        first = jnp.where(mine == i, terms[i][...], first)
+    for term, options in zip([first] + list(terms[late + 1 :]), weights):
         value = term[...].astype(jnp.float32)
         if set(options) != {1.0}:
             value = value * (options[0] if len(set(options)) == 1 else chosen(options, place))
@@ -239,8 +258,9 @@
 
 
 def mix_kernel(limits, weights, *refs):
+    count = len(weights) + 1
     place = whereabouts(len(weights[0]) // 2)
-    total = weighted(limits, refs[: len(weights) + 1], weights, place)
+    total = weighted(limits, refs[:count], weights, place)
     refs[-1][...] = total.astype(refs[-1].dtype)
 
 
@@ -255,7 +275,7 @@
 def part_kernel(limits, weights, table_ref, *refs):
     place = whereabouts(len(weights[0]) // 2)
     out_ref = refs[-1]
-    stack = weighted(limits, refs[: len(weights) + 1], weights, place).reshape(out_ref.shape)
+    stack = weighted(limits, refs[: len(weights) + 2], weights, place).reshape(out_ref.shape)
     out_ref[...] = to_lags(stack, table_ref[...])
 
 
@@ -263,7 +283,7 @@
     out_hbm, stage_ref, sem = rest[-3:]
     place = whereabouts(len(weights[0]) // 2)
     pairs, rows, length = stage_ref.shape
-    stack = weighted(limits, rest[: len(weights) + 1], weights, place)
+    stack = weighted(limits, rest[: len(weights) + 2], weights, place)
     stack = stack.reshape(pairs * rows, length)
     lagged = to_lags(stack, table_ref[...]) * scale
     stage_ref[...] = lagged.astype(stage_ref.dtype).reshape(pairs, rows, length)
@@ -313,7 +333,7 @@
     local_type = jax.ShapeDtypeStruct((pairs, span, length), jnp.bfloat16)
     raw_scratch = pltpu.VMEM((2 * tiles, span * wins, LANES), jnp.float32)
     near_scratch = pltpu.VMEM((2 * span, wins * length), jnp.bfloat16)
-    parts_scratch = [pltpu.VMEM((wins, pairs // 2 * span, length), jnp.float32)] * 2
+    parts_scratch = [pltpu.VMEM((wins, pairs // 4 * span, length), jnp.float32)] * 4
 
     white_a, short_a, table, pick, keep = pl.pallas_call(
         head_kernel,
@@ -369,10 +389,10 @@
             name="cross",
         )(pick, white, short, edge, after)
 
-    white_b, short_b, local_a = tail(True, table)
-    local_b = cross(True, white_b, short_b, table)
-    white_late, short_late, late_a = tail(False, local_b)
-    late_b = cross(False, white_late, short_late, local_b)
+    white_b, short_b, local_a = tail(0, table)
+    local_b = cross(0, white_b, short_b, table)
+    white_late, short_late, late_a = tail(1, local_b)
+    late_b = cross(1, white_late, short_late, local_b)
 
     power = [float(np.float32(factor) ** np.float32(d)) for d in range(groups)]
     def sent(value, even, odd):
@@ -449,20 +469,24 @@
             [ff, ff, ff, ff, 0.0, f, 0.0, f],
         ]
         weights += [[f] * (2 * groups)] * len(alone) + [[f, f, f, f, 0.0, 0.0, f, ff]]
-        return [local, late, got] + alone + [more], weights
+        return total, [got] + alone + [more], weights
 
     def one_hop(local, late, after, apart):
-        terms, weights = [local, late], [unit]
+        terms, weights = [], [unit]
         for d in range(1, groups):
             moves = [(h, h + d) for h in range(groups - d)]
             terms.append(sent(local, moves, moves))
             weights.append([power[d]] * (2 * groups))
-        return terms, weights
+        return local, terms, weights
 
     spread = two_hops if square else one_hop
     scale = bins**-0.5
-    terms_a, weights_a = spread(local_a, late_a, late_b, False)
-    terms_b, weights_b = spread(local_b, late_b, local_b, True)
+    _, terms_a, weights_a = spread(local_a, late_a, late_b, False)
+    ahead, terms_b, weights_b = spread(local_b, late_b, local_b, True)
+    white_last, short_last, last_a = tail(2, ahead)
+    last_b = cross(2, white_last, short_last, ahead)
+    terms_a = [local_a, late_a, last_a] + terms_a
+    terms_b = [local_b, late_b, last_b] + terms_b
     before = part(terms_b[:-1], weights_b[:-1])
     first = functools.partial(lag_kernel, limits, scale, 0, weights_a)
     result = written(first, terms_a, [before])

time: 25.6 us -> 25.6 us (level)
    pallas_call x2 -> x3, Pallas kernels: 1.27 us -> 1.34 us  [tail(): pl.pallas_call(functools.partial(tail_kernel, limits, now), out_shape=(wh...]
    pallas_call x2 -> x3, Pallas kernels: 0.78 us -> 0.79 us  [cross(): pl.pallas_call(functools.partial(cross_kernel, limits, now), out_shape=lo...]
  transfers between devices with their start and end apart: 6 -> 6, of which waited for: 5 -> 5; matrix products, arithmetic and copies ran while one was open for 0% -> 0% of each run, Pallas kernels for 16% -> 17%
where the time goes in v2:
time: 25.6 us; the launch traced here: 25.4 us
  starting transfers between devices  11.6 us (45%)
  Pallas kernels  6.82 us (27%)
  waiting for transfers between devices  6.79 us (27%)
    ppermute x5, starting transfers between devices, sent(): return lax.ppermute(value, ('chan', 'tm'), moves)  9.69 us
    ppermute x5, waiting for transfers between devices, sent(): return lax.ppermute(value, ('chan', 'tm'), moves)  4.26 us
    ppermute x1, waiting for transfers between devices, per_device(): edge = lax.ppermute(short_a, 'chan', [(i, i - 1) for i in range(1, ring)])  2.53 us
    pallas_call x2, Pallas kernels, written(): pl.pallas_call(kernel, out_shape=jax.ShapeDtypeStruct((pairs, chans, leng...  2.18 us
    ppermute x1, starting transfers between devices, per_device(): edge = lax.ppermute(short_a, 'chan', [(i, i - 1) for i in range(1, ring)])  1.92 us
    pallas_call x1, Pallas kernels, per_device(): pl.pallas_call(head_kernel, out_shape=(white_type, short_type, jax.ShapeD...  1.54 us
    pallas_call x3, Pallas kernels, tail(): pl.pallas_call(functools.partial(tail_kernel, limits, now), out_shape=(wh...  1.34 us
    pallas_call x3, Pallas kernels, cross(): pl.pallas_call(functools.partial(cross_kernel, limits, now), out_shape=lo...  0.79 us
  transfers between devices with their start and end apart: 6, of which 5 were waited for; matrix products, arithmetic and copies ran while one was open for 0% of the time, Pallas kernels for 17%

profile of v2, /device:TPU:28, one launch (start us, length us, event | category | flops | bytes accessed | tf_op | source)
XLA Modules:
  0.0 25.4 jit_solution(8698653057482110712)
XLA Ops:
  0.0 0.0 copy-start
  0.0 1.5 %head.1 = (f32[8,32,512]{2,1,0:T(8,128)S(1)}, bf16[32,4096]{1,0:T(8,128)(2,1)S(1)}, bf16[512,512]{1,0:T(8,128)(2,1)S(1)}, bf16[8,32,64]{2,1,0:T(8,128)(2,1)S(1)}, f32[64,1024]{1,0:T(8,128)S(1)}) custom-call(bf16[512,512]{1,0:T(8,128)(2,1)} %bitcast.3, s32[8,64]{1,0:T(8,128)} %bitcast.7, s32[8]{0:T(128)} %offsets_hbm.1), custom_call_target="tpu_custom_call" | custom-call | flops 134217728 | bytes 2097152 | tf_op jit(solution)/shard_map/head/pallas_call | solution.py:338
  1.5 1.9 %collective-permute-start = (bf16[32,4096]{1,0:T(8,128)(2,1)S(1)}, bf16[32,4096]{1,0:T(8,128)(2,1)S(1)}, u32[]{:S(2)}, u32[]{:S(2)}) collective-permute-start(bf16[32,4096]{1,0:T(8,128)(2,1)S(1)} %get-tuple-element.23.edge_ref), channel_id=1, source_target_pairs={{4,0},{8,4},{12,8},{16,12},{20,16},{24,20},{28,24},{5,1},{9,5},{13... | collective-permute-start | bytes 786440 | tf_op jit(solution)/shard_map/ppermute | solution.py:362
  3.5 0.0 copy-done
  3.5 1.3 %collective-permute-start.4 = (bf16[8,32,512]{2,1,0:T(8,128)(2,1)S(1)}, bf16[8,32,512]{2,1,0:T(8,128)(2,1)S(1)}, u32[]{:S(2)}, u32[]{:S(2)}) collective-permute-start(bf16[8,32,512]{2,1,0:T(8,128)(2,1)S(1)} %get-tuple-element.30.refs_0_.rest_0_), channel_id=1, source_target_pairs={{0,2},{1,3},{4,5},{5,4},{6,7},{8,10},{9,11},{12,13},{13,12},{14,15... | collective-permute-start | bytes 786440 | tf_op jit(solution)/shard_map/ppermute | solution.py:404
  4.8 2.5 %collective-permute-done.edge_ref = bf16[32,4096]{1,0:T(8,128)(2,1)S(1)} collective-permute-done((bf16[32,4096]{1,0:T(8,128)(2,1)S(1)}, bf16[32,4096]{1,0:T(8,128)(2,1)S(1)}, u32[]{:S(2)}, u32[]{:S(2)}) %collective-permute-start) | collective-permute-done | bytes 262176 | tf_op jit(solution)/shard_map/ppermute | solution.py:362
  7.3 1.3 %collective-permute-start.1 = (bf16[8,32,512]{2,1,0:T(8,128)(2,1)S(1)}, bf16[8,32,512]{2,1,0:T(8,128)(2,1)S(1)}, u32[]{:S(2)}, u32[]{:S(2)}) collective-permute-start(bf16[8,32,512]{2,1,0:T(8,128)(2,1)S(1)} %cross.3._.after_ref.refs_0_.refs_3_), channel_id=1, source_target_pairs={{0,2},{1,3},{4,5},{5,4},{8,10},{9,11},{12,13},{13,12},{16,18},{17,... | collective-permute-start | bytes 786440 | tf_op jit(solution)/shard_map/ppermute | solution.py:404
  8.6 0.7 %collective-permute-start.2 = (bf16[8,32,512]{2,1,0:T(8,128)(2,1)S(1)}, bf16[8,32,512]{2,1,0:T(8,128)(2,1)S(1)}, u32[]{:S(2)}, u32[]{:S(2)}) collective-permute-start(bf16[8,32,512]{2,1,0:T(8,128)(2,1)S(1)} %cross.3._.after_ref.refs_0_.refs_3_), channel_id=1, source_target_pairs={{6,7},{14,15},{22,23},{30,31}} | collective-permute-start | bytes 786440 | tf_op jit(solution)/shard_map/ppermute | solution.py:404
  9.3 1.3 %tail.4 = (f32[8,32,512]{2,1,0:T(8,128)S(1)}, bf16[32,4096]{1,0:T(8,128)(2,1)S(1)}, bf16[8,32,512]{2,1,0:T(8,128)(2,1)S(1)}) custom-call(bf16[512,512]{1,0:T(8,128)(2,1)S(1)} %bitcast.5, bf16[512,512]{1,0:T(8,128)(2,1)S(1)} %get-tuple-element.20.table_ref.after_ref, f32[64,1024]{1,0:T(8,128)S(1)} %get-tuple-element.21.keep_ref, ...), custom_call_target="tpu_custom_call" | custom-call | flops 268435456 | bytes 4194304 | tf_op jit(solution)/shard_map/tail/pallas_call | solution.py:369
  10.6 0.8 %cross.4.refs_1_.refs_3_ = bf16[8,32,512]{2,1,0:T(8,128)(2,1)S(1)} custom-call(bf16[8,32,64]{2,1,0:T(8,128)(2,1)S(1)} %get-tuple-element.19.pick_ref, f32[8,32,512]{2,1,0:T(8,128)S(1)} %get-tuple-element.26.white_ref, bf16[32,4096]{1,0:T(8,128)(2,1)S(1)} %get-tuple-element.27.short_ref, bf16[32,4096]{1,0:T(8,128)(2,1)S(1)} %collective-permute-done.edge_ref, ...), custom_call_target="tpu_custom_call" | custom-call | flops 4194304 | bytes 4194304 | tf_op jit(solution)/shard_map/cross/pallas_call | solution.py:381
  11.4 0.4 %collective-permute-done.4.refs_2_.rest_3_ = bf16[8,32,512]{2,1,0:T(8,128)(2,1)S(1)} collective-permute-done((bf16[8,32,512]{2,1,0:T(8,128)(2,1)S(1)}, bf16[8,32,512]{2,1,0:T(8,128)(2,1)S(1)}, u32[]{:S(2)}, u32[]{:S(2)}) %collective-permute-start.4) | collective-permute-done | bytes 262176 | tf_op jit(solution)/shard_map/ppermute | solution.py:404
  11.8 0.1 mix.3
  11.9 3.4 %collective-permute-start.5 = (bf16[8,32,512]{2,1,0:T(8,128)(2,1)S(1)}, bf16[8,32,512]{2,1,0:T(8,128)(2,1)S(1)}, u32[]{:S(2)}, u32[]{:S(2)}) collective-permute-start(bf16[8,32,512]{2,1,0:T(8,128)(2,1)S(1)} %mix.3), channel_id=1, source_target_pairs={{0,1},{2,3},{3,2},{4,6},{5,7},{8,9},{10,11},{11,10},{12,14},{13,15... | collective-permute-start | bytes 786440 | tf_op jit(solution)/shard_map/ppermute | solution.py:404
  15.3 0.6 %collective-permute-done.1.refs_2_.refs_3_ = bf16[8,32,512]{2,1,0:T(8,128)(2,1)S(1)} collective-permute-done((bf16[8,32,512]{2,1,0:T(8,128)(2,1)S(1)}, bf16[8,32,512]{2,1,0:T(8,128)(2,1)S(1)}, u32[]{:S(2)}, u32[]{:S(2)}) %collective-permute-start.1) | collective-permute-done | bytes 262176 | tf_op jit(solution)/shard_map/ppermute | solution.py:404
  16.0 0.1 mix.2.after_ref
  16.1 3.0 %collective-permute-start.3 = (bf16[8,32,512]{2,1,0:T(8,128)(2,1)S(1)}, bf16[8,32,512]{2,1,0:T(8,128)(2,1)S(1)}, u32[]{:S(2)}, u32[]{:S(2)}) collective-permute-start(bf16[8,32,512]{2,1,0:T(8,128)(2,1)S(1)} %mix.2.after_ref), channel_id=1, source_target_pairs={{0,1},{2,3},{3,2},{4,6},{5,7},{8,9},{10,11},{11,10},{12,14},{13,15... | collective-permute-start | bytes 786440 | tf_op jit(solution)/shard_map/ppermute | solution.py:404
  19.1 0.3 %inverse.1.table_ref = bf16[512,512]{1,0:T(8,128)(2,1)S(1)} custom-call(bf16[8,32,512]{2,1,0:T(8,128)(2,1)S(1)} %cross.3._.after_ref.refs_0_.refs_3_), custom_call_target="tpu_custom_call" | custom-call | flops 4194304 | bytes 524288 | tf_op jit(solution)/shard_map/inverse/pallas_call | solution.py:417
  19.5 0.0 collective-permute-done.2.refs_4_
  19.5 0.4 %part.1.rest_5_.part_ref = f32[256,512]{1,0:T(8,128)S(1)} custom-call(bf16[512,512]{1,0:T(8,128)(2,1)S(1)} %inverse.1.table_ref, bf16[8,32,512]{2,1,0:T(8,128)(2,1)S(1)} %cross.3._.after_ref.refs_0_.refs_3_, bf16[8,32,512]{2,1,0:T(8,128)(2,1)S(1)} %cross.4.refs_1_.refs_3_, bf16[8,32,512]{2,1,0:T(8,128)(2,1)S(1)} %cross.5.refs_2_, ...), custom_call_target="tpu_custom_call" | custom-call | flops 268435456 | bytes 1048576 | tf_op jit(solution)/shard_map/part/pallas_call | solution.py:444
  20.0 0.2 collective-permute-done.5.rest_4_
  20.2 1.2 %lags.2.rest_0_ = bf16[8,64,512]{2,1,0:T(8,128)(2,1)} custom-call(bf16[512,512]{1,0:T(8,128)(2,1)S(1)} %inverse.1.table_ref, bf16[8,32,512]{2,1,0:T(8,128)(2,1)S(1)} %get-tuple-element.30.refs_0_.rest_0_, bf16[8,32,512]{2,1,0:T(8,128)(2,1)S(1)} %get-tuple-element.31.refs_1_.rest_1_, bf16[8,32,512]{2,1,0:T(8,128)(2,1)S(1)} %get-tuple-element.32.rest_2_, ...), custom_call_target="tpu_custom_call" | custom-call | flops 268435456 | bytes 1048576 | tf_op jit(solution)/shard_map/lags/pallas_call | solution.py:428
  21.3 3.0 %collective-permute-done.3.more_ref = bf16[8,32,512]{2,1,0:T(8,128)(2,1)S(1)} collective-permute-done((bf16[8,32,512]{2,1,0:T(8,128)(2,1)S(1)}, bf16[8,32,512]{2,1,0:T(8,128)(2,1)S(1)}, u32[]{:S(2)}, u32[]{:S(2)}) %collective-permute-start.3) | collective-permute-done | bytes 262176 | tf_op jit(solution)/shard_map/ppermute | solution.py:404
  24.4 1.0 %lags.3 = bf16[8,64,512]{2,1,0:T(8,128)(2,1)} custom-call(bf16[512,512]{1,0:T(8,128)(2,1)S(1)} %inverse.1.table_ref, f32[256,512]{1,0:T(8,128)S(1)} %part.1.rest_5_.part_ref, bf16[8,32,512]{2,1,0:T(8,128)(2,1)S(1)} %collective-permute-done.3.more_ref, bf16[8,64,512]{2,1,0:T(8,128)(2,1)} %lags.2.rest_0_), custom_call_target="tpu_custom_call", output_to_operand_aliasing={{}: (3, {})} | custom-call | flops 268435456 | bytes 1048576 | tf_op jit(solution)/shard_map/lags/pallas_call | solution.py:428
  (4 shorter events, 0.1 us)
Async XLA Ops:
  0.0 3.5 %copy-start = (bf16[64,8,512]{2,1,0:T(8,128)(2,1)S(1)}, bf16[64,8,512]{2,1,0:T(8,128)(2,1)}, u32[]{:S(2)}) copy-start(bf16[64,8,512]{2,1,0:T(8,128)(2,1)} %param.3) | copy-start | bytes 1572868
  1.5 5.8 %collective-permute-start = (bf16[32,4096]{1,0:T(8,128)(2,1)S(1)}, bf16[32,4096]{1,0:T(8,128)(2,1)S(1)}, u32[]{:S(2)}, u32[]{:S(2)}) collective-permute-start(bf16[32,4096]{1,0:T(8,128)(2,1)S(1)} %get-tuple-element.23.edge_ref), channel_id=1, source_target_pairs={{4,0},{8,4},{12,8},{16,12},{20,16},{24,20},{28,24},{5,1},{9,5},{13... | collective-permute-start | bytes 786440 | tf_op jit(solution)/shard_map/ppermute | solution.py:362
  3.5 8.3 %collective-permute-start.4 = (bf16[8,32,512]{2,1,0:T(8,128)(2,1)S(1)}, bf16[8,32,512]{2,1,0:T(8,128)(2,1)S(1)}, u32[]{:S(2)}, u32[]{:S(2)}) collective-permute-start(bf16[8,32,512]{2,1,0:T(8,128)(2,1)S(1)} %get-tuple-element.30.refs_0_.rest_0_), channel_id=1, source_target_pairs={{0,2},{1,3},{4,5},{5,4},{6,7},{8,10},{9,11},{12,13},{13,12},{14,15... | collective-permute-start | bytes 786440 | tf_op jit(solution)/shard_map/ppermute | solution.py:404
  7.3 8.6 %collective-permute-start.1 = (bf16[8,32,512]{2,1,0:T(8,128)(2,1)S(1)}, bf16[8,32,512]{2,1,0:T(8,128)(2,1)S(1)}, u32[]{:S(2)}, u32[]{:S(2)}) collective-permute-start(bf16[8,32,512]{2,1,0:T(8,128)(2,1)S(1)} %cross.3._.after_ref.refs_0_.refs_3_), channel_id=1, source_target_pairs={{0,2},{1,3},{4,5},{5,4},{8,10},{9,11},{12,13},{13,12},{16,18},{17,... | collective-permute-start | bytes 786440 | tf_op jit(solution)/shard_map/ppermute | solution.py:404
  8.6 10.9 %collective-permute-start.2 = (bf16[8,32,512]{2,1,0:T(8,128)(2,1)S(1)}, bf16[8,32,512]{2,1,0:T(8,128)(2,1)S(1)}, u32[]{:S(2)}, u32[]{:S(2)}) collective-permute-start(bf16[8,32,512]{2,1,0:T(8,128)(2,1)S(1)} %cross.3._.after_ref.refs_0_.refs_3_), channel_id=1, source_target_pairs={{6,7},{14,15},{22,23},{30,31}} | collective-permute-start | bytes 786440 | tf_op jit(solution)/shard_map/ppermute | solution.py:404
  11.9 8.3 %collective-permute-start.5 = (bf16[8,32,512]{2,1,0:T(8,128)(2,1)S(1)}, bf16[8,32,512]{2,1,0:T(8,128)(2,1)S(1)}, u32[]{:S(2)}, u32[]{:S(2)}) collective-permute-start(bf16[8,32,512]{2,1,0:T(8,128)(2,1)S(1)} %mix.3), channel_id=1, source_target_pairs={{0,1},{2,3},{3,2},{4,6},{5,7},{8,9},{10,11},{11,10},{12,14},{13,15... | collective-permute-start | bytes 786440 | tf_op jit(solution)/shard_map/ppermute | solution.py:404
  16.1 8.3 %collective-permute-start.3 = (bf16[8,32,512]{2,1,0:T(8,128)(2,1)S(1)}, bf16[8,32,512]{2,1,0:T(8,128)(2,1)S(1)}, u32[]{:S(2)}, u32[]{:S(2)}) collective-permute-start(bf16[8,32,512]{2,1,0:T(8,128)(2,1)S(1)} %mix.2.after_ref), channel_id=1, source_target_pairs={{0,1},{2,3},{3,2},{4,6},{5,7},{8,9},{10,11},{11,10},{12,14},{13,15... | collective-permute-start | bytes 786440 | tf_op jit(solution)/shard_map/ppermute | solution.py:404

commit v3 on v2

--- a/solution.py
+++ b/solution.py
@@ -231,6 +231,30 @@
         stack_pairs(pick_ref, white_ref, near_ref, parts_refs, out_ref)
 
 
+def last_cross_kernel(
+    limits,
+    limits_b,
+    pick_ref,
+    early_white_ref,
+    early_short_ref,
+    white_ref,
+    short_ref,
+    edge_ref,
+    after_ref,
+    out_ref,
+    near_ref,
+    *parts_refs,
+):
+    span = short_ref.shape[0]
+    for late, heads, shorts in ((0, early_white_ref, early_short_ref), (2, white_ref, short_ref)):
+
+        @pl.when((role(limits_b) == 2) & (role(limits) == late))
+        def _(heads=heads, shorts=shorts):
+            near_ref[:span] = shorts[...]
+            near_ref[span:] = edge_ref[...]
+            stack_pairs(pick_ref, heads, near_ref, parts_refs, out_ref)
+
+
 def chosen(options, place):
     value = jnp.float32(options[0])
     for i, option in enumerate(options[1:]):
@@ -358,12 +382,21 @@
         name="head",
     )(in_hbm(flat), in_hbm(valid.T), in_hbm(offsets))
 
-    ring = lax.axis_size("chan")
-    edge = lax.ppermute(short_a, "chan", [(i, i - 1) for i in range(1, ring)])
-
     columns = min(d for d in range(1, groups + 1) if groups % d == 0 and d * d >= groups)
     square = columns == 2 and groups == columns * columns
-    limits = (2, 3) if square else (groups, groups)
+    limits, limits_b = ((2, 3), (2, 2)) if square else ((groups, groups), (groups, groups))
+    ring = lax.axis_size("chan")
+
+    def to_previous(odd, even):
+        moves = [
+            (c * groups + h, (c - 1) * groups + h)
+            for c in range(1, ring)
+            for h in (odd if c % 2 else even)
+        ]
+        return lax.ppermute(short_a, ("chan", "tm"), moves)
+
+    edge = to_previous(range(groups), range(limits_b[0]))
+    edge_last = to_previous([], range(limits_b[0], groups)) if square else edge
 
     def tail(now, after):
         return pl.pallas_call(
@@ -377,22 +410,24 @@
             name="tail",
         )(flat, table, keep, pick, white_a, short_a, after)
 
-    def cross(now, white, short, after):
+    def cross(kernel, halves, edge, after):
         return pl.pallas_call(
-            functools.partial(cross_kernel, limits, now),
+            kernel,
             out_shape=local_type,
-            in_specs=[whole()] * 4 + [whole(pl.ANY)],
+            in_specs=[whole()] * (2 + len(halves)) + [whole(pl.ANY)],
             out_specs=whole(),
             scratch_shapes=[near_scratch] + parts_scratch,
             compiler_params=params,
             cost_estimate=cost(pairs * span * wins * bins * 8, 4 * 1024 * 1024),
             name="cross",
-        )(pick, white, short, edge, after)
+        )(pick, *halves, edge, after)
 
     white_b, short_b, local_a = tail(0, table)
-    local_b = cross(0, white_b, short_b, table)
+    local_b = cross(functools.partial(cross_kernel, limits_b, 0), [white_b, short_b], edge, table)
     white_late, short_late, late_a = tail(1, local_b)
-    late_b = cross(1, white_late, short_late, local_b)
+    late_b = cross(
+        functools.partial(cross_kernel, limits_b, 1), [white_late, short_late], edge, local_b
+    )
 
     power = [float(np.float32(factor) ** np.float32(d)) for d in range(groups)]
     def sent(value, even, odd):
@@ -403,16 +438,16 @@
         ]
         return lax.ppermute(value, ("chan", "tm"), moves)
 
-    def mix(terms, weights, after):
+    def mix(terms, weights, limits_of, after):
         return pl.pallas_call(
-            functools.partial(mix_kernel, limits, weights),
+            functools.partial(mix_kernel, limits_of, weights),
             out_shape=local_type,
-            in_specs=[whole()] * len(terms) + [whole(pl.ANY)],
+            in_specs=[whole()] * len(terms) + [whole(pl.ANY)] * len(after),
             out_specs=whole(),
             compiler_params=params,
             cost_estimate=cost(len(terms) * terms[0].size * 4, 1024 * 1024),
             name="mix",
-        )(*terms, after)
+        )(*terms, *after)
 
     inverse = pl.pallas_call(
         inverse_kernel,
@@ -440,27 +475,27 @@
             name="lags",
         )(inverse, *terms, *later, *so_far)
 
-    def part(terms, weights):
+    def part(terms, weights, after):
         return pl.pallas_call(
-            functools.partial(part_kernel, limits, weights),
+            functools.partial(part_kernel, limits_b, weights),
             out_shape=jax.ShapeDtypeStruct((pairs * span, length), jnp.float32),
-            in_specs=[whole()] * (1 + len(terms)),
+            in_specs=[whole()] * (1 + len(terms)) + [whole(pl.ANY)],
             out_specs=whole(),
             compiler_params=params,
             cost_estimate=cost(pairs * span * length * length * 4, 1024 * 1024),
             name="part",
-        )(inverse, *terms)
+        )(inverse, *terms, after)
 
     unit = [1.0] * (2 * groups)
 
-    def two_hops(local, late, after, apart):
+    def two_hops(local, late, limits_of, after, alone):
         f, ff = power[1], power[2]
         last = [(2, 3)]
-        got = sent(local, [(0, 2), (1, 3)], [(0, 1), (1, 0)] + ([] if apart else last))
-        alone = [sent(local, [], last)] if apart else []
+        got = sent(local, [(0, 2), (1, 3)], [(0, 1), (1, 0)] + ([] if alone else last))
         total = mix(
             [local, late, got],
             [[1.0, 1.0, 1.0, 0.0, f, 1.0, 0.0, 0.0], [ff, ff, ff, 1.0, 1.0, f, 0.0, 0.0]],
+            limits_of,
             after,
         )
         more = sent(total, [(0, 1), (2, 3), (3, 2)], [(0, 2), (1, 3)])
@@ -468,10 +503,10 @@
             unit,
             [ff, ff, ff, ff, 0.0, f, 0.0, f],
         ]
-        weights += [[f] * (2 * groups)] * len(alone) + [[f, f, f, f, 0.0, 0.0, f, ff]]
-        return total, [got] + alone + [more], weights
-
-    def one_hop(local, late, after, apart):
+        weights.append([f, f, f, f, 0.0, 0.0, f, ff])
+        return total, [got, more], weights
+
+    def one_hop(local, late, limits_of, after, alone):
         terms, weights = [], [unit]
         for d in range(1, groups):
             moves = [(h, h + d) for h in range(groups - d)]
@@ -481,15 +516,21 @@
 
     spread = two_hops if square else one_hop
     scale = bins**-0.5
-    _, terms_a, weights_a = spread(local_a, late_a, late_b, False)
-    ahead, terms_b, weights_b = spread(local_b, late_b, local_b, True)
-    white_last, short_last, last_a = tail(2, ahead)
-    last_b = cross(2, white_last, short_last, ahead)
-    terms_a = [local_a, late_a, last_a] + terms_a
-    terms_b = [local_b, late_b, last_b] + terms_b
-    before = part(terms_b[:-1], weights_b[:-1])
+    white_last, short_last, last_a = tail(2, local_b)
+    ahead, terms_a, weights_a = spread(local_a, late_a, limits, [late_b, last_a], False)
+    _, terms_b, weights_b = spread(local_b, late_b, limits_b, [], True)
+    last_b = cross(
+        functools.partial(last_cross_kernel, limits, limits_b),
+        [white_b, short_b, white_last, short_last],
+        edge_last,
+        ahead,
+    )
+    if square:
+        terms_b[1:1] = [sent(last_b, [], [(2, 3)])]
+        weights_b[2:2] = [[power[1]] * (2 * groups)]
     first = functools.partial(lag_kernel, limits, scale, 0, weights_a)
-    result = written(first, terms_a, [before])
+    result = written(first, [local_a, late_a, last_a] + terms_a, [])
+    before = part([local_b, late_b, last_b] + terms_b[:-1], weights_b[:-1], result)
     last = functools.partial(last_kernel, scale, half, weights_b[-1])
     result = written(last, [before, terms_b[-1]], [], result)
     return result.reshape(1, pairs, chans, length)

time: 25.6 us -> 29.5 us (1.15)
  starting transfers between devices: 11.6 us -> 13.4 us
  local copies, waits for them, and re-layouts: 0.01 us -> 1.04 us
  waiting for transfers between devices: 6.79 us -> 7.75 us
    ppermute x1 -> x2, starting transfers between devices: 1.92 us -> 6.24 us  [to_previous(): return lax.ppermute(short_a, ('chan', 'tm'), moves)]
    ppermute x5, waiting for transfers between devices: 4.26 us -> 7.74 us  [sent(): return lax.ppermute(value, ('chan', 'tm'), moves)]
    ppermute x5, starting transfers between devices: 9.69 us -> 7.13 us  [sent(): return lax.ppermute(value, ('chan', 'tm'), moves)]
    ppermute x1 -> x2, waiting for transfers between devices: 2.53 us -> 0.01 us  [to_previous(): return lax.ppermute(short_a, ('chan', 'tm'), moves)]
    unnamed x2 -> x4, local copies, waits for them, and re-layouts: 0.01 us -> 1.04 us
  transfers between devices with their start and end apart: 6 -> 7, of which waited for: 5 -> 2; matrix products, arithmetic and copies ran while one was open for 0% -> 0% of each run, Pallas kernels for 17% -> 15%
where the time goes in v3:
time: 29.5 us; the launch traced here: 29.2 us
  starting transfers between devices  13.4 us (45%)
  waiting for transfers between devices  7.75 us (26%)
  Pallas kernels  6.85 us (23%)
  local copies, waits for them, and re-layouts  1.04 us (4%)
    ppermute x5, waiting for transfers between devices, sent(): return lax.ppermute(value, ('chan', 'tm'), moves)  7.74 us
    ppermute x5, starting transfers between devices, sent(): return lax.ppermute(value, ('chan', 'tm'), moves)  7.13 us
    ppermute x2, starting transfers between devices, to_previous(): return lax.ppermute(short_a, ('chan', 'tm'), moves)  6.24 us
    pallas_call x2, Pallas kernels, written(): pl.pallas_call(kernel, out_shape=jax.ShapeDtypeStruct((pairs, chans, leng...  2.18 us
    pallas_call x1, Pallas kernels, per_device(): pl.pallas_call(head_kernel, out_shape=(white_type, short_type, jax.ShapeD...  1.54 us
    pallas_call x3, Pallas kernels, tail(): pl.pallas_call(functools.partial(tail_kernel, limits, now), out_shape=(wh...  1.33 us
    unnamed x4, local copies, waits for them, and re-layouts  1.04 us
    pallas_call x3, Pallas kernels, cross(): pl.pallas_call(kernel, out_shape=local_type, in_specs=[whole()] * (2 + le...  0.82 us
  transfers between devices with their start and end apart: 7, of which 2 were waited for; matrix products, arithmetic and copies ran while one was open for 0% of the time, Pallas kernels for 15%

profile of v3, /device:TPU:28, one launch (start us, length us, event | category | flops | bytes accessed | tf_op | source)
XLA Modules:
  0.0 29.2 jit_solution(15712197040912192921)
XLA Ops:
  0.0 0.0 copy-start
  0.0 1.5 %head.1 = (f32[8,32,512]{2,1,0:T(8,128)S(1)}, bf16[32,4096]{1,0:T(8,128)(2,1)S(1)}, bf16[512,512]{1,0:T(8,128)(2,1)S(1)}, bf16[8,32,64]{2,1,0:T(8,128)(2,1)S(1)}, f32[64,1024]{1,0:T(8,128)S(1)}) custom-call(bf16[512,512]{1,0:T(8,128)(2,1)} %bitcast.3, s32[8,64]{1,0:T(8,128)} %bitcast.7, s32[8]{0:T(128)} %offsets_hbm.1), custom_call_target="tpu_custom_call" | custom-call | flops 134217728 | bytes 2097152 | tf_op jit(solution)/shard_map/head/pallas_call | solution.py:362
  1.5 1.3 %collective-permute-start = (bf16[32,4096]{1,0:T(8,128)(2,1)S(1)}, bf16[32,4096]{1,0:T(8,128)(2,1)S(1)}, u32[]{:S(2)}, u32[]{:S(2)}) collective-permute-start(bf16[32,4096]{1,0:T(8,128)(2,1)S(1)} %get-tuple-element.23.edge_ref), channel_id=1, source_target_pairs={{4,0},{5,1},{6,2},{7,3},{8,4},{9,5},{12,8},{13,9},{14,10},{15,11},... | collective-permute-start | bytes 786440 | tf_op jit(solution)/shard_map/ppermute | solution.py:396
  2.8 0.0 copy-done
  2.9 1.3 %collective-permute-start.2 = (bf16[8,32,512]{2,1,0:T(8,128)(2,1)S(1)}, bf16[8,32,512]{2,1,0:T(8,128)(2,1)S(1)}, u32[]{:S(2)}, u32[]{:S(2)}) collective-permute-start(bf16[8,32,512]{2,1,0:T(8,128)(2,1)S(1)} %get-tuple-element.30.refs_0_.rest_0_), channel_id=1, source_target_pairs={{0,2},{1,3},{4,5},{5,4},{6,7},{8,10},{9,11},{12,13},{13,12},{14,15... | collective-permute-start | bytes 786440 | tf_op jit(solution)/shard_map/ppermute | solution.py:439
  4.2 5.0 %collective-permute-start.1 = (bf16[32,4096]{1,0:T(8,128)(2,1)S(1)}, bf16[32,4096]{1,0:T(8,128)(2,1)S(1)}, u32[]{:S(2)}, u32[]{:S(2)}) collective-permute-start(bf16[32,4096]{1,0:T(8,128)(2,1)S(1)} %get-tuple-element.23.edge_ref), channel_id=1, source_target_pairs={{10,6},{11,7},{18,14},{19,15},{26,22},{27,23}} | collective-permute-start | bytes 786440 | tf_op jit(solution)/shard_map/ppermute | solution.py:396
  9.2 0.0 collective-permute-done.edge_ref
  9.2 1.3 %collective-permute-start.3 = (bf16[8,32,512]{2,1,0:T(8,128)(2,1)S(1)}, bf16[8,32,512]{2,1,0:T(8,128)(2,1)S(1)}, u32[]{:S(2)}, u32[]{:S(2)}) collective-permute-start(bf16[8,32,512]{2,1,0:T(8,128)(2,1)S(1)} %cross.3._.after_ref.refs_0_), channel_id=1, source_target_pairs={{0,2},{1,3},{4,5},{5,4},{8,10},{9,11},{12,13},{13,12},{16,18},{17,... | collective-permute-start | bytes 786440 | tf_op jit(solution)/shard_map/ppermute | solution.py:439
  10.5 1.3 %tail.4 = (f32[8,32,512]{2,1,0:T(8,128)S(1)}, bf16[32,4096]{1,0:T(8,128)(2,1)S(1)}, bf16[8,32,512]{2,1,0:T(8,128)(2,1)S(1)}) custom-call(bf16[512,512]{1,0:T(8,128)(2,1)S(1)} %bitcast.5, bf16[512,512]{1,0:T(8,128)(2,1)S(1)} %get-tuple-element.20.table_ref.after_ref, f32[64,1024]{1,0:T(8,128)S(1)} %get-tuple-element.21.keep_ref, ...), custom_call_target="tpu_custom_call" | custom-call | flops 268435456 | bytes 4194304 | tf_op jit(solution)/shard_map/tail/pallas_call | solution.py:402
  11.8 0.8 %cross.4.refs_3_.refs_1_ = bf16[8,32,512]{2,1,0:T(8,128)(2,1)S(1)} custom-call(bf16[8,32,64]{2,1,0:T(8,128)(2,1)S(1)} %get-tuple-element.19.pick_ref, f32[8,32,512]{2,1,0:T(8,128)S(1)} %get-tuple-element.26.white_ref, bf16[32,4096]{1,0:T(8,128)(2,1)S(1)} %get-tuple-element.27.short_ref, bf16[32,4096]{1,0:T(8,128)(2,1)S(1)} %collective-permute-done.edge_ref, ...), custom_call_target="tpu_custom_call" | custom-call | flops 4194304 | bytes 4194304 | tf_op jit(solution)/shard_map/cross/pallas_call | solution.py:414
  12.6 0.0 collective-permute-done.2.refs_2_.rest_3_
  12.6 0.1 mix.2.after_ref
  12.7 2.0 %collective-permute-start.5 = (bf16[8,32,512]{2,1,0:T(8,128)(2,1)S(1)}, bf16[8,32,512]{2,1,0:T(8,128)(2,1)S(1)}, u32[]{:S(2)}, u32[]{:S(2)}) collective-permute-start(bf16[8,32,512]{2,1,0:T(8,128)(2,1)S(1)} %mix.2.after_ref), channel_id=1, source_target_pairs={{0,1},{2,3},{3,2},{4,6},{5,7},{8,9},{10,11},{11,10},{12,14},{13,15... | collective-permute-start | bytes 786440 | tf_op jit(solution)/shard_map/ppermute | solution.py:439
  14.7 0.0 collective-permute-done.1.edge_ref
  14.7 0.7 %collective-permute-start.4 = (bf16[8,32,512]{2,1,0:T(8,128)(2,1)S(1)}, bf16[8,32,512]{2,1,0:T(8,128)(2,1)S(1)}, u32[]{:S(2)}, u32[]{:S(2)}) collective-permute-start(bf16[8,32,512]{2,1,0:T(8,128)(2,1)S(1)} %cross.5.refs_2_), channel_id=1, source_target_pairs={{6,7},{14,15},{22,23},{30,31}} | collective-permute-start | bytes 786440 | tf_op jit(solution)/shard_map/ppermute | solution.py:439
  15.4 4.4 %collective-permute-done.3.refs_3_.refs_2_ = bf16[8,32,512]{2,1,0:T(8,128)(2,1)S(1)} collective-permute-done((bf16[8,32,512]{2,1,0:T(8,128)(2,1)S(1)}, bf16[8,32,512]{2,1,0:T(8,128)(2,1)S(1)}, u32[]{:S(2)}, u32[]{:S(2)}) %collective-permute-start.3) | collective-permute-done | bytes 262176 | tf_op jit(solution)/shard_map/ppermute | solution.py:439
  19.8 0.1 mix.3
  19.9 1.9 %collective-permute-start.6 = (bf16[8,32,512]{2,1,0:T(8,128)(2,1)S(1)}, bf16[8,32,512]{2,1,0:T(8,128)(2,1)S(1)}, u32[]{:S(2)}, u32[]{:S(2)}) collective-permute-start(bf16[8,32,512]{2,1,0:T(8,128)(2,1)S(1)} %mix.3), channel_id=1, source_target_pairs={{0,1},{2,3},{3,2},{4,6},{5,7},{8,9},{10,11},{11,10},{12,14},{13,15... | collective-permute-start | bytes 786440 | tf_op jit(solution)/shard_map/ppermute | solution.py:439
  21.9 0.3 %inverse.1.table_ref = bf16[512,512]{1,0:T(8,128)(2,1)S(1)} custom-call(bf16[8,32,512]{2,1,0:T(8,128)(2,1)S(1)} %cross.3._.after_ref.refs_0_), custom_call_target="tpu_custom_call" | custom-call | flops 4194304 | bytes 524288 | tf_op jit(solution)/shard_map/inverse/pallas_call | solution.py:452
  22.2 0.0 collective-permute-done.5.rest_4_
  22.2 1.2 %lags.2.refs_5_.rest_0_ = bf16[8,64,512]{2,1,0:T(8,128)(2,1)} custom-call(bf16[512,512]{1,0:T(8,128)(2,1)S(1)} %inverse.1.table_ref, bf16[8,32,512]{2,1,0:T(8,128)(2,1)S(1)} %get-tuple-element.30.refs_0_.rest_0_, bf16[8,32,512]{2,1,0:T(8,128)(2,1)S(1)} %get-tuple-element.31.refs_1_.rest_1_, bf16[8,32,512]{2,1,0:T(8,128)(2,1)S(1)} %get-tuple-element.32.refs_4_.rest_2_, ...), custom_call_target="tpu_custom_call" | custom-call | flops 268435456 | bytes 1048576 | tf_op jit(solution)/shard_map/lags/pallas_call | solution.py:463
  23.3 0.0 collective-permute-done.4.refs_4_
  23.4 0.0 copy-start.1
  23.4 1.0 %copy-done.1 = bf16[8,64,512]{2,1,0:T(8,128)(2,1)S(1)} copy-done((bf16[8,64,512]{2,1,0:T(8,128)(2,1)S(1)}, bf16[8,64,512]{2,1,0:T(8,128)(2,1)}, u32[]{:S(2)}) %copy-start.1) | copy-done | bytes 524312
  24.4 0.4 %part.1.part_ref = f32[256,512]{1,0:T(8,128)S(1)} custom-call(bf16[512,512]{1,0:T(8,128)(2,1)S(1)} %inverse.1.table_ref, bf16[8,32,512]{2,1,0:T(8,128)(2,1)S(1)} %cross.3._.after_ref.refs_0_, bf16[8,32,512]{2,1,0:T(8,128)(2,1)S(1)} %cross.4.refs_3_.refs_1_, bf16[8,32,512]{2,1,0:T(8,128)(2,1)S(1)} %cross.5.refs_2_, ...), custom_call_target="tpu_custom_call" | custom-call | flops 268435456 | bytes 1048576 | tf_op jit(solution)/shard_map/part/pallas_call | solution.py:479
  24.8 3.4 %collective-permute-done.6.more_ref = bf16[8,32,512]{2,1,0:T(8,128)(2,1)S(1)} collective-permute-done((bf16[8,32,512]{2,1,0:T(8,128)(2,1)S(1)}, bf16[8,32,512]{2,1,0:T(8,128)(2,1)S(1)}, u32[]{:S(2)}, u32[]{:S(2)}) %collective-permute-start.6) | collective-permute-done | bytes 262176 | tf_op jit(solution)/shard_map/ppermute | solution.py:439
  28.2 1.0 %lags.3 = bf16[8,64,512]{2,1,0:T(8,128)(2,1)} custom-call(bf16[512,512]{1,0:T(8,128)(2,1)S(1)} %inverse.1.table_ref, f32[256,512]{1,0:T(8,128)S(1)} %part.1.part_ref, bf16[8,32,512]{2,1,0:T(8,128)(2,1)S(1)} %collective-permute-done.6.more_ref, bf16[8,64,512]{2,1,0:T(8,128)(2,1)} %lags.2.refs_5_.rest_0_), custom_call_target="tpu_custom_call", output_to_operand_aliasing={{}: (3, {})} | custom-call | flops 268435456 | bytes 1048576 | tf_op jit(solution)/shard_map/lags/pallas_call | solution.py:463
  (4 shorter events, 0.1 us)
Async XLA Ops:
  0.0 2.9 %copy-start = (bf16[64,8,512]{2,1,0:T(8,128)(2,1)S(1)}, bf16[64,8,512]{2,1,0:T(8,128)(2,1)}, u32[]{:S(2)}) copy-start(bf16[64,8,512]{2,1,0:T(8,128)(2,1)} %param.3) | copy-start | bytes 1572868
  1.5 7.6 %collective-permute-start = (bf16[32,4096]{1,0:T(8,128)(2,1)S(1)}, bf16[32,4096]{1,0:T(8,128)(2,1)S(1)}, u32[]{:S(2)}, u32[]{:S(2)}) collective-permute-start(bf16[32,4096]{1,0:T(8,128)(2,1)S(1)} %get-tuple-element.23.edge_ref), channel_id=1, source_target_pairs={{4,0},{5,1},{6,2},{7,3},{8,4},{9,5},{12,8},{13,9},{14,10},{15,11},... | collective-permute-start | bytes 786440 | tf_op jit(solution)/shard_map/ppermute | solution.py:396
  2.9 9.7 %collective-permute-start.2 = (bf16[8,32,512]{2,1,0:T(8,128)(2,1)S(1)}, bf16[8,32,512]{2,1,0:T(8,128)(2,1)S(1)}, u32[]{:S(2)}, u32[]{:S(2)}) collective-permute-start(bf16[8,32,512]{2,1,0:T(8,128)(2,1)S(1)} %get-tuple-element.30.refs_0_.rest_0_), channel_id=1, source_target_pairs={{0,2},{1,3},{4,5},{5,4},{6,7},{8,10},{9,11},{12,13},{13,12},{14,15... | collective-permute-start | bytes 786440 | tf_op jit(solution)/shard_map/ppermute | solution.py:439
  4.2 10.5 %collective-permute-start.1 = (bf16[32,4096]{1,0:T(8,128)(2,1)S(1)}, bf16[32,4096]{1,0:T(8,128)(2,1)S(1)}, u32[]{:S(2)}, u32[]{:S(2)}) collective-permute-start(bf16[32,4096]{1,0:T(8,128)(2,1)S(1)} %get-tuple-element.23.edge_ref), channel_id=1, source_target_pairs={{10,6},{11,7},{18,14},{19,15},{26,22},{27,23}} | collective-permute-start | bytes 786440 | tf_op jit(solution)/shard_map/ppermute | solution.py:396
  9.2 10.6 %collective-permute-start.3 = (bf16[8,32,512]{2,1,0:T(8,128)(2,1)S(1)}, bf16[8,32,512]{2,1,0:T(8,128)(2,1)S(1)}, u32[]{:S(2)}, u32[]{:S(2)}) collective-permute-start(bf16[8,32,512]{2,1,0:T(8,128)(2,1)S(1)} %cross.3._.after_ref.refs_0_), channel_id=1, source_target_pairs={{0,2},{1,3},{4,5},{5,4},{8,10},{9,11},{12,13},{13,12},{16,18},{17,... | collective-permute-start | bytes 786440 | tf_op jit(solution)/shard_map/ppermute | solution.py:439
  12.7 9.4 %collective-permute-start.5 = (bf16[8,32,512]{2,1,0:T(8,128)(2,1)S(1)}, bf16[8,32,512]{2,1,0:T(8,128)(2,1)S(1)}, u32[]{:S(2)}, u32[]{:S(2)}) collective-permute-start(bf16[8,32,512]{2,1,0:T(8,128)(2,1)S(1)} %mix.2.after_ref), channel_id=1, source_target_pairs={{0,1},{2,3},{3,2},{4,6},{5,7},{8,9},{10,11},{11,10},{12,14},{13,15... | collective-permute-start | bytes 786440 | tf_op jit(solution)/shard_map/ppermute | solution.py:439
  14.7 8.6 %collective-permute-start.4 = (bf16[8,32,512]{2,1,0:T(8,128)(2,1)S(1)}, bf16[8,32,512]{2,1,0:T(8,128)(2,1)S(1)}, u32[]{:S(2)}, u32[]{:S(2)}) collective-permute-start(bf16[8,32,512]{2,1,0:T(8,128)(2,1)S(1)} %cross.5.refs_2_), channel_id=1, source_target_pairs={{6,7},{14,15},{22,23},{30,31}} | collective-permute-start | bytes 786440 | tf_op jit(solution)/shard_map/ppermute | solution.py:439
  19.9 8.3 %collective-permute-start.6 = (bf16[8,32,512]{2,1,0:T(8,128)(2,1)S(1)}, bf16[8,32,512]{2,1,0:T(8,128)(2,1)S(1)}, u32[]{:S(2)}, u32[]{:S(2)}) collective-permute-start(bf16[8,32,512]{2,1,0:T(8,128)(2,1)S(1)} %mix.3), channel_id=1, source_target_pairs={{0,1},{2,3},{3,2},{4,6},{5,7},{8,9},{10,11},{11,10},{12,14},{13,15... | collective-permute-start | bytes 786440 | tf_op jit(solution)/shard_map/ppermute | solution.py:439
  23.4 1.0 %copy-start.1 = (bf16[8,64,512]{2,1,0:T(8,128)(2,1)S(1)}, bf16[8,64,512]{2,1,0:T(8,128)(2,1)}, u32[]{:S(2)}) copy-start(bf16[8,64,512]{2,1,0:T(8,128)(2,1)} %lags.2.refs_5_.rest_0_) | copy-start | bytes 1572868

commit v4 on v2

--- a/solution.py
+++ b/solution.py
@@ -12,6 +12,7 @@
 OFFSET_SPAN = 32
 LANES = 128
 DECAY = 0.99
+X_PIECES = 4
 VMEM = 24 * 1024 * 1024
 
 
@@ -119,16 +120,19 @@
 ):
     wins, span, length = white_ref.shape
     pairs = offsets_ref.shape[0]
-    copies = [
-        pltpu.make_async_copy(valid_hbm, valid_ref, sems.at[0]),
-        pltpu.make_async_copy(offsets_hbm, offsets_ref, sems.at[1]),
-        pltpu.make_async_copy(x_hbm.at[pl.ds(0, span * wins)], x_ref, sems.at[2]),
+    valid_copy = pltpu.make_async_copy(valid_hbm, valid_ref, sems.at[0])
+    offsets_copy = pltpu.make_async_copy(offsets_hbm, offsets_ref, sems.at[1])
+    size = span * wins // X_PIECES
+    pieces = [pl.ds(i * size, size) for i in range(X_PIECES)]
+    x_copies = [
+        pltpu.make_async_copy(x_hbm.at[piece], x_ref.at[piece], sems.at[2 + i])
+        for i, piece in enumerate(pieces)
     ]
-    for copy in copies:
+    for copy in x_copies + [valid_copy, offsets_copy]:
         copy.start()
     fill_table(table_ref, 16)
-    copies[0].wait()
-    copies[1].wait()
+    valid_copy.wait()
+    offsets_copy.wait()
     ahead = lax.broadcasted_iota(jnp.int32, (span, 2 * span), 1) - lax.broadcasted_iota(
         jnp.int32, (span, 2 * span), 0
     )
@@ -143,7 +147,8 @@
         (((0,), (0,)), ((), ())),
         preferred_element_type=jnp.float32,
     )
-    copies[2].wait()
+    for copy in x_copies:
+        copy.wait()
     whiten_block(x_ref[...], table_ref, keep_ref[:span], raw_ref, white_ref, short_ref)
 
 
@@ -280,29 +285,37 @@
 
 
 def lag_kernel(limits, scale, first, weights, table_ref, *rest):
-    out_hbm, stage_ref, sem = rest[-3:]
+    out_hbm, stage_ref, sems = rest[-3:]
     place = whereabouts(len(weights[0]) // 2)
     pairs, rows, length = stage_ref.shape
     stack = weighted(limits, rest[: len(weights) + 2], weights, place)
     stack = stack.reshape(pairs * rows, length)
     lagged = to_lags(stack, table_ref[...]) * scale
     stage_ref[...] = lagged.astype(stage_ref.dtype).reshape(pairs, rows, length)
-    copy = pltpu.make_async_copy(stage_ref, out_hbm.at[:, pl.ds(first, rows)], sem)
+    copy = pltpu.make_async_copy(stage_ref, out_hbm.at[:, pl.ds(first, rows)], sems.at[0])
     copy.start()
     copy.wait()
 
 
 def last_kernel(scale, first, weights, table_ref, part_ref, more_ref, *rest):
-    out_hbm, stage_ref, sem = rest[-3:]
+    out_hbm, stage_ref, sems = rest[-3:]
     place = whereabouts(len(weights) // 2)
     pairs, rows, length = stage_ref.shape
     more = more_ref[...].reshape(pairs * rows, length)
     lagged = jnp.dot(more, table_ref[...], preferred_element_type=jnp.float32)
-    lagged = (part_ref[...] + lagged * chosen(weights, place)) * scale
-    stage_ref[...] = lagged.astype(stage_ref.dtype).reshape(pairs, rows, length)
-    copy = pltpu.make_async_copy(stage_ref, out_hbm.at[:, pl.ds(first, rows)], sem)
-    copy.start()
-    copy.wait()
+    weight = chosen(weights, place)
+    size = pairs // 2
+    copies = []
+    for piece in range(2):
+        here = slice(piece * size * rows, (piece + 1) * size * rows)
+        value = (part_ref[here] + lagged[here] * weight) * scale
+        there = pl.ds(piece * size, size)
+        stage_ref[there] = value.astype(stage_ref.dtype).reshape(size, rows, length)
+        target = out_hbm.at[there, pl.ds(first, rows)]
+        copies.append(pltpu.make_async_copy(stage_ref.at[there], target, sems.at[piece]))
+        copies[-1].start()
+    for copy in copies:
+        copy.wait()
 
 
 def cost(flops, moved):
@@ -351,7 +364,7 @@
             pltpu.VMEM((wins, chans), jnp.int32),
             pltpu.SMEM((pairs,), jnp.int32),
             raw_scratch,
-            pltpu.SemaphoreType.DMA((3,)),
+            pltpu.SemaphoreType.DMA((2 + X_PIECES,)),
         ],
         compiler_params=params,
         cost_estimate=cost(span * wins * length * length * 2, 2 * 1024 * 1024),
@@ -432,7 +445,7 @@
             out_specs=whole(pl.ANY),
             scratch_shapes=[
                 pltpu.VMEM((pairs, span, length), jnp.bfloat16),
-                pltpu.SemaphoreType.DMA,
+                pltpu.SemaphoreType.DMA((2,)),
             ],
             input_output_aliases={1 + len(terms) + len(later): 0} if so_far else {},
             compiler_params=params,

time: 25.6 us -> 25.7 us (level)
  no operation moved by 1% of the time
where the time goes in v4:
time: 25.7 us; the launch traced here: 25.4 us
  starting transfers between devices  11.6 us (45%)
  Pallas kernels  6.9 us (27%)
  waiting for transfers between devices  6.77 us (26%)
    ppermute x5, starting transfers between devices, sent(): return lax.ppermute(value, ('chan', 'tm'), moves)  9.69 us
    ppermute x5, waiting for transfers between devices, sent(): return lax.ppermute(value, ('chan', 'tm'), moves)  4.24 us
    ppermute x1, waiting for transfers between devices, per_device(): edge = lax.ppermute(short_a, 'chan', [(i, i - 1) for i in range(1, ring)])  2.53 us
    pallas_call x2, Pallas kernels, written(): pl.pallas_call(kernel, out_shape=jax.ShapeDtypeStruct((pairs, chans, leng...  2.15 us
    ppermute x1, starting transfers between devices, per_device(): edge = lax.ppermute(short_a, 'chan', [(i, i - 1) for i in range(1, ring)])  1.92 us
    pallas_call x1, Pallas kernels, per_device(): pl.pallas_call(head_kernel, out_shape=(white_type, short_type, jax.ShapeD...  1.63 us
    pallas_call x3, Pallas kernels, tail(): pl.pallas_call(functools.partial(tail_kernel, limits, now), out_shape=(wh...  1.33 us
    pallas_call x3, Pallas kernels, cross(): pl.pallas_call(functools.partial(cross_kernel, limits, now), out_shape=lo...  0.81 us
  transfers between devices with their start and end apart: 6, of which 5 were waited for; matrix products, arithmetic and copies ran while one was open for 0% of the time, Pallas kernels for 17%

profile of v4, /device:TPU:28, one launch (start us, length us, event | category | flops | bytes accessed | tf_op | source)
XLA Modules:
  0.0 25.4 jit_solution(11872526477325482019)
XLA Ops:
  0.0 0.0 copy-start
  0.0 1.6 %head.1 = (f32[8,32,512]{2,1,0:T(8,128)S(1)}, bf16[32,4096]{1,0:T(8,128)(2,1)S(1)}, bf16[512,512]{1,0:T(8,128)(2,1)S(1)}, bf16[8,32,64]{2,1,0:T(8,128)(2,1)S(1)}, f32[64,1024]{1,0:T(8,128)S(1)}) custom-call(bf16[512,512]{1,0:T(8,128)(2,1)} %bitcast.3, s32[8,64]{1,0:T(8,128)} %bitcast.7, s32[8]{0:T(128)} %offsets_hbm.1), custom_call_target="tpu_custom_call" | custom-call | flops 134217728 | bytes 2097152 | tf_op jit(solution)/shard_map/head/pallas_call | solution.py:351
  1.6 1.9 %collective-permute-start = (bf16[32,4096]{1,0:T(8,128)(2,1)S(1)}, bf16[32,4096]{1,0:T(8,128)(2,1)S(1)}, u32[]{:S(2)}, u32[]{:S(2)}) collective-permute-start(bf16[32,4096]{1,0:T(8,128)(2,1)S(1)} %get-tuple-element.23.edge_ref), channel_id=1, source_target_pairs={{4,0},{8,4},{12,8},{16,12},{20,16},{24,20},{28,24},{5,1},{9,5},{13... | collective-permute-start | bytes 786440 | tf_op jit(solution)/shard_map/ppermute | solution.py:375
  3.6 0.0 copy-done
  3.6 1.3 %collective-permute-start.4 = (bf16[8,32,512]{2,1,0:T(8,128)(2,1)S(1)}, bf16[8,32,512]{2,1,0:T(8,128)(2,1)S(1)}, u32[]{:S(2)}, u32[]{:S(2)}) collective-permute-start(bf16[8,32,512]{2,1,0:T(8,128)(2,1)S(1)} %get-tuple-element.30.refs_0_.rest_0_), channel_id=1, source_target_pairs={{0,2},{1,3},{4,5},{5,4},{6,7},{8,10},{9,11},{12,13},{13,12},{14,15... | collective-permute-start | bytes 786440 | tf_op jit(solution)/shard_map/ppermute | solution.py:417
  4.9 2.5 %collective-permute-done.edge_ref = bf16[32,4096]{1,0:T(8,128)(2,1)S(1)} collective-permute-done((bf16[32,4096]{1,0:T(8,128)(2,1)S(1)}, bf16[32,4096]{1,0:T(8,128)(2,1)S(1)}, u32[]{:S(2)}, u32[]{:S(2)}) %collective-permute-start) | collective-permute-done | bytes 262176 | tf_op jit(solution)/shard_map/ppermute | solution.py:375
  7.4 1.3 %collective-permute-start.1 = (bf16[8,32,512]{2,1,0:T(8,128)(2,1)S(1)}, bf16[8,32,512]{2,1,0:T(8,128)(2,1)S(1)}, u32[]{:S(2)}, u32[]{:S(2)}) collective-permute-start(bf16[8,32,512]{2,1,0:T(8,128)(2,1)S(1)} %cross.3._.after_ref.refs_0_.refs_3_), channel_id=1, source_target_pairs={{0,2},{1,3},{4,5},{5,4},{8,10},{9,11},{12,13},{13,12},{16,18},{17,... | collective-permute-start | bytes 786440 | tf_op jit(solution)/shard_map/ppermute | solution.py:417
  8.7 0.7 %collective-permute-start.2 = (bf16[8,32,512]{2,1,0:T(8,128)(2,1)S(1)}, bf16[8,32,512]{2,1,0:T(8,128)(2,1)S(1)}, u32[]{:S(2)}, u32[]{:S(2)}) collective-permute-start(bf16[8,32,512]{2,1,0:T(8,128)(2,1)S(1)} %cross.3._.after_ref.refs_0_.refs_3_), channel_id=1, source_target_pairs={{6,7},{14,15},{22,23},{30,31}} | collective-permute-start | bytes 786440 | tf_op jit(solution)/shard_map/ppermute | solution.py:417
  9.4 1.3 %tail.4 = (f32[8,32,512]{2,1,0:T(8,128)S(1)}, bf16[32,4096]{1,0:T(8,128)(2,1)S(1)}, bf16[8,32,512]{2,1,0:T(8,128)(2,1)S(1)}) custom-call(bf16[512,512]{1,0:T(8,128)(2,1)S(1)} %bitcast.5, bf16[512,512]{1,0:T(8,128)(2,1)S(1)} %get-tuple-element.20.table_ref.after_ref, f32[64,1024]{1,0:T(8,128)S(1)} %get-tuple-element.21.keep_ref, ...), custom_call_target="tpu_custom_call" | custom-call | flops 268435456 | bytes 4194304 | tf_op jit(solution)/shard_map/tail/pallas_call | solution.py:382
  10.7 0.8 %cross.4.refs_1_.refs_3_ = bf16[8,32,512]{2,1,0:T(8,128)(2,1)S(1)} custom-call(bf16[8,32,64]{2,1,0:T(8,128)(2,1)S(1)} %get-tuple-element.19.pick_ref, f32[8,32,512]{2,1,0:T(8,128)S(1)} %get-tuple-element.26.white_ref, bf16[32,4096]{1,0:T(8,128)(2,1)S(1)} %get-tuple-element.27.short_ref, bf16[32,4096]{1,0:T(8,128)(2,1)S(1)} %collective-permute-done.edge_ref, ...), custom_call_target="tpu_custom_call" | custom-call | flops 4194304 | bytes 4194304 | tf_op jit(solution)/shard_map/cross/pallas_call | solution.py:394
  11.5 0.4 %collective-permute-done.4.refs_2_.rest_3_ = bf16[8,32,512]{2,1,0:T(8,128)(2,1)S(1)} collective-permute-done((bf16[8,32,512]{2,1,0:T(8,128)(2,1)S(1)}, bf16[8,32,512]{2,1,0:T(8,128)(2,1)S(1)}, u32[]{:S(2)}, u32[]{:S(2)}) %collective-permute-start.4) | collective-permute-done | bytes 262176 | tf_op jit(solution)/shard_map/ppermute | solution.py:417
  11.9 0.1 mix.3
  12.0 3.4 %collective-permute-start.5 = (bf16[8,32,512]{2,1,0:T(8,128)(2,1)S(1)}, bf16[8,32,512]{2,1,0:T(8,128)(2,1)S(1)}, u32[]{:S(2)}, u32[]{:S(2)}) collective-permute-start(bf16[8,32,512]{2,1,0:T(8,128)(2,1)S(1)} %mix.3), channel_id=1, source_target_pairs={{0,1},{2,3},{3,2},{4,6},{5,7},{8,9},{10,11},{11,10},{12,14},{13,15... | collective-permute-start | bytes 786440 | tf_op jit(solution)/shard_map/ppermute | solution.py:417
  15.4 0.6 %collective-permute-done.1.refs_2_.refs_3_ = bf16[8,32,512]{2,1,0:T(8,128)(2,1)S(1)} collective-permute-done((bf16[8,32,512]{2,1,0:T(8,128)(2,1)S(1)}, bf16[8,32,512]{2,1,0:T(8,128)(2,1)S(1)}, u32[]{:S(2)}, u32[]{:S(2)}) %collective-permute-start.1) | collective-permute-done | bytes 262176 | tf_op jit(solution)/shard_map/ppermute | solution.py:417
  16.1 0.1 mix.2.after_ref
  16.2 3.0 %collective-permute-start.3 = (bf16[8,32,512]{2,1,0:T(8,128)(2,1)S(1)}, bf16[8,32,512]{2,1,0:T(8,128)(2,1)S(1)}, u32[]{:S(2)}, u32[]{:S(2)}) collective-permute-start(bf16[8,32,512]{2,1,0:T(8,128)(2,1)S(1)} %mix.2.after_ref), channel_id=1, source_target_pairs={{0,1},{2,3},{3,2},{4,6},{5,7},{8,9},{10,11},{11,10},{12,14},{13,15... | collective-permute-start | bytes 786440 | tf_op jit(solution)/shard_map/ppermute | solution.py:417
  19.2 0.3 %inverse.1.table_ref = bf16[512,512]{1,0:T(8,128)(2,1)S(1)} custom-call(bf16[8,32,512]{2,1,0:T(8,128)(2,1)S(1)} %cross.3._.after_ref.refs_0_.refs_3_), custom_call_target="tpu_custom_call" | custom-call | flops 4194304 | bytes 524288 | tf_op jit(solution)/shard_map/inverse/pallas_call | solution.py:430
  19.6 0.0 collective-permute-done.2.refs_4_
  19.6 0.4 %part.1.rest_5_.part_ref = f32[256,512]{1,0:T(8,128)S(1)} custom-call(bf16[512,512]{1,0:T(8,128)(2,1)S(1)} %inverse.1.table_ref, bf16[8,32,512]{2,1,0:T(8,128)(2,1)S(1)} %cross.3._.after_ref.refs_0_.refs_3_, bf16[8,32,512]{2,1,0:T(8,128)(2,1)S(1)} %cross.4.refs_1_.refs_3_, bf16[8,32,512]{2,1,0:T(8,128)(2,1)S(1)} %cross.5.refs_2_, ...), custom_call_target="tpu_custom_call" | custom-call | flops 268435456 | bytes 1048576 | tf_op jit(solution)/shard_map/part/pallas_call | solution.py:457
  20.1 0.2 collective-permute-done.5.rest_4_
  20.3 1.2 %lags.2.rest_0_ = bf16[8,64,512]{2,1,0:T(8,128)(2,1)} custom-call(bf16[512,512]{1,0:T(8,128)(2,1)S(1)} %inverse.1.table_ref, bf16[8,32,512]{2,1,0:T(8,128)(2,1)S(1)} %get-tuple-element.30.refs_0_.rest_0_, bf16[8,32,512]{2,1,0:T(8,128)(2,1)S(1)} %get-tuple-element.31.refs_1_.rest_1_, bf16[8,32,512]{2,1,0:T(8,128)(2,1)S(1)} %get-tuple-element.32.rest_2_, ...), custom_call_target="tpu_custom_call" | custom-call | flops 268435456 | bytes 1048576 | tf_op jit(solution)/shard_map/lags/pallas_call | solution.py:441
  21.5 3.0 %collective-permute-done.3.more_ref = bf16[8,32,512]{2,1,0:T(8,128)(2,1)S(1)} collective-permute-done((bf16[8,32,512]{2,1,0:T(8,128)(2,1)S(1)}, bf16[8,32,512]{2,1,0:T(8,128)(2,1)S(1)}, u32[]{:S(2)}, u32[]{:S(2)}) %collective-permute-start.3) | collective-permute-done | bytes 262176 | tf_op jit(solution)/shard_map/ppermute | solution.py:417
  24.4 1.0 %lags.3 = bf16[8,64,512]{2,1,0:T(8,128)(2,1)} custom-call(bf16[512,512]{1,0:T(8,128)(2,1)S(1)} %inverse.1.table_ref, f32[256,512]{1,0:T(8,128)S(1)} %part.1.rest_5_.part_ref, bf16[8,32,512]{2,1,0:T(8,128)(2,1)S(1)} %collective-permute-done.3.more_ref, bf16[8,64,512]{2,1,0:T(8,128)(2,1)} %lags.2.rest_0_), custom_call_target="tpu_custom_call", output_to_operand_aliasing={{}: (3, {})} | custom-call | flops 268435456 | bytes 1048576 | tf_op jit(solution)/shard_map/lags/pallas_call | solution.py:441
  (4 shorter events, 0.1 us)
Async XLA Ops:
  0.0 3.6 %copy-start = (bf16[64,8,512]{2,1,0:T(8,128)(2,1)S(1)}, bf16[64,8,512]{2,1,0:T(8,128)(2,1)}, u32[]{:S(2)}) copy-start(bf16[64,8,512]{2,1,0:T(8,128)(2,1)} %param.3) | copy-start | bytes 1572868
  1.6 5.8 %collective-permute-start = (bf16[32,4096]{1,0:T(8,128)(2,1)S(1)}, bf16[32,4096]{1,0:T(8,128)(2,1)S(1)}, u32[]{:S(2)}, u32[]{:S(2)}) collective-permute-start(bf16[32,4096]{1,0:T(8,128)(2,1)S(1)} %get-tuple-element.23.edge_ref), channel_id=1, source_target_pairs={{4,0},{8,4},{12,8},{16,12},{20,16},{24,20},{28,24},{5,1},{9,5},{13... | collective-permute-start | bytes 786440 | tf_op jit(solution)/shard_map/ppermute | solution.py:375
  3.6 8.3 %collective-permute-start.4 = (bf16[8,32,512]{2,1,0:T(8,128)(2,1)S(1)}, bf16[8,32,512]{2,1,0:T(8,128)(2,1)S(1)}, u32[]{:S(2)}, u32[]{:S(2)}) collective-permute-start(bf16[8,32,512]{2,1,0:T(8,128)(2,1)S(1)} %get-tuple-element.30.refs_0_.rest_0_), channel_id=1, source_target_pairs={{0,2},{1,3},{4,5},{5,4},{6,7},{8,10},{9,11},{12,13},{13,12},{14,15... | collective-permute-start | bytes 786440 | tf_op jit(solution)/shard_map/ppermute | solution.py:417
  7.4 8.6 %collective-permute-start.1 = (bf16[8,32,512]{2,1,0:T(8,128)(2,1)S(1)}, bf16[8,32,512]{2,1,0:T(8,128)(2,1)S(1)}, u32[]{:S(2)}, u32[]{:S(2)}) collective-permute-start(bf16[8,32,512]{2,1,0:T(8,128)(2,1)S(1)} %cross.3._.after_ref.refs_0_.refs_3_), channel_id=1, source_target_pairs={{0,2},{1,3},{4,5},{5,4},{8,10},{9,11},{12,13},{13,12},{16,18},{17,... | collective-permute-start | bytes 786440 | tf_op jit(solution)/shard_map/ppermute | solution.py:417
  8.7 10.9 %collective-permute-start.2 = (bf16[8,32,512]{2,1,0:T(8,128)(2,1)S(1)}, bf16[8,32,512]{2,1,0:T(8,128)(2,1)S(1)}, u32[]{:S(2)}, u32[]{:S(2)}) collective-permute-start(bf16[8,32,512]{2,1,0:T(8,128)(2,1)S(1)} %cross.3._.after_ref.refs_0_.refs_3_), channel_id=1, source_target_pairs={{6,7},{14,15},{22,23},{30,31}} | collective-permute-start | bytes 786440 | tf_op jit(solution)/shard_map/ppermute | solution.py:417
  12.0 8.3 %collective-permute-start.5 = (bf16[8,32,512]{2,1,0:T(8,128)(2,1)S(1)}, bf16[8,32,512]{2,1,0:T(8,128)(2,1)S(1)}, u32[]{:S(2)}, u32[]{:S(2)}) collective-permute-start(bf16[8,32,512]{2,1,0:T(8,128)(2,1)S(1)} %mix.3), channel_id=1, source_target_pairs={{0,1},{2,3},{3,2},{4,6},{5,7},{8,9},{10,11},{11,10},{12,14},{13,15... | collective-permute-start | bytes 786440 | tf_op jit(solution)/shard_map/ppermute | solution.py:417
  16.2 8.3 %collective-permute-start.3 = (bf16[8,32,512]{2,1,0:T(8,128)(2,1)S(1)}, bf16[8,32,512]{2,1,0:T(8,128)(2,1)S(1)}, u32[]{:S(2)}, u32[]{:S(2)}) collective-permute-start(bf16[8,32,512]{2,1,0:T(8,128)(2,1)S(1)} %mix.2.after_ref), channel_id=1, source_target_pairs={{0,1},{2,3},{3,2},{4,6},{5,7},{8,9},{10,11},{11,10},{12,14},{13,15... | collective-permute-start | bytes 786440 | tf_op jit(solution)/shard_map/ppermute | solution.py:417

commit v5 on v2

--- a/solution.py
+++ b/solution.py
@@ -68,8 +68,9 @@
         table_ref[bins + first : bins + first + step, :] = (-sine).astype(jnp.bfloat16)
 
 
-def whiten_block(x, table_ref, keep, raw_ref, white_ref, short_ref):
-    wins, span, length = white_ref.shape
+def whiten_block(x, table_ref, keep, raw_ref, white_ref, short_ref, send_ref=None):
+    span = short_ref.shape[0]
+    wins, length = x.shape[0] // span, x.shape[1]
     bins = length // 2
     tiles = bins // LANES
 
@@ -90,16 +91,25 @@
     for w in range(wins):
         decay = float(np.float32(DECAY) ** np.float32(wins - 1 - w))
         level = jnp.sum(total[w], axis=-1, keepdims=True) * (0.01 / bins) + 1e-06
-        alive = keep[:, w * LANES : (w + 1) * LANES]
         for t in range(tiles):
             part = [strided(2 * t, w), strided(2 * t + 1, w)]
             power = part[0] * part[0] + part[1] * part[1]
-            scale = alive * lax.rsqrt(power + level)
+            scale = lax.rsqrt(power + level)
+            if keep is not None:
+                scale = scale * keep[:, w * LANES : (w + 1) * LANES]
             for i, s in enumerate((t, tiles + t)):
                 value = part[i] * scale
                 here = pl.ds(w * length + s * LANES, LANES)
-                white_ref[w, :, s * LANES : (s + 1) * LANES] = value * decay
                 short_ref[:, here] = value.astype(jnp.bfloat16)
+                if white_ref is not None:
+                    white_ref[w, :, s * LANES : (s + 1) * LANES] = value * decay
+                if send_ref is not None:
+                    rows = slice(w * span, (w + 1) * span)
+                    send_ref[rows, s * LANES : (s + 1) * LANES] = value.astype(jnp.bfloat16)
+
+
+def on_odd():
+    return lax.rem(lax.axis_index("chan"), 2) == 1
 
 
 def head_kernel(
@@ -108,6 +118,7 @@
     offsets_hbm,
     white_ref,
     short_ref,
+    send_ref,
     table_ref,
     pick_ref,
     keep_ref,
@@ -144,7 +155,40 @@
         preferred_element_type=jnp.float32,
     )
     copies[2].wait()
-    whiten_block(x_ref[...], table_ref, keep_ref[:span], raw_ref, white_ref, short_ref)
+
+    @pl.when(jnp.logical_not(on_odd()))
+    def _():
+        keep = keep_ref[:span]
+        whiten_block(x_ref[...], table_ref, keep, raw_ref, white_ref, short_ref, send_ref)
+
+    @pl.when(on_odd())
+    def _():
+        count = span * wins
+        row = lax.broadcasted_iota(jnp.int32, (count, valid_ref.shape[1]), 0) // wins
+        chan = lax.broadcasted_iota(jnp.int32, (count, valid_ref.shape[1]), 1)
+        per_window = lax.dot_general(
+            (row == chan).astype(jnp.float32).astype(jnp.bfloat16),
+            valid_ref[...].astype(jnp.float32).astype(jnp.bfloat16),
+            (((1,), (1,)), ((), ())),
+            preferred_element_type=jnp.float32,
+        )
+        window = lax.rem(lax.broadcasted_iota(jnp.int32, (count, wins), 0), wins)
+        mine = window == lax.broadcasted_iota(jnp.int32, (count, wins), 1)
+        chosen_one = jnp.where(mine, per_window, 0.0).astype(jnp.bfloat16)
+        ones = jnp.ones((wins, LANES), jnp.bfloat16)
+        mask = jnp.dot(chosen_one, ones, preferred_element_type=jnp.float32)
+        for t in range(length // LANES):
+            lanes = slice(t * LANES, (t + 1) * LANES)
+            send_ref[:, lanes] = (x_ref[:, lanes].astype(jnp.float32) * mask).astype(jnp.bfloat16)
+
+
+def odd_head_kernel(x_ref, table_ref, keep_ref, _, __, white_ref, short_ref, raw_ref):
+    wins, span, _ = white_ref.shape
+
+    @pl.when(on_odd())
+    def _():
+        x = x_ref[: span * wins, :]
+        whiten_block(x, table_ref, keep_ref[:span], raw_ref, white_ref, short_ref)
 
 
 def stack_pairs(pick_ref, white_ref, near_ref, parts_refs, out_ref):
@@ -220,14 +264,35 @@
 
 
 def cross_kernel(
-    limits, now, pick_ref, white_ref, short_ref, edge_ref, after_ref, out_ref, near_ref, *parts_refs
+    limits,
+    now,
+    pick_ref,
+    white_ref,
+    short_ref,
+    edge_ref,
+    table_ref,
+    after_ref,
+    out_ref,
+    raw_ref,
+    near_ref,
+    *parts_refs,
 ):
     span = short_ref.shape[0]
+    wins, _, length = white_ref.shape
+    far_ref = near_ref.at[pl.ds(span, span)]
+
+    @pl.when((role(limits) == now) & jnp.logical_not(on_odd()))
+    def _():
+        whiten_block(edge_ref[...], table_ref, None, raw_ref, None, far_ref)
+
+    @pl.when((role(limits) == now) & on_odd())
+    def _():
+        for w in range(wins):
+            far_ref[:, w * length : (w + 1) * length] = edge_ref[w * span : (w + 1) * span, :]
 
     @pl.when(role(limits) == now)
     def _():
         near_ref[:span] = short_ref[...]
-        near_ref[span:] = edge_ref[...]
         stack_pairs(pick_ref, white_ref, near_ref, parts_refs, out_ref)
 
 
@@ -335,17 +400,18 @@
     near_scratch = pltpu.VMEM((2 * span, wins * length), jnp.bfloat16)
     parts_scratch = [pltpu.VMEM((wins, pairs // 4 * span, length), jnp.float32)] * 4
 
-    white_a, short_a, table, pick, keep = pl.pallas_call(
+    white_a, short_a, edge, table, pick, keep = pl.pallas_call(
         head_kernel,
         out_shape=(
             white_type,
             short_type,
+            jax.ShapeDtypeStruct((wins * span, length), jnp.bfloat16),
             jax.ShapeDtypeStruct((length, length), jnp.bfloat16),
             jax.ShapeDtypeStruct((pairs, span, 2 * span), jnp.bfloat16),
             jax.ShapeDtypeStruct((chans, wins * LANES), jnp.float32),
         ),
         in_specs=[whole(pltpu.HBM)] * 3,
-        out_specs=(whole(),) * 5,
+        out_specs=(whole(),) * 6,
         scratch_shapes=[
             pltpu.VMEM((span * wins, length), jnp.bfloat16),
             pltpu.VMEM((wins, chans), jnp.int32),
@@ -359,7 +425,19 @@
     )(in_hbm(flat), in_hbm(valid.T), in_hbm(offsets))
 
     ring = lax.axis_size("chan")
-    edge = lax.ppermute(short_a, "chan", [(i, i - 1) for i in range(1, ring)])
+    edge = lax.ppermute(edge, "chan", [(i, i - 1) for i in range(1, ring)])
+
+    white_a, short_a = pl.pallas_call(
+        odd_head_kernel,
+        out_shape=(white_type, short_type),
+        in_specs=[whole()] * 5,
+        out_specs=(whole(),) * 2,
+        scratch_shapes=[raw_scratch],
+        input_output_aliases={3: 0, 4: 1},
+        compiler_params=params,
+        cost_estimate=cost(span * wins * length * length * 2, 2 * 1024 * 1024),
+        name="odd_head",
+    )(flat, table, keep, white_a, short_a)
 
     columns = min(d for d in range(1, groups + 1) if groups % d == 0 and d * d >= groups)
     square = columns == 2 and groups == columns * columns
@@ -381,17 +459,17 @@
         return pl.pallas_call(
             functools.partial(cross_kernel, limits, now),
             out_shape=local_type,
-            in_specs=[whole()] * 4 + [whole(pl.ANY)],
+            in_specs=[whole()] * 5 + [whole(pl.ANY)],
             out_specs=whole(),
-            scratch_shapes=[near_scratch] + parts_scratch,
+            scratch_shapes=[raw_scratch, near_scratch] + parts_scratch,
             compiler_params=params,
             cost_estimate=cost(pairs * span * wins * bins * 8, 4 * 1024 * 1024),
             name="cross",
-        )(pick, white, short, edge, after)
+        )(pick, white, short, edge, table, after)
 
     white_b, short_b, local_a = tail(0, table)
-    local_b = cross(0, white_b, short_b, table)
-    white_late, short_late, late_a = tail(1, local_b)
+    white_late, short_late, late_a = tail(1, local_a)
+    local_b = cross(0, white_b, short_b, late_a)
     late_b = cross(1, white_late, short_late, local_b)
 
     power = [float(np.float32(factor) ** np.float32(d)) for d in range(groups)]

time: 25.6 us -> 25.9 us (1.012)
  the two profiles are of different devices: /device:TPU:28 before, /device:TPU:7 now
where the time goes in v5:
time: 25.9 us; the launch traced here: 25.6 us
  waiting for transfers between devices  9.59 us (37%)
  starting transfers between devices  8.64 us (33%)
  Pallas kernels  7.25 us (28%)
    ppermute x5, waiting for transfers between devices, sent(): return lax.ppermute(value, ('chan', 'tm'), moves)  5.95 us
    ppermute x5, starting transfers between devices, sent(): return lax.ppermute(value, ('chan', 'tm'), moves)  5.83 us
    ppermute x1, waiting for transfers between devices, per_device(): edge = lax.ppermute(edge, 'chan', [(i, i - 1) for i in range(1, ring)])  3.64 us
    ppermute x1, starting transfers between devices, per_device(): edge = lax.ppermute(edge, 'chan', [(i, i - 1) for i in range(1, ring)])  2.81 us
    pallas_call x2, Pallas kernels, written(): pl.pallas_call(kernel, out_shape=jax.ShapeDtypeStruct((pairs, chans, leng...  2.18 us
    pallas_call x1, Pallas kernels, per_device(): pl.pallas_call(head_kernel, out_shape=(white_type, short_type, jax.ShapeD...  1.33 us
    pallas_call x3, Pallas kernels, tail(): pl.pallas_call(functools.partial(tail_kernel, limits, now), out_shape=(wh...  1.33 us
    pallas_call x3, Pallas kernels, cross(): pl.pallas_call(functools.partial(cross_kernel, limits, now), out_shape=lo...  0.93 us
  transfers between devices with their start and end apart: 6, of which 5 were waited for; matrix products, arithmetic and copies ran while one was open for 0% of the time, Pallas kernels for 19%

profile of v5, /device:TPU:7, one launch (start us, length us, event | category | flops | bytes accessed | tf_op | source)
XLA Modules:
  0.0 25.6 jit_solution(10317397351011972308)
XLA Ops:
  0.0 0.0 copy-start
  0.0 1.3 %head.1 = (f32[8,32,512]{2,1,0:T(8,128)S(1)}, bf16[32,4096]{1,0:T(8,128)(2,1)S(1)}, bf16[256,512]{1,0:T(8,128)(2,1)S(1)}, bf16[512,512]{1,0:T(8,128)(2,1)S(1)}, ...) custom-call(bf16[512,512]{1,0:T(8,128)(2,1)} %bitcast.3, s32[8,64]{1,0:T(8,128)} %bitcast.8, s32[8]{0:T(128)} %offsets_hbm.1), custom_call_target="tpu_custom_call" | custom-call | flops 134217728 | bytes 2097152 | tf_op jit(solution)/shard_map/head/pallas_call | solution.py:403
  1.3 2.8 %collective-permute-start = (bf16[256,512]{1,0:T(8,128)(2,1)S(1)}, bf16[256,512]{1,0:T(8,128)(2,1)S(1)}, u32[]{:S(2)}, u32[]{:S(2)}) collective-permute-start(bf16[256,512]{1,0:T(8,128)(2,1)S(1)} %get-tuple-element.31), channel_id=1, source_target_pairs={{4,0},{8,4},{12,8},{16,12},{20,16},{24,20},{28,24},{5,1},{9,5},{13... | collective-permute-start | bytes 786440 | tf_op jit(solution)/shard_map/ppermute | solution.py:428
  4.2 0.0 copy-done
  4.2 0.5 %odd_head.1 = (f32[8,32,512]{2,1,0:T(8,128)S(1)}, bf16[32,4096]{1,0:T(8,128)(2,1)S(1)}) custom-call(bf16[512,512]{1,0:T(8,128)(2,1)S(1)} %bitcast.4, bf16[512,512]{1,0:T(8,128)(2,1)S(1)} %get-tuple-element.23.table_ref.after_ref, f32[64,1024]{1,0:T(8,128)S(1)} %get-tuple-element.24.keep_ref, ...), custom_call_target="tpu_custom_call", output_to_operand_aliasing={{0}: (3, {}), {1}: (4, {})} | custom-call | flops 134217728 | bytes 2097152 | tf_op jit(solution)/shard_map/odd_head/pallas_call | solution.py:430
  4.7 1.3 %collective-permute-start.4 = (bf16[8,32,512]{2,1,0:T(8,128)(2,1)S(1)}, bf16[8,32,512]{2,1,0:T(8,128)(2,1)S(1)}, u32[]{:S(2)}, u32[]{:S(2)}) collective-permute-start(bf16[8,32,512]{2,1,0:T(8,128)(2,1)S(1)} %get-tuple-element.32.after_ref.refs_0_.rest_0_), channel_id=1, source_target_pairs={{0,2},{1,3},{4,5},{5,4},{6,7},{8,10},{9,11},{12,13},{13,12},{14,15... | collective-permute-start | bytes 786440 | tf_op jit(solution)/shard_map/ppermute | solution.py:482
  6.0 3.6 %collective-permute-done.edge_ref = bf16[256,512]{1,0:T(8,128)(2,1)S(1)} collective-permute-done((bf16[256,512]{1,0:T(8,128)(2,1)S(1)}, bf16[256,512]{1,0:T(8,128)(2,1)S(1)}, u32[]{:S(2)}, u32[]{:S(2)}) %collective-permute-start) | collective-permute-done | bytes 262176 | tf_op jit(solution)/shard_map/ppermute | solution.py:428
  9.7 0.7 %collective-permute-start.1 = (bf16[8,32,512]{2,1,0:T(8,128)(2,1)S(1)}, bf16[8,32,512]{2,1,0:T(8,128)(2,1)S(1)}, u32[]{:S(2)}, u32[]{:S(2)}) collective-permute-start(bf16[8,32,512]{2,1,0:T(8,128)(2,1)S(1)} %cross.3._.after_ref.refs_0_.refs_3_), channel_id=1, source_target_pairs={{0,2},{1,3},{4,5},{5,4},{8,10},{9,11},{12,13},{13,12},{16,18},{17,... | collective-permute-start | bytes 786440 | tf_op jit(solution)/shard_map/ppermute | solution.py:482
  10.4 1.3 %collective-permute-start.2 = (bf16[8,32,512]{2,1,0:T(8,128)(2,1)S(1)}, bf16[8,32,512]{2,1,0:T(8,128)(2,1)S(1)}, u32[]{:S(2)}, u32[]{:S(2)}) collective-permute-start(bf16[8,32,512]{2,1,0:T(8,128)(2,1)S(1)} %cross.3._.after_ref.refs_0_.refs_3_), channel_id=1, source_target_pairs={{6,7},{14,15},{22,23},{30,31}} | collective-permute-start | bytes 786440 | tf_op jit(solution)/shard_map/ppermute | solution.py:482
  11.7 0.4 %collective-permute-done.4.refs_2_.rest_3_ = bf16[8,32,512]{2,1,0:T(8,128)(2,1)S(1)} collective-permute-done((bf16[8,32,512]{2,1,0:T(8,128)(2,1)S(1)}, bf16[8,32,512]{2,1,0:T(8,128)(2,1)S(1)}, u32[]{:S(2)}, u32[]{:S(2)}) %collective-permute-start.4) | collective-permute-done | bytes 262176 | tf_op jit(solution)/shard_map/ppermute | solution.py:482
  12.1 0.1 mix.3
  12.2 1.3 %collective-permute-start.5 = (bf16[8,32,512]{2,1,0:T(8,128)(2,1)S(1)}, bf16[8,32,512]{2,1,0:T(8,128)(2,1)S(1)}, u32[]{:S(2)}, u32[]{:S(2)}) collective-permute-start(bf16[8,32,512]{2,1,0:T(8,128)(2,1)S(1)} %mix.3), channel_id=1, source_target_pairs={{0,1},{2,3},{3,2},{4,6},{5,7},{8,9},{10,11},{11,10},{12,14},{13,15... | collective-permute-start | bytes 786440 | tf_op jit(solution)/shard_map/ppermute | solution.py:482
  13.5 0.0 collective-permute-done.1.refs_2_.refs_3_
  13.6 0.1 mix.2.after_ref
  13.7 1.3 %collective-permute-start.3 = (bf16[8,32,512]{2,1,0:T(8,128)(2,1)S(1)}, bf16[8,32,512]{2,1,0:T(8,128)(2,1)S(1)}, u32[]{:S(2)}, u32[]{:S(2)}) collective-permute-start(bf16[8,32,512]{2,1,0:T(8,128)(2,1)S(1)} %mix.2.after_ref), channel_id=1, source_target_pairs={{0,1},{2,3},{3,2},{4,6},{5,7},{8,9},{10,11},{11,10},{12,14},{13,15... | collective-permute-start | bytes 786440 | tf_op jit(solution)/shard_map/ppermute | solution.py:482
  15.0 0.3 %inverse.1.table_ref = bf16[512,512]{1,0:T(8,128)(2,1)S(1)} custom-call(bf16[8,32,512]{2,1,0:T(8,128)(2,1)S(1)} %cross.3._.after_ref.refs_0_.refs_3_), custom_call_target="tpu_custom_call" | custom-call | flops 4194304 | bytes 524288 | tf_op jit(solution)/shard_map/inverse/pallas_call | solution.py:495
  15.3 1.3 %tail.5 = (f32[8,32,512]{2,1,0:T(8,128)S(1)}, bf16[32,4096]{1,0:T(8,128)(2,1)S(1)}, bf16[8,32,512]{2,1,0:T(8,128)(2,1)S(1)}) custom-call(bf16[512,512]{1,0:T(8,128)(2,1)S(1)} %bitcast.7, bf16[512,512]{1,0:T(8,128)(2,1)S(1)} %get-tuple-element.23.table_ref.after_ref, f32[64,1024]{1,0:T(8,128)S(1)} %get-tuple-element.24.keep_ref, ...), custom_call_target="tpu_custom_call" | custom-call | flops 268435456 | bytes 4194304 | tf_op jit(solution)/shard_map/tail/pallas_call | solution.py:447
  16.6 0.9 %cross.5.refs_2_ = bf16[8,32,512]{2,1,0:T(8,128)(2,1)S(1)} custom-call(bf16[8,32,64]{2,1,0:T(8,128)(2,1)S(1)} %get-tuple-element.22.pick_ref, f32[8,32,512]{2,1,0:T(8,128)S(1)} %get-tuple-element.36.white_ref, bf16[32,4096]{1,0:T(8,128)(2,1)S(1)} %get-tuple-element.37.short_ref, bf16[256,512]{1,0:T(8,128)(2,1)S(1)} %collective-permute-done.edge_ref, ...), custom_call_target="tpu_custom_call" | custom-call | flops 4194304 | bytes 4194304 | tf_op jit(solution)/shard_map/cross/pallas_call | solution.py:459
  17.5 0.9 %collective-permute-done.2.refs_4_ = bf16[8,32,512]{2,1,0:T(8,128)(2,1)S(1)} collective-permute-done((bf16[8,32,512]{2,1,0:T(8,128)(2,1)S(1)}, bf16[8,32,512]{2,1,0:T(8,128)(2,1)S(1)}, u32[]{:S(2)}, u32[]{:S(2)}) %collective-permute-start.2) | collective-permute-done | bytes 262176 | tf_op jit(solution)/shard_map/ppermute | solution.py:482
  18.4 0.4 %part.1.rest_5_.part_ref = f32[256,512]{1,0:T(8,128)S(1)} custom-call(bf16[512,512]{1,0:T(8,128)(2,1)S(1)} %inverse.1.table_ref, bf16[8,32,512]{2,1,0:T(8,128)(2,1)S(1)} %cross.3._.after_ref.refs_0_.refs_3_, bf16[8,32,512]{2,1,0:T(8,128)(2,1)S(1)} %cross.4.refs_1_.refs_3_, bf16[8,32,512]{2,1,0:T(8,128)(2,1)S(1)} %cross.5.refs_2_, ...), custom_call_target="tpu_custom_call" | custom-call | flops 268435456 | bytes 1048576 | tf_op jit(solution)/shard_map/part/pallas_call | solution.py:522
  18.8 0.8 %collective-permute-done.5.rest_4_ = bf16[8,32,512]{2,1,0:T(8,128)(2,1)S(1)} collective-permute-done((bf16[8,32,512]{2,1,0:T(8,128)(2,1)S(1)}, bf16[8,32,512]{2,1,0:T(8,128)(2,1)S(1)}, u32[]{:S(2)}, u32[]{:S(2)}) %collective-permute-start.5) | collective-permute-done | bytes 262176 | tf_op jit(solution)/shard_map/ppermute | solution.py:482
  19.7 1.2 %lags.2.rest_0_ = bf16[8,64,512]{2,1,0:T(8,128)(2,1)} custom-call(bf16[512,512]{1,0:T(8,128)(2,1)S(1)} %inverse.1.table_ref, bf16[8,32,512]{2,1,0:T(8,128)(2,1)S(1)} %get-tuple-element.32.after_ref.refs_0_.rest_0_, bf16[8,32,512]{2,1,0:T(8,128)(2,1)S(1)} %get-tuple-element.33.after_ref.refs_1_.rest_1_, bf16[8,32,512]{2,1,0:T(8,128)(2,1)S(1)} %get-tuple-element.38.rest_2_, ...), custom_call_target="tpu_custom_call" | custom-call | flops 268435456 | bytes 1048576 | tf_op jit(solution)/shard_map/lags/pallas_call | solution.py:506
  20.8 3.8 %collective-permute-done.3.more_ref = bf16[8,32,512]{2,1,0:T(8,128)(2,1)S(1)} collective-permute-done((bf16[8,32,512]{2,1,0:T(8,128)(2,1)S(1)}, bf16[8,32,512]{2,1,0:T(8,128)(2,1)S(1)}, u32[]{:S(2)}, u32[]{:S(2)}) %collective-permute-start.3) | collective-permute-done | bytes 262176 | tf_op jit(solution)/shard_map/ppermute | solution.py:482
  24.6 1.0 %lags.3 = bf16[8,64,512]{2,1,0:T(8,128)(2,1)} custom-call(bf16[512,512]{1,0:T(8,128)(2,1)S(1)} %inverse.1.table_ref, f32[256,512]{1,0:T(8,128)S(1)} %part.1.rest_5_.part_ref, bf16[8,32,512]{2,1,0:T(8,128)(2,1)S(1)} %collective-permute-done.3.more_ref, bf16[8,64,512]{2,1,0:T(8,128)(2,1)} %lags.2.rest_0_), custom_call_target="tpu_custom_call", output_to_operand_aliasing={{}: (3, {})} | custom-call | flops 268435456 | bytes 1048576 | tf_op jit(solution)/shard_map/lags/pallas_call | solution.py:506
  (4 shorter events, 0.1 us)
Async XLA Ops:
  0.0 4.2 %copy-start = (bf16[64,8,512]{2,1,0:T(8,128)(2,1)S(1)}, bf16[64,8,512]{2,1,0:T(8,128)(2,1)}, u32[]{:S(2)}) copy-start(bf16[64,8,512]{2,1,0:T(8,128)(2,1)} %param.3) | copy-start | bytes 1572868
  1.3 8.3 %collective-permute-start = (bf16[256,512]{1,0:T(8,128)(2,1)S(1)}, bf16[256,512]{1,0:T(8,128)(2,1)S(1)}, u32[]{:S(2)}, u32[]{:S(2)}) collective-permute-start(bf16[256,512]{1,0:T(8,128)(2,1)S(1)} %get-tuple-element.31), channel_id=1, source_target_pairs={{4,0},{8,4},{12,8},{16,12},{20,16},{24,20},{28,24},{5,1},{9,5},{13... | collective-permute-start | bytes 786440 | tf_op jit(solution)/shard_map/ppermute | solution.py:428
  4.7 7.4 %collective-permute-start.4 = (bf16[8,32,512]{2,1,0:T(8,128)(2,1)S(1)}, bf16[8,32,512]{2,1,0:T(8,128)(2,1)S(1)}, u32[]{:S(2)}, u32[]{:S(2)}) collective-permute-start(bf16[8,32,512]{2,1,0:T(8,128)(2,1)S(1)} %get-tuple-element.32.after_ref.refs_0_.rest_0_), channel_id=1, source_target_pairs={{0,2},{1,3},{4,5},{5,4},{6,7},{8,10},{9,11},{12,13},{13,12},{14,15... | collective-permute-start | bytes 786440 | tf_op jit(solution)/shard_map/ppermute | solution.py:482
  9.7 3.9 %collective-permute-start.1 = (bf16[8,32,512]{2,1,0:T(8,128)(2,1)S(1)}, bf16[8,32,512]{2,1,0:T(8,128)(2,1)S(1)}, u32[]{:S(2)}, u32[]{:S(2)}) collective-permute-start(bf16[8,32,512]{2,1,0:T(8,128)(2,1)S(1)} %cross.3._.after_ref.refs_0_.refs_3_), channel_id=1, source_target_pairs={{0,2},{1,3},{4,5},{5,4},{8,10},{9,11},{12,13},{13,12},{16,18},{17,... | collective-permute-start | bytes 786440 | tf_op jit(solution)/shard_map/ppermute | solution.py:482
  10.4 8.0 %collective-permute-start.2 = (bf16[8,32,512]{2,1,0:T(8,128)(2,1)S(1)}, bf16[8,32,512]{2,1,0:T(8,128)(2,1)S(1)}, u32[]{:S(2)}, u32[]{:S(2)}) collective-permute-start(bf16[8,32,512]{2,1,0:T(8,128)(2,1)S(1)} %cross.3._.after_ref.refs_0_.refs_3_), channel_id=1, source_target_pairs={{6,7},{14,15},{22,23},{30,31}} | collective-permute-start | bytes 786440 | tf_op jit(solution)/shard_map/ppermute | solution.py:482
  12.2 7.4 %collective-permute-start.5 = (bf16[8,32,512]{2,1,0:T(8,128)(2,1)S(1)}, bf16[8,32,512]{2,1,0:T(8,128)(2,1)S(1)}, u32[]{:S(2)}, u32[]{:S(2)}) collective-permute-start(bf16[8,32,512]{2,1,0:T(8,128)(2,1)S(1)} %mix.3), channel_id=1, source_target_pairs={{0,1},{2,3},{3,2},{4,6},{5,7},{8,9},{10,11},{11,10},{12,14},{13,15... | collective-permute-start | bytes 786440 | tf_op jit(solution)/shard_map/ppermute | solution.py:482
  13.7 10.9 %collective-permute-start.3 = (bf16[8,32,512]{2,1,0:T(8,128)(2,1)S(1)}, bf16[8,32,512]{2,1,0:T(8,128)(2,1)S(1)}, u32[]{:S(2)}, u32[]{:S(2)}) collective-permute-start(bf16[8,32,512]{2,1,0:T(8,128)(2,1)S(1)} %mix.2.after_ref), channel_id=1, source_target_pairs={{0,1},{2,3},{3,2},{4,6},{5,7},{8,9},{10,11},{11,10},{12,14},{13,15... | collective-permute-start | bytes 786440 | tf_op jit(solution)/shard_map/ppermute | solution.py:482

commit v6 on v4

--- a/solution.py
+++ b/solution.py
@@ -12,7 +12,6 @@
 OFFSET_SPAN = 32
 LANES = 128
 DECAY = 0.99
-X_PIECES = 4
 VMEM = 24 * 1024 * 1024
 
 
@@ -120,19 +119,16 @@
 ):
     wins, span, length = white_ref.shape
     pairs = offsets_ref.shape[0]
-    valid_copy = pltpu.make_async_copy(valid_hbm, valid_ref, sems.at[0])
-    offsets_copy = pltpu.make_async_copy(offsets_hbm, offsets_ref, sems.at[1])
-    size = span * wins // X_PIECES
-    pieces = [pl.ds(i * size, size) for i in range(X_PIECES)]
-    x_copies = [
-        pltpu.make_async_copy(x_hbm.at[piece], x_ref.at[piece], sems.at[2 + i])
-        for i, piece in enumerate(pieces)
+    copies = [
+        pltpu.make_async_copy(valid_hbm, valid_ref, sems.at[0]),
+        pltpu.make_async_copy(offsets_hbm, offsets_ref, sems.at[1]),
+        pltpu.make_async_copy(x_hbm.at[pl.ds(0, span * wins)], x_ref, sems.at[2]),
     ]
-    for copy in x_copies + [valid_copy, offsets_copy]:
+    for copy in copies:
         copy.start()
     fill_table(table_ref, 16)
-    valid_copy.wait()
-    offsets_copy.wait()
+    copies[0].wait()
+    copies[1].wait()
     ahead = lax.broadcasted_iota(jnp.int32, (span, 2 * span), 1) - lax.broadcasted_iota(
         jnp.int32, (span, 2 * span), 0
     )
@@ -147,8 +143,7 @@
         (((0,), (0,)), ((), ())),
         preferred_element_type=jnp.float32,
     )
-    for copy in x_copies:
-        copy.wait()
+    copies[2].wait()
     whiten_block(x_ref[...], table_ref, keep_ref[:span], raw_ref, white_ref, short_ref)
 
 
@@ -364,7 +359,7 @@
             pltpu.VMEM((wins, chans), jnp.int32),
             pltpu.SMEM((pairs,), jnp.int32),
             raw_scratch,
-            pltpu.SemaphoreType.DMA((2 + X_PIECES,)),
+            pltpu.SemaphoreType.DMA((3,)),
         ],
         compiler_params=params,
         cost_estimate=cost(span * wins * length * length * 2, 2 * 1024 * 1024),

time: 25.7 us -> 25.6 us (level)
  no operation moved by 1% of the time
where the time goes in v6:
time: 25.6 us; the launch traced here: 25.3 us
  starting transfers between devices  11.6 us (45%)
  Pallas kernels  6.8 us (27%)
  waiting for transfers between devices  6.78 us (26%)
    ppermute x5, starting transfers between devices, sent(): return lax.ppermute(value, ('chan', 'tm'), moves)  9.69 us
    ppermute x5, waiting for transfers between devices, sent(): return lax.ppermute(value, ('chan', 'tm'), moves)  4.25 us
    ppermute x1, waiting for transfers between devices, per_device(): edge = lax.ppermute(short_a, 'chan', [(i, i - 1) for i in range(1, ring)])  2.53 us
    pallas_call x2, Pallas kernels, written(): pl.pallas_call(kernel, out_shape=jax.ShapeDtypeStruct((pairs, chans, leng...  2.16 us
    ppermute x1, starting transfers between devices, per_device(): edge = lax.ppermute(short_a, 'chan', [(i, i - 1) for i in range(1, ring)])  1.92 us
    pallas_call x1, Pallas kernels, per_device(): pl.pallas_call(head_kernel, out_shape=(white_type, short_type, jax.ShapeD...  1.54 us
    pallas_call x3, Pallas kernels, tail(): pl.pallas_call(functools.partial(tail_kernel, limits, now), out_shape=(wh...  1.34 us
    pallas_call x3, Pallas kernels, cross(): pl.pallas_call(functools.partial(cross_kernel, limits, now), out_shape=lo...  0.79 us
  transfers between devices with their start and end apart: 6, of which 5 were waited for; matrix products, arithmetic and copies ran while one was open for 0% of the time, Pallas kernels for 17%

profile of v6, /device:TPU:28, one launch (start us, length us, event | category | flops | bytes accessed | tf_op | source)
XLA Modules:
  0.0 25.3 jit_solution(9928506187185223390)
XLA Ops:
  0.0 0.0 copy-start
  0.0 1.5 %head.1 = (f32[8,32,512]{2,1,0:T(8,128)S(1)}, bf16[32,4096]{1,0:T(8,128)(2,1)S(1)}, bf16[512,512]{1,0:T(8,128)(2,1)S(1)}, bf16[8,32,64]{2,1,0:T(8,128)(2,1)S(1)}, f32[64,1024]{1,0:T(8,128)S(1)}) custom-call(bf16[512,512]{1,0:T(8,128)(2,1)} %bitcast.3, s32[8,64]{1,0:T(8,128)} %bitcast.7, s32[8]{0:T(128)} %offsets_hbm.1), custom_call_target="tpu_custom_call" | custom-call | flops 134217728 | bytes 2097152 | tf_op jit(solution)/shard_map/head/pallas_call | solution.py:346
  1.5 1.9 %collective-permute-start = (bf16[32,4096]{1,0:T(8,128)(2,1)S(1)}, bf16[32,4096]{1,0:T(8,128)(2,1)S(1)}, u32[]{:S(2)}, u32[]{:S(2)}) collective-permute-start(bf16[32,4096]{1,0:T(8,128)(2,1)S(1)} %get-tuple-element.23.edge_ref), channel_id=1, source_target_pairs={{4,0},{8,4},{12,8},{16,12},{20,16},{24,20},{28,24},{5,1},{9,5},{13... | collective-permute-start | bytes 786440 | tf_op jit(solution)/shard_map/ppermute | solution.py:370
  3.5 0.0 copy-done
  3.5 1.3 %collective-permute-start.4 = (bf16[8,32,512]{2,1,0:T(8,128)(2,1)S(1)}, bf16[8,32,512]{2,1,0:T(8,128)(2,1)S(1)}, u32[]{:S(2)}, u32[]{:S(2)}) collective-permute-start(bf16[8,32,512]{2,1,0:T(8,128)(2,1)S(1)} %get-tuple-element.30.refs_0_.rest_0_), channel_id=1, source_target_pairs={{0,2},{1,3},{4,5},{5,4},{6,7},{8,10},{9,11},{12,13},{13,12},{14,15... | collective-permute-start | bytes 786440 | tf_op jit(solution)/shard_map/ppermute | solution.py:412
  4.8 2.5 %collective-permute-done.edge_ref = bf16[32,4096]{1,0:T(8,128)(2,1)S(1)} collective-permute-done((bf16[32,4096]{1,0:T(8,128)(2,1)S(1)}, bf16[32,4096]{1,0:T(8,128)(2,1)S(1)}, u32[]{:S(2)}, u32[]{:S(2)}) %collective-permute-start) | collective-permute-done | bytes 262176 | tf_op jit(solution)/shard_map/ppermute | solution.py:370
  7.3 1.3 %collective-permute-start.1 = (bf16[8,32,512]{2,1,0:T(8,128)(2,1)S(1)}, bf16[8,32,512]{2,1,0:T(8,128)(2,1)S(1)}, u32[]{:S(2)}, u32[]{:S(2)}) collective-permute-start(bf16[8,32,512]{2,1,0:T(8,128)(2,1)S(1)} %cross.3._.after_ref.refs_0_.refs_3_), channel_id=1, source_target_pairs={{0,2},{1,3},{4,5},{5,4},{8,10},{9,11},{12,13},{13,12},{16,18},{17,... | collective-permute-start | bytes 786440 | tf_op jit(solution)/shard_map/ppermute | solution.py:412
  8.6 0.7 %collective-permute-start.2 = (bf16[8,32,512]{2,1,0:T(8,128)(2,1)S(1)}, bf16[8,32,512]{2,1,0:T(8,128)(2,1)S(1)}, u32[]{:S(2)}, u32[]{:S(2)}) collective-permute-start(bf16[8,32,512]{2,1,0:T(8,128)(2,1)S(1)} %cross.3._.after_ref.refs_0_.refs_3_), channel_id=1, source_target_pairs={{6,7},{14,15},{22,23},{30,31}} | collective-permute-start | bytes 786440 | tf_op jit(solution)/shard_map/ppermute | solution.py:412
  9.3 1.3 %tail.4 = (f32[8,32,512]{2,1,0:T(8,128)S(1)}, bf16[32,4096]{1,0:T(8,128)(2,1)S(1)}, bf16[8,32,512]{2,1,0:T(8,128)(2,1)S(1)}) custom-call(bf16[512,512]{1,0:T(8,128)(2,1)S(1)} %bitcast.5, bf16[512,512]{1,0:T(8,128)(2,1)S(1)} %get-tuple-element.20.table_ref.after_ref, f32[64,1024]{1,0:T(8,128)S(1)} %get-tuple-element.21.keep_ref, ...), custom_call_target="tpu_custom_call" | custom-call | flops 268435456 | bytes 4194304 | tf_op jit(solution)/shard_map/tail/pallas_call | solution.py:377
  10.6 0.8 %cross.4.refs_1_.refs_3_ = bf16[8,32,512]{2,1,0:T(8,128)(2,1)S(1)} custom-call(bf16[8,32,64]{2,1,0:T(8,128)(2,1)S(1)} %get-tuple-element.19.pick_ref, f32[8,32,512]{2,1,0:T(8,128)S(1)} %get-tuple-element.26.white_ref, bf16[32,4096]{1,0:T(8,128)(2,1)S(1)} %get-tuple-element.27.short_ref, bf16[32,4096]{1,0:T(8,128)(2,1)S(1)} %collective-permute-done.edge_ref, ...), custom_call_target="tpu_custom_call" | custom-call | flops 4194304 | bytes 4194304 | tf_op jit(solution)/shard_map/cross/pallas_call | solution.py:389
  11.4 0.4 %collective-permute-done.4.refs_2_.rest_3_ = bf16[8,32,512]{2,1,0:T(8,128)(2,1)S(1)} collective-permute-done((bf16[8,32,512]{2,1,0:T(8,128)(2,1)S(1)}, bf16[8,32,512]{2,1,0:T(8,128)(2,1)S(1)}, u32[]{:S(2)}, u32[]{:S(2)}) %collective-permute-start.4) | collective-permute-done | bytes 262176 | tf_op jit(solution)/shard_map/ppermute | solution.py:412
  11.8 0.1 mix.3
  11.9 3.4 %collective-permute-start.5 = (bf16[8,32,512]{2,1,0:T(8,128)(2,1)S(1)}, bf16[8,32,512]{2,1,0:T(8,128)(2,1)S(1)}, u32[]{:S(2)}, u32[]{:S(2)}) collective-permute-start(bf16[8,32,512]{2,1,0:T(8,128)(2,1)S(1)} %mix.3), channel_id=1, source_target_pairs={{0,1},{2,3},{3,2},{4,6},{5,7},{8,9},{10,11},{11,10},{12,14},{13,15... | collective-permute-start | bytes 786440 | tf_op jit(solution)/shard_map/ppermute | solution.py:412
  15.3 0.6 %collective-permute-done.1.refs_2_.refs_3_ = bf16[8,32,512]{2,1,0:T(8,128)(2,1)S(1)} collective-permute-done((bf16[8,32,512]{2,1,0:T(8,128)(2,1)S(1)}, bf16[8,32,512]{2,1,0:T(8,128)(2,1)S(1)}, u32[]{:S(2)}, u32[]{:S(2)}) %collective-permute-start.1) | collective-permute-done | bytes 262176 | tf_op jit(solution)/shard_map/ppermute | solution.py:412
  16.0 0.1 mix.2.after_ref
  16.1 3.0 %collective-permute-start.3 = (bf16[8,32,512]{2,1,0:T(8,128)(2,1)S(1)}, bf16[8,32,512]{2,1,0:T(8,128)(2,1)S(1)}, u32[]{:S(2)}, u32[]{:S(2)}) collective-permute-start(bf16[8,32,512]{2,1,0:T(8,128)(2,1)S(1)} %mix.2.after_ref), channel_id=1, source_target_pairs={{0,1},{2,3},{3,2},{4,6},{5,7},{8,9},{10,11},{11,10},{12,14},{13,15... | collective-permute-start | bytes 786440 | tf_op jit(solution)/shard_map/ppermute | solution.py:412
  19.1 0.3 %inverse.1.table_ref = bf16[512,512]{1,0:T(8,128)(2,1)S(1)} custom-call(bf16[8,32,512]{2,1,0:T(8,128)(2,1)S(1)} %cross.3._.after_ref.refs_0_.refs_3_), custom_call_target="tpu_custom_call" | custom-call | flops 4194304 | bytes 524288 | tf_op jit(solution)/shard_map/inverse/pallas_call | solution.py:425
  19.5 0.0 collective-permute-done.2.refs_4_
  19.5 0.4 %part.1.rest_5_.part_ref = f32[256,512]{1,0:T(8,128)S(1)} custom-call(bf16[512,512]{1,0:T(8,128)(2,1)S(1)} %inverse.1.table_ref, bf16[8,32,512]{2,1,0:T(8,128)(2,1)S(1)} %cross.3._.after_ref.refs_0_.refs_3_, bf16[8,32,512]{2,1,0:T(8,128)(2,1)S(1)} %cross.4.refs_1_.refs_3_, bf16[8,32,512]{2,1,0:T(8,128)(2,1)S(1)} %cross.5.refs_2_, ...), custom_call_target="tpu_custom_call" | custom-call | flops 268435456 | bytes 1048576 | tf_op jit(solution)/shard_map/part/pallas_call | solution.py:452
  20.0 0.2 collective-permute-done.5.rest_4_
  20.2 1.2 %lags.2.rest_0_ = bf16[8,64,512]{2,1,0:T(8,128)(2,1)} custom-call(bf16[512,512]{1,0:T(8,128)(2,1)S(1)} %inverse.1.table_ref, bf16[8,32,512]{2,1,0:T(8,128)(2,1)S(1)} %get-tuple-element.30.refs_0_.rest_0_, bf16[8,32,512]{2,1,0:T(8,128)(2,1)S(1)} %get-tuple-element.31.refs_1_.rest_1_, bf16[8,32,512]{2,1,0:T(8,128)(2,1)S(1)} %get-tuple-element.32.rest_2_, ...), custom_call_target="tpu_custom_call" | custom-call | flops 268435456 | bytes 1048576 | tf_op jit(solution)/shard_map/lags/pallas_call | solution.py:436
  21.4 3.0 %collective-permute-done.3.more_ref = bf16[8,32,512]{2,1,0:T(8,128)(2,1)S(1)} collective-permute-done((bf16[8,32,512]{2,1,0:T(8,128)(2,1)S(1)}, bf16[8,32,512]{2,1,0:T(8,128)(2,1)S(1)}, u32[]{:S(2)}, u32[]{:S(2)}) %collective-permute-start.3) | collective-permute-done | bytes 262176 | tf_op jit(solution)/shard_map/ppermute | solution.py:412
  24.4 1.0 %lags.3 = bf16[8,64,512]{2,1,0:T(8,128)(2,1)} custom-call(bf16[512,512]{1,0:T(8,128)(2,1)S(1)} %inverse.1.table_ref, f32[256,512]{1,0:T(8,128)S(1)} %part.1.rest_5_.part_ref, bf16[8,32,512]{2,1,0:T(8,128)(2,1)S(1)} %collective-permute-done.3.more_ref, bf16[8,64,512]{2,1,0:T(8,128)(2,1)} %lags.2.rest_0_), custom_call_target="tpu_custom_call", output_to_operand_aliasing={{}: (3, {})} | custom-call | flops 268435456 | bytes 1048576 | tf_op jit(solution)/shard_map/lags/pallas_call | solution.py:436
  (4 shorter events, 0.1 us)
Async XLA Ops:
  0.0 3.5 %copy-start = (bf16[64,8,512]{2,1,0:T(8,128)(2,1)S(1)}, bf16[64,8,512]{2,1,0:T(8,128)(2,1)}, u32[]{:S(2)}) copy-start(bf16[64,8,512]{2,1,0:T(8,128)(2,1)} %param.3) | copy-start | bytes 1572868
  1.5 5.8 %collective-permute-start = (bf16[32,4096]{1,0:T(8,128)(2,1)S(1)}, bf16[32,4096]{1,0:T(8,128)(2,1)S(1)}, u32[]{:S(2)}, u32[]{:S(2)}) collective-permute-start(bf16[32,4096]{1,0:T(8,128)(2,1)S(1)} %get-tuple-element.23.edge_ref), channel_id=1, source_target_pairs={{4,0},{8,4},{12,8},{16,12},{20,16},{24,20},{28,24},{5,1},{9,5},{13... | collective-permute-start | bytes 786440 | tf_op jit(solution)/shard_map/ppermute | solution.py:370
  3.5 8.3 %collective-permute-start.4 = (bf16[8,32,512]{2,1,0:T(8,128)(2,1)S(1)}, bf16[8,32,512]{2,1,0:T(8,128)(2,1)S(1)}, u32[]{:S(2)}, u32[]{:S(2)}) collective-permute-start(bf16[8,32,512]{2,1,0:T(8,128)(2,1)S(1)} %get-tuple-element.30.refs_0_.rest_0_), channel_id=1, source_target_pairs={{0,2},{1,3},{4,5},{5,4},{6,7},{8,10},{9,11},{12,13},{13,12},{14,15... | collective-permute-start | bytes 786440 | tf_op jit(solution)/shard_map/ppermute | solution.py:412
  7.3 8.6 %collective-permute-start.1 = (bf16[8,32,512]{2,1,0:T(8,128)(2,1)S(1)}, bf16[8,32,512]{2,1,0:T(8,128)(2,1)S(1)}, u32[]{:S(2)}, u32[]{:S(2)}) collective-permute-start(bf16[8,32,512]{2,1,0:T(8,128)(2,1)S(1)} %cross.3._.after_ref.refs_0_.refs_3_), channel_id=1, source_target_pairs={{0,2},{1,3},{4,5},{5,4},{8,10},{9,11},{12,13},{13,12},{16,18},{17,... | collective-permute-start | bytes 786440 | tf_op jit(solution)/shard_map/ppermute | solution.py:412
  8.6 10.9 %collective-permute-start.2 = (bf16[8,32,512]{2,1,0:T(8,128)(2,1)S(1)}, bf16[8,32,512]{2,1,0:T(8,128)(2,1)S(1)}, u32[]{:S(2)}, u32[]{:S(2)}) collective-permute-start(bf16[8,32,512]{2,1,0:T(8,128)(2,1)S(1)} %cross.3._.after_ref.refs_0_.refs_3_), channel_id=1, source_target_pairs={{6,7},{14,15},{22,23},{30,31}} | collective-permute-start | bytes 786440 | tf_op jit(solution)/shard_map/ppermute | solution.py:412
  11.9 8.3 %collective-permute-start.5 = (bf16[8,32,512]{2,1,0:T(8,128)(2,1)S(1)}, bf16[8,32,512]{2,1,0:T(8,128)(2,1)S(1)}, u32[]{:S(2)}, u32[]{:S(2)}) collective-permute-start(bf16[8,32,512]{2,1,0:T(8,128)(2,1)S(1)} %mix.3), channel_id=1, source_target_pairs={{0,1},{2,3},{3,2},{4,6},{5,7},{8,9},{10,11},{11,10},{12,14},{13,15... | collective-permute-start | bytes 786440 | tf_op jit(solution)/shard_map/ppermute | solution.py:412
  16.1 8.3 %collective-permute-start.3 = (bf16[8,32,512]{2,1,0:T(8,128)(2,1)S(1)}, bf16[8,32,512]{2,1,0:T(8,128)(2,1)S(1)}, u32[]{:S(2)}, u32[]{:S(2)}) collective-permute-start(bf16[8,32,512]{2,1,0:T(8,128)(2,1)S(1)} %mix.2.after_ref), channel_id=1, source_target_pairs={{0,1},{2,3},{3,2},{4,6},{5,7},{8,9},{10,11},{11,10},{12,14},{13,15... | collective-permute-start | bytes 786440 | tf_op jit(solution)/shard_map/ppermute | solution.py:412

commit v7 on v6

--- a/solution.py
+++ b/solution.py
@@ -68,8 +68,9 @@
         table_ref[bins + first : bins + first + step, :] = (-sine).astype(jnp.bfloat16)
 
 
-def whiten_block(x, table_ref, keep, raw_ref, white_ref, short_ref):
-    wins, span, length = white_ref.shape
+def whiten_block(x, table_ref, keep, raw_ref, short_ref):
+    span = short_ref.shape[0]
+    wins, length = x.shape[0] // span, x.shape[1]
     bins = length // 2
     tiles = bins // LANES
 
@@ -88,7 +89,6 @@
             power = real_part * real_part + imag_part * imag_part
             total[w] = power if t == 0 else total[w] + power
     for w in range(wins):
-        decay = float(np.float32(DECAY) ** np.float32(wins - 1 - w))
         level = jnp.sum(total[w], axis=-1, keepdims=True) * (0.01 / bins) + 1e-06
         alive = keep[:, w * LANES : (w + 1) * LANES]
         for t in range(tiles):
@@ -98,7 +98,6 @@
             for i, s in enumerate((t, tiles + t)):
                 value = part[i] * scale
                 here = pl.ds(w * length + s * LANES, LANES)
-                white_ref[w, :, s * LANES : (s + 1) * LANES] = value * decay
                 short_ref[:, here] = value.astype(jnp.bfloat16)
 
 
@@ -106,7 +105,6 @@
     x_hbm,
     valid_hbm,
     offsets_hbm,
-    white_ref,
     short_ref,
     table_ref,
     pick_ref,
@@ -117,7 +115,8 @@
     raw_ref,
     sems,
 ):
-    wins, span, length = white_ref.shape
+    span = short_ref.shape[0]
+    wins = valid_ref.shape[0]
     pairs = offsets_ref.shape[0]
     copies = [
         pltpu.make_async_copy(valid_hbm, valid_ref, sems.at[0]),
@@ -144,12 +143,13 @@
         preferred_element_type=jnp.float32,
     )
     copies[2].wait()
-    whiten_block(x_ref[...], table_ref, keep_ref[:span], raw_ref, white_ref, short_ref)
-
-
-def stack_pairs(pick_ref, white_ref, near_ref, parts_refs, out_ref):
-    wins, _, length = white_ref.shape
+    whiten_block(x_ref[...], table_ref, keep_ref[:span], raw_ref, short_ref)
+
+
+def stack_pairs(pick_ref, near_ref, parts_refs, out_ref):
     pairs, rows, reach = pick_ref.shape
+    length = out_ref.shape[2]
+    wins = near_ref.shape[1] // length
     bins = length // 2
     size = pairs // len(parts_refs)
 
@@ -157,6 +157,11 @@
         pick = pick_ref[group * size : (group + 1) * size].reshape(size * rows, reach)
         near = near_ref[:, w * length : (w + 1) * length]
         parts_refs[group][w] = jnp.dot(pick, near, preferred_element_type=jnp.float32)
+
+    def head(w, c, lane):
+        lanes = slice(w * length + lane, w * length + lane + LANES)
+        decay = float(np.float32(DECAY) ** np.float32(wins - 1 - w))
+        return near_ref[c : c + 16, lanes].astype(jnp.float32) * decay
 
     blocks = [(c, t) for c in range(0, rows, 16) for t in range(bins // LANES)]
     for w in range(wins):
@@ -168,8 +173,8 @@
                 select(group + 1, w)
             re = slice(t * LANES, (t + 1) * LANES)
             im = slice(bins + t * LANES, bins + (t + 1) * LANES)
-            head_re = [white_ref[w, c : c + 16, re] for w in range(wins)]
-            head_im = [white_ref[w, c : c + 16, im] for w in range(wins)]
+            head_re = [head(w, c, t * LANES) for w in range(wins)]
+            head_im = [head(w, c, bins + t * LANES) for w in range(wins)]
             for k in range(size):
                 here = slice(k * rows + c, k * rows + c + 16)
                 total_re = total_im = None
@@ -197,30 +202,29 @@
     table_ref,
     keep_ref,
     pick_ref,
-    head_ref,
     edge_ref,
     after_ref,
-    white_ref,
     short_ref,
     out_ref,
     raw_ref,
     near_ref,
     *parts_refs,
 ):
-    wins, span, length = white_ref.shape
+    span = short_ref.shape[0]
+    wins = x_ref.shape[0] // (2 * span)
     rows = slice(span * wins, 2 * span * wins)
 
     @pl.when(role(limits) == now)
     def _():
         x = x_ref[rows, :]
-        whiten_block(x, table_ref, keep_ref[span:], raw_ref, white_ref, short_ref)
+        whiten_block(x, table_ref, keep_ref[span:], raw_ref, short_ref)
         near_ref[:span] = edge_ref[...]
         near_ref[span:] = short_ref[...]
-        stack_pairs(pick_ref, head_ref, near_ref, parts_refs, out_ref)
+        stack_pairs(pick_ref, near_ref, parts_refs, out_ref)
 
 
 def cross_kernel(
-    limits, now, pick_ref, white_ref, short_ref, edge_ref, after_ref, out_ref, near_ref, *parts_refs
+    limits, now, pick_ref, short_ref, edge_ref, after_ref, out_ref, near_ref, *parts_refs
 ):
     span = short_ref.shape[0]
 
@@ -228,7 +232,7 @@
     def _():
         near_ref[:span] = short_ref[...]
         near_ref[span:] = edge_ref[...]
-        stack_pairs(pick_ref, white_ref, near_ref, parts_refs, out_ref)
+        stack_pairs(pick_ref, near_ref, parts_refs, out_ref)
 
 
 def chosen(options, place):
@@ -336,24 +340,22 @@
 
     half = chans - span
     flat = samples.reshape(chans * wins, length)
-    white_type = jax.ShapeDtypeStruct((wins, span, length), jnp.float32)
     short_type = jax.ShapeDtypeStruct((span, wins * length), jnp.bfloat16)
     local_type = jax.ShapeDtypeStruct((pairs, span, length), jnp.bfloat16)
     raw_scratch = pltpu.VMEM((2 * tiles, span * wins, LANES), jnp.float32)
     near_scratch = pltpu.VMEM((2 * span, wins * length), jnp.bfloat16)
     parts_scratch = [pltpu.VMEM((wins, pairs // 4 * span, length), jnp.float32)] * 4
 
-    white_a, short_a, table, pick, keep = pl.pallas_call(
+    short_a, table, pick, keep = pl.pallas_call(
         head_kernel,
         out_shape=(
-            white_type,
             short_type,
             jax.ShapeDtypeStruct((length, length), jnp.bfloat16),
             jax.ShapeDtypeStruct((pairs, span, 2 * span), jnp.bfloat16),
             jax.ShapeDtypeStruct((chans, wins * LANES), jnp.float32),
         ),
         in_specs=[whole(pltpu.HBM)] * 3,
-        out_specs=(whole(),) * 5,
+        out_specs=(whole(),) * 4,
         scratch_shapes=[
             pltpu.VMEM((span * wins, length), jnp.bfloat16),
             pltpu.VMEM((wins, chans), jnp.int32),
@@ -376,31 +378,31 @@
     def tail(now, after):
         return pl.pallas_call(
             functools.partial(tail_kernel, limits, now),
-            out_shape=(white_type, short_type, local_type),
-            in_specs=[whole()] * 6 + [whole(pl.ANY)],
-            out_specs=(whole(),) * 3,
+            out_shape=(short_type, local_type),
+            in_specs=[whole()] * 5 + [whole(pl.ANY)],
+            out_specs=(whole(),) * 2,
             scratch_shapes=[raw_scratch, near_scratch] + parts_scratch,
             compiler_params=params,
             cost_estimate=cost(span * wins * length * length * 4, 4 * 1024 * 1024),
             name="tail",
-        )(flat, table, keep, pick, white_a, short_a, after)
-
-    def cross(now, white, short, after):
+        )(flat, table, keep, pick, short_a, after)
+
+    def cross(now, short, after):
         return pl.pallas_call(
             functools.partial(cross_kernel, limits, now),
             out_shape=local_type,
-            in_specs=[whole()] * 4 + [whole(pl.ANY)],
+            in_specs=[whole()] * 3 + [whole(pl.ANY)],
             out_specs=whole(),
             scratch_shapes=[near_scratch] + parts_scratch,
             compiler_params=params,
             cost_estimate=cost(pairs * span * wins * bins * 8, 4 * 1024 * 1024),
             name="cross",
-        )(pick, white, short, edge, after)
-
-    white_b, short_b, local_a = tail(0, table)
-    local_b = cross(0, white_b, short_b, table)
-    white_late, short_late, late_a = tail(1, local_b)
-    late_b = cross(1, white_late, short_late, local_b)
+        )(pick, short, edge, after)
+
+    short_b, local_a = tail(0, table)
+    local_b = cross(0, short_b, table)
+    short_late, late_a = tail(1, local_b)
+    late_b = cross(1, short_late, local_b)
 
     power = [float(np.float32(factor) ** np.float32(d)) for d in range(groups)]
     def sent(value, even, odd):
@@ -491,8 +493,8 @@
     scale = bins**-0.5
     _, terms_a, weights_a = spread(local_a, late_a, late_b, False)
     ahead, terms_b, weights_b = spread(local_b, late_b, local_b, True)
-    white_last, short_last, last_a = tail(2, ahead)
-    last_b = cross(2, white_last, short_last, ahead)
+    short_last, last_a = tail(2, ahead)
+    last_b = cross(2, short_last, ahead)
     terms_a = [local_a, late_a, last_a] + terms_a
     terms_b = [local_b, late_b, last_b] + terms_b
     before = part(terms_b[:-1], weights_b[:-1])

time: 25.6 us -> 26.4 us (1.031)
  the two profiles are of different devices: /device:TPU:28 before, /device:TPU:7 now
where the time goes in v7:
time: 26.4 us; the launch traced here: 26.2 us
  waiting for transfers between devices  9.93 us (38%)
  starting transfers between devices  8.42 us (32%)
  Pallas kernels  7.69 us (29%)
    ppermute x5, starting transfers between devices, sent(): return lax.ppermute(value, ('chan', 'tm'), moves)  5.83 us
    ppermute x5, waiting for transfers between devices, sent(): return lax.ppermute(value, ('chan', 'tm'), moves)  5.76 us
    ppermute x1, waiting for transfers between devices, per_device(): edge = lax.ppermute(short_a, 'chan', [(i, i - 1) for i in range(1, ring)])  4.18 us
    ppermute x1, starting transfers between devices, per_device(): edge = lax.ppermute(short_a, 'chan', [(i, i - 1) for i in range(1, ring)])  2.58 us
    pallas_call x2, Pallas kernels, written(): pl.pallas_call(kernel, out_shape=jax.ShapeDtypeStruct((pairs, chans, leng...  2.16 us
    pallas_call x3, Pallas kernels, tail(): pl.pallas_call(functools.partial(tail_kernel, limits, now), out_shape=(sh...  1.83 us
    pallas_call x1, Pallas kernels, per_device(): pl.pallas_call(head_kernel, out_shape=(short_type, jax.ShapeDtypeStruct((...  1.51 us
    pallas_call x3, Pallas kernels, cross(): pl.pallas_call(functools.partial(cross_kernel, limits, now), out_shape=lo...  1.21 us
  transfers between devices with their start and end apart: 6, of which 4 were waited for; matrix products, arithmetic and copies ran while one was open for 0% of the time, Pallas kernels for 20%

profile of v7, /device:TPU:7, one launch (start us, length us, event | category | flops | bytes accessed | tf_op | source)
XLA Modules:
  0.0 26.2 jit_solution(14896079067873069093)
XLA Ops:
  0.0 0.0 copy-start
  0.0 1.5 %head.1 = (bf16[32,4096]{1,0:T(8,128)(2,1)S(1)}, bf16[512,512]{1,0:T(8,128)(2,1)S(1)}, bf16[8,32,64]{2,1,0:T(8,128)(2,1)S(1)}, f32[64,1024]{1,0:T(8,128)S(1)}) custom-call(bf16[512,512]{1,0:T(8,128)(2,1)} %bitcast.3, s32[8,64]{1,0:T(8,128)} %bitcast.7, s32[8]{0:T(128)} %offsets_hbm.1), custom_call_target="tpu_custom_call" | custom-call | flops 134217728 | bytes 2097152 | tf_op jit(solution)/shard_map/head/pallas_call | solution.py:349
  1.5 2.6 %collective-permute-start = (bf16[32,4096]{1,0:T(8,128)(2,1)S(1)}, bf16[32,4096]{1,0:T(8,128)(2,1)S(1)}, u32[]{:S(2)}, u32[]{:S(2)}) collective-permute-start(bf16[32,4096]{1,0:T(8,128)(2,1)S(1)} %get-tuple-element.18.edge_ref), channel_id=1, source_target_pairs={{4,0},{8,4},{12,8},{16,12},{20,16},{24,20},{28,24},{5,1},{9,5},{13... | collective-permute-start | bytes 786440 | tf_op jit(solution)/shard_map/ppermute | solution.py:372
  4.1 0.0 copy-done
  4.2 1.3 %collective-permute-start.4 = (bf16[8,32,512]{2,1,0:T(8,128)(2,1)S(1)}, bf16[8,32,512]{2,1,0:T(8,128)(2,1)S(1)}, u32[]{:S(2)}, u32[]{:S(2)}) collective-permute-start(bf16[8,32,512]{2,1,0:T(8,128)(2,1)S(1)} %get-tuple-element.22.refs_0_.rest_0_), channel_id=1, source_target_pairs={{0,2},{1,3},{4,5},{5,4},{6,7},{8,10},{9,11},{12,13},{13,12},{14,15... | collective-permute-start | bytes 786440 | tf_op jit(solution)/shard_map/ppermute | solution.py:414
  5.5 4.2 %collective-permute-done.edge_ref = bf16[32,4096]{1,0:T(8,128)(2,1)S(1)} collective-permute-done((bf16[32,4096]{1,0:T(8,128)(2,1)S(1)}, bf16[32,4096]{1,0:T(8,128)(2,1)S(1)}, u32[]{:S(2)}, u32[]{:S(2)}) %collective-permute-start) | collective-permute-done | bytes 262176 | tf_op jit(solution)/shard_map/ppermute | solution.py:372
  9.6 0.7 %collective-permute-start.1 = (bf16[8,32,512]{2,1,0:T(8,128)(2,1)S(1)}, bf16[8,32,512]{2,1,0:T(8,128)(2,1)S(1)}, u32[]{:S(2)}, u32[]{:S(2)}) collective-permute-start(bf16[8,32,512]{2,1,0:T(8,128)(2,1)S(1)} %cross.3._.after_ref.refs_0_.refs_3_), channel_id=1, source_target_pairs={{0,2},{1,3},{4,5},{5,4},{8,10},{9,11},{12,13},{13,12},{16,18},{17,... | collective-permute-start | bytes 786440 | tf_op jit(solution)/shard_map/ppermute | solution.py:414
  10.3 1.3 %collective-permute-start.2 = (bf16[8,32,512]{2,1,0:T(8,128)(2,1)S(1)}, bf16[8,32,512]{2,1,0:T(8,128)(2,1)S(1)}, u32[]{:S(2)}, u32[]{:S(2)}) collective-permute-start(bf16[8,32,512]{2,1,0:T(8,128)(2,1)S(1)} %cross.3._.after_ref.refs_0_.refs_3_), channel_id=1, source_target_pairs={{6,7},{14,15},{22,23},{30,31}} | collective-permute-start | bytes 786440 | tf_op jit(solution)/shard_map/ppermute | solution.py:414
  11.7 0.0 collective-permute-done.4.refs_2_.rest_3_
  11.7 0.1 mix.3
  11.8 1.3 %collective-permute-start.5 = (bf16[8,32,512]{2,1,0:T(8,128)(2,1)S(1)}, bf16[8,32,512]{2,1,0:T(8,128)(2,1)S(1)}, u32[]{:S(2)}, u32[]{:S(2)}) collective-permute-start(bf16[8,32,512]{2,1,0:T(8,128)(2,1)S(1)} %mix.3), channel_id=1, source_target_pairs={{0,1},{2,3},{3,2},{4,6},{5,7},{8,9},{10,11},{11,10},{12,14},{13,15... | collective-permute-start | bytes 786440 | tf_op jit(solution)/shard_map/ppermute | solution.py:414
  13.1 0.0 collective-permute-done.1.refs_2_.refs_3_
  13.1 0.1 mix.2.after_ref
  13.3 1.3 %collective-permute-start.3 = (bf16[8,32,512]{2,1,0:T(8,128)(2,1)S(1)}, bf16[8,32,512]{2,1,0:T(8,128)(2,1)S(1)}, u32[]{:S(2)}, u32[]{:S(2)}) collective-permute-start(bf16[8,32,512]{2,1,0:T(8,128)(2,1)S(1)} %mix.2.after_ref), channel_id=1, source_target_pairs={{0,1},{2,3},{3,2},{4,6},{5,7},{8,9},{10,11},{11,10},{12,14},{13,15... | collective-permute-start | bytes 786440 | tf_op jit(solution)/shard_map/ppermute | solution.py:414
  14.6 0.3 %inverse.1.table_ref = bf16[512,512]{1,0:T(8,128)(2,1)S(1)} custom-call(bf16[8,32,512]{2,1,0:T(8,128)(2,1)S(1)} %cross.3._.after_ref.refs_0_.refs_3_), custom_call_target="tpu_custom_call" | custom-call | flops 4194304 | bytes 524288 | tf_op jit(solution)/shard_map/inverse/pallas_call | solution.py:427
  14.9 1.8 %tail.5 = (bf16[32,4096]{1,0:T(8,128)(2,1)S(1)}, bf16[8,32,512]{2,1,0:T(8,128)(2,1)S(1)}) custom-call(bf16[512,512]{1,0:T(8,128)(2,1)S(1)} %bitcast.6, bf16[512,512]{1,0:T(8,128)(2,1)S(1)} %get-tuple-element.16.table_ref.after_ref, f32[64,1024]{1,0:T(8,128)S(1)} %get-tuple-element.17.keep_ref, bf16[8,32,64]{2,1,0:T(8,128)(2,1)S(1)} %get-tuple-element.15.pick_ref, ...), custom_call_target="tpu_custom_call" | custom-call | flops 268435456 | bytes 4194304 | tf_op jit(solution)/shard_map/tail/pallas_call | solution.py:379
  16.6 1.2 %cross.5.refs_2_ = bf16[8,32,512]{2,1,0:T(8,128)(2,1)S(1)} custom-call(bf16[8,32,64]{2,1,0:T(8,128)(2,1)S(1)} %get-tuple-element.15.pick_ref, bf16[32,4096]{1,0:T(8,128)(2,1)S(1)} %get-tuple-element.21.short_ref, bf16[32,4096]{1,0:T(8,128)(2,1)S(1)} %collective-permute-done.edge_ref, bf16[8,32,512]{2,1,0:T(8,128)(2,1)S(1)} %mix.2.after_ref), custom_call_target="tpu_custom_call" | custom-call | flops 4194304 | bytes 4194304 | tf_op jit(solution)/shard_map/cross/pallas_call | solution.py:391
  17.8 0.5 %collective-permute-done.2.refs_4_ = bf16[8,32,512]{2,1,0:T(8,128)(2,1)S(1)} collective-permute-done((bf16[8,32,512]{2,1,0:T(8,128)(2,1)S(1)}, bf16[8,32,512]{2,1,0:T(8,128)(2,1)S(1)}, u32[]{:S(2)}, u32[]{:S(2)}) %collective-permute-start.2) | collective-permute-done | bytes 262176 | tf_op jit(solution)/shard_map/ppermute | solution.py:414
  18.4 0.4 %part.1.rest_5_.part_ref = f32[256,512]{1,0:T(8,128)S(1)} custom-call(bf16[512,512]{1,0:T(8,128)(2,1)S(1)} %inverse.1.table_ref, bf16[8,32,512]{2,1,0:T(8,128)(2,1)S(1)} %cross.3._.after_ref.refs_0_.refs_3_, bf16[8,32,512]{2,1,0:T(8,128)(2,1)S(1)} %cross.4.refs_1_.refs_3_, bf16[8,32,512]{2,1,0:T(8,128)(2,1)S(1)} %cross.5.refs_2_, ...), custom_call_target="tpu_custom_call" | custom-call | flops 268435456 | bytes 1048576 | tf_op jit(solution)/shard_map/part/pallas_call | solution.py:454
  18.8 0.4 %collective-permute-done.5.rest_4_ = bf16[8,32,512]{2,1,0:T(8,128)(2,1)S(1)} collective-permute-done((bf16[8,32,512]{2,1,0:T(8,128)(2,1)S(1)}, bf16[8,32,512]{2,1,0:T(8,128)(2,1)S(1)}, u32[]{:S(2)}, u32[]{:S(2)}) %collective-permute-start.5) | collective-permute-done | bytes 262176 | tf_op jit(solution)/shard_map/ppermute | solution.py:414
  19.2 1.2 %lags.2.rest_0_ = bf16[8,64,512]{2,1,0:T(8,128)(2,1)} custom-call(bf16[512,512]{1,0:T(8,128)(2,1)S(1)} %inverse.1.table_ref, bf16[8,32,512]{2,1,0:T(8,128)(2,1)S(1)} %get-tuple-element.22.refs_0_.rest_0_, bf16[8,32,512]{2,1,0:T(8,128)(2,1)S(1)} %get-tuple-element.23.refs_1_.rest_1_, bf16[8,32,512]{2,1,0:T(8,128)(2,1)S(1)} %get-tuple-element.24.rest_2_, ...), custom_call_target="tpu_custom_call" | custom-call | flops 268435456 | bytes 1048576 | tf_op jit(solution)/shard_map/lags/pallas_call | solution.py:438
  20.4 4.8 %collective-permute-done.3.more_ref = bf16[8,32,512]{2,1,0:T(8,128)(2,1)S(1)} collective-permute-done((bf16[8,32,512]{2,1,0:T(8,128)(2,1)S(1)}, bf16[8,32,512]{2,1,0:T(8,128)(2,1)S(1)}, u32[]{:S(2)}, u32[]{:S(2)}) %collective-permute-start.3) | collective-permute-done | bytes 262176 | tf_op jit(solution)/shard_map/ppermute | solution.py:414
  25.2 1.0 %lags.3 = bf16[8,64,512]{2,1,0:T(8,128)(2,1)} custom-call(bf16[512,512]{1,0:T(8,128)(2,1)S(1)} %inverse.1.table_ref, f32[256,512]{1,0:T(8,128)S(1)} %part.1.rest_5_.part_ref, bf16[8,32,512]{2,1,0:T(8,128)(2,1)S(1)} %collective-permute-done.3.more_ref, bf16[8,64,512]{2,1,0:T(8,128)(2,1)} %lags.2.rest_0_), custom_call_target="tpu_custom_call", output_to_operand_aliasing={{}: (3, {})} | custom-call | flops 268435456 | bytes 1048576 | tf_op jit(solution)/shard_map/lags/pallas_call | solution.py:438
  (4 shorter events, 0.1 us)
Async XLA Ops:
  0.0 4.1 %copy-start = (bf16[64,8,512]{2,1,0:T(8,128)(2,1)S(1)}, bf16[64,8,512]{2,1,0:T(8,128)(2,1)}, u32[]{:S(2)}) copy-start(bf16[64,8,512]{2,1,0:T(8,128)(2,1)} %param.3) | copy-start | bytes 1572868
  1.5 8.1 %collective-permute-start = (bf16[32,4096]{1,0:T(8,128)(2,1)S(1)}, bf16[32,4096]{1,0:T(8,128)(2,1)S(1)}, u32[]{:S(2)}, u32[]{:S(2)}) collective-permute-start(bf16[32,4096]{1,0:T(8,128)(2,1)S(1)} %get-tuple-element.18.edge_ref), channel_id=1, source_target_pairs={{4,0},{8,4},{12,8},{16,12},{20,16},{24,20},{28,24},{5,1},{9,5},{13... | collective-permute-start | bytes 786440 | tf_op jit(solution)/shard_map/ppermute | solution.py:372
  4.2 7.5 %collective-permute-start.4 = (bf16[8,32,512]{2,1,0:T(8,128)(2,1)S(1)}, bf16[8,32,512]{2,1,0:T(8,128)(2,1)S(1)}, u32[]{:S(2)}, u32[]{:S(2)}) collective-permute-start(bf16[8,32,512]{2,1,0:T(8,128)(2,1)S(1)} %get-tuple-element.22.refs_0_.rest_0_), channel_id=1, source_target_pairs={{0,2},{1,3},{4,5},{5,4},{6,7},{8,10},{9,11},{12,13},{13,12},{14,15... | collective-permute-start | bytes 786440 | tf_op jit(solution)/shard_map/ppermute | solution.py:414
  9.6 3.5 %collective-permute-start.1 = (bf16[8,32,512]{2,1,0:T(8,128)(2,1)S(1)}, bf16[8,32,512]{2,1,0:T(8,128)(2,1)S(1)}, u32[]{:S(2)}, u32[]{:S(2)}) collective-permute-start(bf16[8,32,512]{2,1,0:T(8,128)(2,1)S(1)} %cross.3._.after_ref.refs_0_.refs_3_), channel_id=1, source_target_pairs={{0,2},{1,3},{4,5},{5,4},{8,10},{9,11},{12,13},{13,12},{16,18},{17,... | collective-permute-start | bytes 786440 | tf_op jit(solution)/shard_map/ppermute | solution.py:414
  10.3 8.1 %collective-permute-start.2 = (bf16[8,32,512]{2,1,0:T(8,128)(2,1)S(1)}, bf16[8,32,512]{2,1,0:T(8,128)(2,1)S(1)}, u32[]{:S(2)}, u32[]{:S(2)}) collective-permute-start(bf16[8,32,512]{2,1,0:T(8,128)(2,1)S(1)} %cross.3._.after_ref.refs_0_.refs_3_), channel_id=1, source_target_pairs={{6,7},{14,15},{22,23},{30,31}} | collective-permute-start | bytes 786440 | tf_op jit(solution)/shard_map/ppermute | solution.py:414
  11.8 7.4 %collective-permute-start.5 = (bf16[8,32,512]{2,1,0:T(8,128)(2,1)S(1)}, bf16[8,32,512]{2,1,0:T(8,128)(2,1)S(1)}, u32[]{:S(2)}, u32[]{:S(2)}) collective-permute-start(bf16[8,32,512]{2,1,0:T(8,128)(2,1)S(1)} %mix.3), channel_id=1, source_target_pairs={{0,1},{2,3},{3,2},{4,6},{5,7},{8,9},{10,11},{11,10},{12,14},{13,15... | collective-permute-start | bytes 786440 | tf_op jit(solution)/shard_map/ppermute | solution.py:414
  13.3 12.0 %collective-permute-start.3 = (bf16[8,32,512]{2,1,0:T(8,128)(2,1)S(1)}, bf16[8,32,512]{2,1,0:T(8,128)(2,1)S(1)}, u32[]{:S(2)}, u32[]{:S(2)}) collective-permute-start(bf16[8,32,512]{2,1,0:T(8,128)(2,1)S(1)} %mix.2.after_ref), channel_id=1, source_target_pairs={{0,1},{2,3},{3,2},{4,6},{5,7},{8,9},{10,11},{11,10},{12,14},{13,15... | collective-permute-start | bytes 786440 | tf_op jit(solution)/shard_map/ppermute | solution.py:414

commit v8 on v2

--- a/solution.py
+++ b/solution.py
@@ -111,6 +111,7 @@
     table_ref,
     pick_ref,
     keep_ref,
+    rest_ref,
     x_ref,
     valid_ref,
     offsets_ref,
@@ -123,6 +124,7 @@
         pltpu.make_async_copy(valid_hbm, valid_ref, sems.at[0]),
         pltpu.make_async_copy(offsets_hbm, offsets_ref, sems.at[1]),
         pltpu.make_async_copy(x_hbm.at[pl.ds(0, span * wins)], x_ref, sems.at[2]),
+        pltpu.make_async_copy(x_hbm.at[pl.ds(span * wins, span * wins)], rest_ref, sems.at[3]),
     ]
     for copy in copies:
         copy.start()
@@ -145,6 +147,7 @@
     )
     copies[2].wait()
     whiten_block(x_ref[...], table_ref, keep_ref[:span], raw_ref, white_ref, short_ref)
+    copies[3].wait()
 
 
 def stack_pairs(pick_ref, white_ref, near_ref, parts_refs, out_ref):
@@ -208,12 +211,10 @@
     *parts_refs,
 ):
     wins, span, length = white_ref.shape
-    rows = slice(span * wins, 2 * span * wins)
 
     @pl.when(role(limits) == now)
     def _():
-        x = x_ref[rows, :]
-        whiten_block(x, table_ref, keep_ref[span:], raw_ref, white_ref, short_ref)
+        whiten_block(x_ref[...], table_ref, keep_ref[span:], raw_ref, white_ref, short_ref)
         near_ref[:span] = edge_ref[...]
         near_ref[span:] = short_ref[...]
         stack_pairs(pick_ref, head_ref, near_ref, parts_refs, out_ref)
@@ -335,7 +336,7 @@
     near_scratch = pltpu.VMEM((2 * span, wins * length), jnp.bfloat16)
     parts_scratch = [pltpu.VMEM((wins, pairs // 4 * span, length), jnp.float32)] * 4
 
-    white_a, short_a, table, pick, keep = pl.pallas_call(
+    white_a, short_a, table, pick, keep, rest = pl.pallas_call(
         head_kernel,
         out_shape=(
             white_type,
@@ -343,15 +344,16 @@
             jax.ShapeDtypeStruct((length, length), jnp.bfloat16),
             jax.ShapeDtypeStruct((pairs, span, 2 * span), jnp.bfloat16),
             jax.ShapeDtypeStruct((chans, wins * LANES), jnp.float32),
+            jax.ShapeDtypeStruct((span * wins, length), jnp.bfloat16),
         ),
         in_specs=[whole(pltpu.HBM)] * 3,
-        out_specs=(whole(),) * 5,
+        out_specs=(whole(),) * 6,
         scratch_shapes=[
             pltpu.VMEM((span * wins, length), jnp.bfloat16),
             pltpu.VMEM((wins, chans), jnp.int32),
             pltpu.SMEM((pairs,), jnp.int32),
             raw_scratch,
-            pltpu.SemaphoreType.DMA((3,)),
+            pltpu.SemaphoreType.DMA((4,)),
         ],
         compiler_params=params,
         cost_estimate=cost(span * wins * length * length * 2, 2 * 1024 * 1024),
@@ -375,7 +377,7 @@
             compiler_params=params,
             cost_estimate=cost(span * wins * length * length * 4, 4 * 1024 * 1024),
             name="tail",
-        )(flat, table, keep, pick, white_a, short_a, after)
+        )(rest, table, keep, pick, white_a, short_a, after)
 
     def cross(now, white, short, after):
         return pl.pallas_call(

time: 25.6 us -> 25.6 us (level)
  no operation moved by 1% of the time
where the time goes in v8:
time: 25.6 us; the launch traced here: 25.4 us
  starting transfers between devices  11.6 us (45%)
  waiting for transfers between devices  6.83 us (27%)
  Pallas kernels  6.81 us (27%)
    ppermute x5, starting transfers between devices, sent(): return lax.ppermute(value, ('chan', 'tm'), moves)  9.67 us
    ppermute x5, waiting for transfers between devices, sent(): return lax.ppermute(value, ('chan', 'tm'), moves)  4.3 us
    ppermute x1, waiting for transfers between devices, per_device(): edge = lax.ppermute(short_a, 'chan', [(i, i - 1) for i in range(1, ring)])  2.54 us
    pallas_call x2, Pallas kernels, written(): pl.pallas_call(kernel, out_shape=jax.ShapeDtypeStruct((pairs, chans, leng...  2.18 us
    ppermute x1, starting transfers between devices, per_device(): edge = lax.ppermute(short_a, 'chan', [(i, i - 1) for i in range(1, ring)])  1.92 us
    pallas_call x1, Pallas kernels, per_device(): pl.pallas_call(head_kernel, out_shape=(white_type, short_type, jax.ShapeD...  1.53 us
    pallas_call x3, Pallas kernels, tail(): pl.pallas_call(functools.partial(tail_kernel, limits, now), out_shape=(wh...  1.34 us
    pallas_call x3, Pallas kernels, cross(): pl.pallas_call(functools.partial(cross_kernel, limits, now), out_shape=lo...  0.79 us
  transfers between devices with their start and end apart: 6, of which 5 were waited for; matrix products, arithmetic and copies ran while one was open for 0% of the time, Pallas kernels for 17%

profile of v8, /device:TPU:28, one launch (start us, length us, event | category | flops | bytes accessed | tf_op | source)
XLA Modules:
  0.0 25.4 jit_solution(9005334432460213717)
XLA Ops:
  0.0 1.5 %head.1 = (f32[8,32,512]{2,1,0:T(8,128)S(1)}, bf16[32,4096]{1,0:T(8,128)(2,1)S(1)}, bf16[512,512]{1,0:T(8,128)(2,1)S(1)}, bf16[8,32,64]{2,1,0:T(8,128)(2,1)S(1)}...) custom-call(bf16[512,512]{1,0:T(8,128)(2,1)} %bitcast.3, s32[8,64]{1,0:T(8,128)} %bitcast.4, s32[8]{0:T(128)} %offsets_hbm.1), custom_call_target="tpu_custom_call" | custom-call | flops 134217728 | bytes 2097152 | tf_op jit(solution)/shard_map/head/pallas_call | solution.py:339
  1.5 1.9 %collective-permute-start = (bf16[32,4096]{1,0:T(8,128)(2,1)S(1)}, bf16[32,4096]{1,0:T(8,128)(2,1)S(1)}, u32[]{:S(2)}, u32[]{:S(2)}) collective-permute-start(bf16[32,4096]{1,0:T(8,128)(2,1)S(1)} %get-tuple-element.25.edge_ref), channel_id=1, source_target_pairs={{4,0},{8,4},{12,8},{16,12},{20,16},{24,20},{28,24},{5,1},{9,5},{13... | collective-permute-start | bytes 786440 | tf_op jit(solution)/shard_map/ppermute | solution.py:364
  3.5 1.3 %collective-permute-start.4 = (bf16[8,32,512]{2,1,0:T(8,128)(2,1)S(1)}, bf16[8,32,512]{2,1,0:T(8,128)(2,1)S(1)}, u32[]{:S(2)}, u32[]{:S(2)}) collective-permute-start(bf16[8,32,512]{2,1,0:T(8,128)(2,1)S(1)} %get-tuple-element.32.refs_0_.rest_0_), channel_id=1, source_target_pairs={{0,2},{1,3},{4,5},{5,4},{6,7},{8,10},{9,11},{12,13},{13,12},{14,15... | collective-permute-start | bytes 786440 | tf_op jit(solution)/shard_map/ppermute | solution.py:406
  4.8 2.5 %collective-permute-done.edge_ref = bf16[32,4096]{1,0:T(8,128)(2,1)S(1)} collective-permute-done((bf16[32,4096]{1,0:T(8,128)(2,1)S(1)}, bf16[32,4096]{1,0:T(8,128)(2,1)S(1)}, u32[]{:S(2)}, u32[]{:S(2)}) %collective-permute-start) | collective-permute-done | bytes 262176 | tf_op jit(solution)/shard_map/ppermute | solution.py:364
  7.3 1.3 %collective-permute-start.1 = (bf16[8,32,512]{2,1,0:T(8,128)(2,1)S(1)}, bf16[8,32,512]{2,1,0:T(8,128)(2,1)S(1)}, u32[]{:S(2)}, u32[]{:S(2)}) collective-permute-start(bf16[8,32,512]{2,1,0:T(8,128)(2,1)S(1)} %cross.3._.after_ref.refs_0_.refs_3_), channel_id=1, source_target_pairs={{0,2},{1,3},{4,5},{5,4},{8,10},{9,11},{12,13},{13,12},{16,18},{17,... | collective-permute-start | bytes 786440 | tf_op jit(solution)/shard_map/ppermute | solution.py:406
  8.6 0.7 %collective-permute-start.2 = (bf16[8,32,512]{2,1,0:T(8,128)(2,1)S(1)}, bf16[8,32,512]{2,1,0:T(8,128)(2,1)S(1)}, u32[]{:S(2)}, u32[]{:S(2)}) collective-permute-start(bf16[8,32,512]{2,1,0:T(8,128)(2,1)S(1)} %cross.3._.after_ref.refs_0_.refs_3_), channel_id=1, source_target_pairs={{6,7},{14,15},{22,23},{30,31}} | collective-permute-start | bytes 786440 | tf_op jit(solution)/shard_map/ppermute | solution.py:406
  9.3 1.3 %tail.4 = (f32[8,32,512]{2,1,0:T(8,128)S(1)}, bf16[32,4096]{1,0:T(8,128)(2,1)S(1)}, bf16[8,32,512]{2,1,0:T(8,128)(2,1)S(1)}) custom-call(bf16[256,512]{1,0:T(8,128)(2,1)S(1)} %get-tuple-element.21.x_ref, bf16[512,512]{1,0:T(8,128)(2,1)S(1)} %get-tuple-element.22.table_ref.after_ref, f32[64,1024]{1,0:T(8,128)S(1)} %get-tuple-element.23.keep_ref, ...), custom_call_target="tpu_custom_call" | custom-call | flops 268435456 | bytes 4194304 | tf_op jit(solution)/shard_map/tail/pallas_call | solution.py:371
  10.6 0.8 %cross.4.refs_1_.refs_3_ = bf16[8,32,512]{2,1,0:T(8,128)(2,1)S(1)} custom-call(bf16[8,32,64]{2,1,0:T(8,128)(2,1)S(1)} %get-tuple-element.20.pick_ref, f32[8,32,512]{2,1,0:T(8,128)S(1)} %get-tuple-element.28.white_ref, bf16[32,4096]{1,0:T(8,128)(2,1)S(1)} %get-tuple-element.29.short_ref, bf16[32,4096]{1,0:T(8,128)(2,1)S(1)} %collective-permute-done.edge_ref, ...), custom_call_target="tpu_custom_call" | custom-call | flops 4194304 | bytes 4194304 | tf_op jit(solution)/shard_map/cross/pallas_call | solution.py:383
  11.4 0.4 %collective-permute-done.4.refs_2_.rest_3_ = bf16[8,32,512]{2,1,0:T(8,128)(2,1)S(1)} collective-permute-done((bf16[8,32,512]{2,1,0:T(8,128)(2,1)S(1)}, bf16[8,32,512]{2,1,0:T(8,128)(2,1)S(1)}, u32[]{:S(2)}, u32[]{:S(2)}) %collective-permute-start.4) | collective-permute-done | bytes 262176 | tf_op jit(solution)/shard_map/ppermute | solution.py:406
  11.8 0.1 mix.3
  11.9 3.4 %collective-permute-start.5 = (bf16[8,32,512]{2,1,0:T(8,128)(2,1)S(1)}, bf16[8,32,512]{2,1,0:T(8,128)(2,1)S(1)}, u32[]{:S(2)}, u32[]{:S(2)}) collective-permute-start(bf16[8,32,512]{2,1,0:T(8,128)(2,1)S(1)} %mix.3), channel_id=1, source_target_pairs={{0,1},{2,3},{3,2},{4,6},{5,7},{8,9},{10,11},{11,10},{12,14},{13,15... | collective-permute-start | bytes 786440 | tf_op jit(solution)/shard_map/ppermute | solution.py:406
  15.3 0.7 %collective-permute-done.1.refs_2_.refs_3_ = bf16[8,32,512]{2,1,0:T(8,128)(2,1)S(1)} collective-permute-done((bf16[8,32,512]{2,1,0:T(8,128)(2,1)S(1)}, bf16[8,32,512]{2,1,0:T(8,128)(2,1)S(1)}, u32[]{:S(2)}, u32[]{:S(2)}) %collective-permute-start.1) | collective-permute-done | bytes 262176 | tf_op jit(solution)/shard_map/ppermute | solution.py:406
  16.0 0.1 mix.2.after_ref
  16.1 3.0 %collective-permute-start.3 = (bf16[8,32,512]{2,1,0:T(8,128)(2,1)S(1)}, bf16[8,32,512]{2,1,0:T(8,128)(2,1)S(1)}, u32[]{:S(2)}, u32[]{:S(2)}) collective-permute-start(bf16[8,32,512]{2,1,0:T(8,128)(2,1)S(1)} %mix.2.after_ref), channel_id=1, source_target_pairs={{0,1},{2,3},{3,2},{4,6},{5,7},{8,9},{10,11},{11,10},{12,14},{13,15... | collective-permute-start | bytes 786440 | tf_op jit(solution)/shard_map/ppermute | solution.py:406
  19.1 0.3 %inverse.1.table_ref = bf16[512,512]{1,0:T(8,128)(2,1)S(1)} custom-call(bf16[8,32,512]{2,1,0:T(8,128)(2,1)S(1)} %cross.3._.after_ref.refs_0_.refs_3_), custom_call_target="tpu_custom_call" | custom-call | flops 4194304 | bytes 524288 | tf_op jit(solution)/shard_map/inverse/pallas_call | solution.py:419
  19.5 0.0 collective-permute-done.2.refs_4_
  19.5 0.4 %part.1.rest_5_.part_ref = f32[256,512]{1,0:T(8,128)S(1)} custom-call(bf16[512,512]{1,0:T(8,128)(2,1)S(1)} %inverse.1.table_ref, bf16[8,32,512]{2,1,0:T(8,128)(2,1)S(1)} %cross.3._.after_ref.refs_0_.refs_3_, bf16[8,32,512]{2,1,0:T(8,128)(2,1)S(1)} %cross.4.refs_1_.refs_3_, bf16[8,32,512]{2,1,0:T(8,128)(2,1)S(1)} %cross.5.refs_2_, ...), custom_call_target="tpu_custom_call" | custom-call | flops 268435456 | bytes 1048576 | tf_op jit(solution)/shard_map/part/pallas_call | solution.py:446
  19.9 0.2 collective-permute-done.5.rest_4_
  20.2 1.2 %lags.2.rest_0_ = bf16[8,64,512]{2,1,0:T(8,128)(2,1)} custom-call(bf16[512,512]{1,0:T(8,128)(2,1)S(1)} %inverse.1.table_ref, bf16[8,32,512]{2,1,0:T(8,128)(2,1)S(1)} %get-tuple-element.32.refs_0_.rest_0_, bf16[8,32,512]{2,1,0:T(8,128)(2,1)S(1)} %get-tuple-element.33.refs_1_.rest_1_, bf16[8,32,512]{2,1,0:T(8,128)(2,1)S(1)} %get-tuple-element.34.rest_2_, ...), custom_call_target="tpu_custom_call" | custom-call | flops 268435456 | bytes 1048576 | tf_op jit(solution)/shard_map/lags/pallas_call | solution.py:430
  21.3 3.0 %collective-permute-done.3.more_ref = bf16[8,32,512]{2,1,0:T(8,128)(2,1)S(1)} collective-permute-done((bf16[8,32,512]{2,1,0:T(8,128)(2,1)S(1)}, bf16[8,32,512]{2,1,0:T(8,128)(2,1)S(1)}, u32[]{:S(2)}, u32[]{:S(2)}) %collective-permute-start.3) | collective-permute-done | bytes 262176 | tf_op jit(solution)/shard_map/ppermute | solution.py:406
  24.4 1.0 %lags.3 = bf16[8,64,512]{2,1,0:T(8,128)(2,1)} custom-call(bf16[512,512]{1,0:T(8,128)(2,1)S(1)} %inverse.1.table_ref, f32[256,512]{1,0:T(8,128)S(1)} %part.1.rest_5_.part_ref, bf16[8,32,512]{2,1,0:T(8,128)(2,1)S(1)} %collective-permute-done.3.more_ref, bf16[8,64,512]{2,1,0:T(8,128)(2,1)} %lags.2.rest_0_), custom_call_target="tpu_custom_call", output_to_operand_aliasing={{}: (3, {})} | custom-call | flops 268435456 | bytes 1048576 | tf_op jit(solution)/shard_map/lags/pallas_call | solution.py:430
  (4 shorter events, 0.1 us)
Async XLA Ops:
  1.5 5.8 %collective-permute-start = (bf16[32,4096]{1,0:T(8,128)(2,1)S(1)}, bf16[32,4096]{1,0:T(8,128)(2,1)S(1)}, u32[]{:S(2)}, u32[]{:S(2)}) collective-permute-start(bf16[32,4096]{1,0:T(8,128)(2,1)S(1)} %get-tuple-element.25.edge_ref), channel_id=1, source_target_pairs={{4,0},{8,4},{12,8},{16,12},{20,16},{24,20},{28,24},{5,1},{9,5},{13... | collective-permute-start | bytes 786440 | tf_op jit(solution)/shard_map/ppermute | solution.py:364
  3.5 8.3 %collective-permute-start.4 = (bf16[8,32,512]{2,1,0:T(8,128)(2,1)S(1)}, bf16[8,32,512]{2,1,0:T(8,128)(2,1)S(1)}, u32[]{:S(2)}, u32[]{:S(2)}) collective-permute-start(bf16[8,32,512]{2,1,0:T(8,128)(2,1)S(1)} %get-tuple-element.32.refs_0_.rest_0_), channel_id=1, source_target_pairs={{0,2},{1,3},{4,5},{5,4},{6,7},{8,10},{9,11},{12,13},{13,12},{14,15... | collective-permute-start | bytes 786440 | tf_op jit(solution)/shard_map/ppermute | solution.py:406
  7.3 8.6 %collective-permute-start.1 = (bf16[8,32,512]{2,1,0:T(8,128)(2,1)S(1)}, bf16[8,32,512]{2,1,0:T(8,128)(2,1)S(1)}, u32[]{:S(2)}, u32[]{:S(2)}) collective-permute-start(bf16[8,32,512]{2,1,0:T(8,128)(2,1)S(1)} %cross.3._.after_ref.refs_0_.refs_3_), channel_id=1, source_target_pairs={{0,2},{1,3},{4,5},{5,4},{8,10},{9,11},{12,13},{13,12},{16,18},{17,... | collective-permute-start | bytes 786440 | tf_op jit(solution)/shard_map/ppermute | solution.py:406
  8.6 10.9 %collective-permute-start.2 = (bf16[8,32,512]{2,1,0:T(8,128)(2,1)S(1)}, bf16[8,32,512]{2,1,0:T(8,128)(2,1)S(1)}, u32[]{:S(2)}, u32[]{:S(2)}) collective-permute-start(bf16[8,32,512]{2,1,0:T(8,128)(2,1)S(1)} %cross.3._.after_ref.refs_0_.refs_3_), channel_id=1, source_target_pairs={{6,7},{14,15},{22,23},{30,31}} | collective-permute-start | bytes 786440 | tf_op jit(solution)/shard_map/ppermute | solution.py:406
  11.9 8.3 %collective-permute-start.5 = (bf16[8,32,512]{2,1,0:T(8,128)(2,1)S(1)}, bf16[8,32,512]{2,1,0:T(8,128)(2,1)S(1)}, u32[]{:S(2)}, u32[]{:S(2)}) collective-permute-start(bf16[8,32,512]{2,1,0:T(8,128)(2,1)S(1)} %mix.3), channel_id=1, source_target_pairs={{0,1},{2,3},{3,2},{4,6},{5,7},{8,9},{10,11},{11,10},{12,14},{13,15... | collective-permute-start | bytes 786440 | tf_op jit(solution)/shard_map/ppermute | solution.py:406
  16.1 8.3 %collective-permute-start.3 = (bf16[8,32,512]{2,1,0:T(8,128)(2,1)S(1)}, bf16[8,32,512]{2,1,0:T(8,128)(2,1)S(1)}, u32[]{:S(2)}, u32[]{:S(2)}) collective-permute-start(bf16[8,32,512]{2,1,0:T(8,128)(2,1)S(1)} %mix.2.after_ref), channel_id=1, source_target_pairs={{0,1},{2,3},{3,2},{4,6},{5,7},{8,9},{10,11},{11,10},{12,14},{13,15... | collective-permute-start | bytes 786440 | tf_op jit(solution)/shard_map/ppermute | solution.py:406

commit v9 on v2

--- a/solution.py
+++ b/solution.py
@@ -185,7 +185,7 @@
 
 
 def role(limits):
-    odd = lax.rem(lax.axis_index("chan"), 2)
+    odd = lax.rem(lax.axis_index("chan") + 1, 2)
     first = lax.axis_index("tm") < jnp.where(odd == 0, *limits)
     return jnp.where(first, 0, 1 + odd)
 
@@ -254,7 +254,7 @@
 
 
 def whereabouts(groups):
-    return lax.rem(lax.axis_index("chan"), 2) * groups + lax.axis_index("tm")
+    return lax.rem(lax.axis_index("chan") + 1, 2) * groups + lax.axis_index("tm")
 
 
 def mix_kernel(limits, weights, *refs):
@@ -399,7 +399,7 @@
         moves = [
             (c * groups + here, c * groups + there)
             for c in range(ring)
-            for here, there in (odd if c % 2 else even)
+            for here, there in (even if c % 2 else odd)
         ]
         return lax.ppermute(value, ("chan", "tm"), moves)
 

time: 25.6 us -> 25.9 us (1.012)
  the two profiles are of different devices: /device:TPU:28 before, /device:TPU:5 now
where the time goes in v9:
time: 25.9 us; the launch traced here: 25.7 us
  starting transfers between devices  11.7 us (45%)
  waiting for transfers between devices  6.99 us (27%)
  Pallas kernels  6.83 us (26%)
    ppermute x5, starting transfers between devices, sent(): return lax.ppermute(value, ('chan', 'tm'), moves)  9.12 us
    ppermute x1, waiting for transfers between devices, per_device(): edge = lax.ppermute(short_a, 'chan', [(i, i - 1) for i in range(1, ring)])  3.88 us
    ppermute x5, waiting for transfers between devices, sent(): return lax.ppermute(value, ('chan', 'tm'), moves)  3.11 us
    ppermute x1, starting transfers between devices, per_device(): edge = lax.ppermute(short_a, 'chan', [(i, i - 1) for i in range(1, ring)])  2.58 us
    pallas_call x2, Pallas kernels, written(): pl.pallas_call(kernel, out_shape=jax.ShapeDtypeStruct((pairs, chans, leng...  2.18 us
    pallas_call x1, Pallas kernels, per_device(): pl.pallas_call(head_kernel, out_shape=(white_type, short_type, jax.ShapeD...  1.54 us
    pallas_call x3, Pallas kernels, tail(): pl.pallas_call(functools.partial(tail_kernel, limits, now), out_shape=(wh...  1.34 us
    pallas_call x3, Pallas kernels, cross(): pl.pallas_call(functools.partial(cross_kernel, limits, now), out_shape=lo...  0.79 us
  transfers between devices with their start and end apart: 6, of which 4 were waited for; matrix products, arithmetic and copies ran while one was open for 0% of the time, Pallas kernels for 17%

profile of v9, /device:TPU:5, one launch (start us, length us, event | category | flops | bytes accessed | tf_op | source)
XLA Modules:
  0.0 25.7 jit_solution(5349185869099147136)
XLA Ops:
  0.0 0.0 copy-start
  0.0 1.5 %head.1 = (f32[8,32,512]{2,1,0:T(8,128)S(1)}, bf16[32,4096]{1,0:T(8,128)(2,1)S(1)}, bf16[512,512]{1,0:T(8,128)(2,1)S(1)}, bf16[8,32,64]{2,1,0:T(8,128)(2,1)S(1)}, f32[64,1024]{1,0:T(8,128)S(1)}) custom-call(bf16[512,512]{1,0:T(8,128)(2,1)} %bitcast.3, s32[8,64]{1,0:T(8,128)} %bitcast.7, s32[8]{0:T(128)} %offsets_hbm.1), custom_call_target="tpu_custom_call" | custom-call | flops 134217728 | bytes 2097152 | tf_op jit(solution)/shard_map/head/pallas_call | solution.py:338
  1.5 2.6 %collective-permute-start = (bf16[32,4096]{1,0:T(8,128)(2,1)S(1)}, bf16[32,4096]{1,0:T(8,128)(2,1)S(1)}, u32[]{:S(2)}, u32[]{:S(2)}) collective-permute-start(bf16[32,4096]{1,0:T(8,128)(2,1)S(1)} %get-tuple-element.23.edge_ref), channel_id=1, source_target_pairs={{4,0},{8,4},{12,8},{16,12},{20,16},{24,20},{28,24},{5,1},{9,5},{13... | collective-permute-start | bytes 786440 | tf_op jit(solution)/shard_map/ppermute | solution.py:362
  4.1 0.0 copy-done
  4.2 1.3 %collective-permute-start.4 = (bf16[8,32,512]{2,1,0:T(8,128)(2,1)S(1)}, bf16[8,32,512]{2,1,0:T(8,128)(2,1)S(1)}, u32[]{:S(2)}, u32[]{:S(2)}) collective-permute-start(bf16[8,32,512]{2,1,0:T(8,128)(2,1)S(1)} %get-tuple-element.30.refs_0_.rest_0_), channel_id=1, source_target_pairs={{0,1},{1,0},{2,3},{4,6},{5,7},{8,9},{9,8},{10,11},{12,14},{13,15},... | collective-permute-start | bytes 786440 | tf_op jit(solution)/shard_map/ppermute | solution.py:404
  5.5 3.9 %collective-permute-done.edge_ref = bf16[32,4096]{1,0:T(8,128)(2,1)S(1)} collective-permute-done((bf16[32,4096]{1,0:T(8,128)(2,1)S(1)}, bf16[32,4096]{1,0:T(8,128)(2,1)S(1)}, u32[]{:S(2)}, u32[]{:S(2)}) %collective-permute-start) | collective-permute-done | bytes 262176 | tf_op jit(solution)/shard_map/ppermute | solution.py:362
  9.4 1.3 %collective-permute-start.1 = (bf16[8,32,512]{2,1,0:T(8,128)(2,1)S(1)}, bf16[8,32,512]{2,1,0:T(8,128)(2,1)S(1)}, u32[]{:S(2)}, u32[]{:S(2)}) collective-permute-start(bf16[8,32,512]{2,1,0:T(8,128)(2,1)S(1)} %cross.3._.after_ref.refs_0_.refs_3_), channel_id=1, source_target_pairs={{0,1},{1,0},{4,6},{5,7},{8,9},{9,8},{12,14},{13,15},{16,17},{17,16... | collective-permute-start | bytes 786440 | tf_op jit(solution)/shard_map/ppermute | solution.py:404
  10.7 0.7 %collective-permute-start.2 = (bf16[8,32,512]{2,1,0:T(8,128)(2,1)S(1)}, bf16[8,32,512]{2,1,0:T(8,128)(2,1)S(1)}, u32[]{:S(2)}, u32[]{:S(2)}) collective-permute-start(bf16[8,32,512]{2,1,0:T(8,128)(2,1)S(1)} %cross.3._.after_ref.refs_0_.refs_3_), channel_id=1, source_target_pairs={{2,3},{10,11},{18,19},{26,27}} | collective-permute-start | bytes 786440 | tf_op jit(solution)/shard_map/ppermute | solution.py:404
  11.3 1.3 %tail.4 = (f32[8,32,512]{2,1,0:T(8,128)S(1)}, bf16[32,4096]{1,0:T(8,128)(2,1)S(1)}, bf16[8,32,512]{2,1,0:T(8,128)(2,1)S(1)}) custom-call(bf16[512,512]{1,0:T(8,128)(2,1)S(1)} %bitcast.5, bf16[512,512]{1,0:T(8,128)(2,1)S(1)} %get-tuple-element.20.table_ref.after_ref, f32[64,1024]{1,0:T(8,128)S(1)} %get-tuple-element.21.keep_ref, ...), custom_call_target="tpu_custom_call" | custom-call | flops 268435456 | bytes 4194304 | tf_op jit(solution)/shard_map/tail/pallas_call | solution.py:369
  12.6 0.8 %cross.4.refs_1_.refs_3_ = bf16[8,32,512]{2,1,0:T(8,128)(2,1)S(1)} custom-call(bf16[8,32,64]{2,1,0:T(8,128)(2,1)S(1)} %get-tuple-element.19.pick_ref, f32[8,32,512]{2,1,0:T(8,128)S(1)} %get-tuple-element.26.white_ref, bf16[32,4096]{1,0:T(8,128)(2,1)S(1)} %get-tuple-element.27.short_ref, bf16[32,4096]{1,0:T(8,128)(2,1)S(1)} %collective-permute-done.edge_ref, ...), custom_call_target="tpu_custom_call" | custom-call | flops 4194304 | bytes 4194304 | tf_op jit(solution)/shard_map/cross/pallas_call | solution.py:381
  13.4 0.0 collective-permute-done.4.refs_2_.rest_3_
  13.4 0.1 mix.3
  13.6 3.4 %collective-permute-start.5 = (bf16[8,32,512]{2,1,0:T(8,128)(2,1)S(1)}, bf16[8,32,512]{2,1,0:T(8,128)(2,1)S(1)}, u32[]{:S(2)}, u32[]{:S(2)}) collective-permute-start(bf16[8,32,512]{2,1,0:T(8,128)(2,1)S(1)} %mix.3), channel_id=1, source_target_pairs={{0,2},{1,3},{4,5},{6,7},{7,6},{8,10},{9,11},{12,13},{14,15},{15,14... | collective-permute-start | bytes 786440 | tf_op jit(solution)/shard_map/ppermute | solution.py:404
  17.0 0.4 %collective-permute-done.1.refs_2_.refs_3_ = bf16[8,32,512]{2,1,0:T(8,128)(2,1)S(1)} collective-permute-done((bf16[8,32,512]{2,1,0:T(8,128)(2,1)S(1)}, bf16[8,32,512]{2,1,0:T(8,128)(2,1)S(1)}, u32[]{:S(2)}, u32[]{:S(2)}) %collective-permute-start.1) | collective-permute-done | bytes 262176 | tf_op jit(solution)/shard_map/ppermute | solution.py:404
  17.4 0.1 mix.2.after_ref
  17.6 2.5 %collective-permute-start.3 = (bf16[8,32,512]{2,1,0:T(8,128)(2,1)S(1)}, bf16[8,32,512]{2,1,0:T(8,128)(2,1)S(1)}, u32[]{:S(2)}, u32[]{:S(2)}) collective-permute-start(bf16[8,32,512]{2,1,0:T(8,128)(2,1)S(1)} %mix.2.after_ref), channel_id=1, source_target_pairs={{0,2},{1,3},{4,5},{6,7},{7,6},{8,10},{9,11},{12,13},{14,15},{15,14... | collective-permute-start | bytes 786440 | tf_op jit(solution)/shard_map/ppermute | solution.py:404
  20.0 0.3 %inverse.1.table_ref = bf16[512,512]{1,0:T(8,128)(2,1)S(1)} custom-call(bf16[8,32,512]{2,1,0:T(8,128)(2,1)S(1)} %cross.3._.after_ref.refs_0_.refs_3_), custom_call_target="tpu_custom_call" | custom-call | flops 4194304 | bytes 524288 | tf_op jit(solution)/shard_map/inverse/pallas_call | solution.py:417
  20.4 0.0 collective-permute-done.2.refs_4_
  20.4 0.4 %part.1.rest_5_.part_ref = f32[256,512]{1,0:T(8,128)S(1)} custom-call(bf16[512,512]{1,0:T(8,128)(2,1)S(1)} %inverse.1.table_ref, bf16[8,32,512]{2,1,0:T(8,128)(2,1)S(1)} %cross.3._.after_ref.refs_0_.refs_3_, bf16[8,32,512]{2,1,0:T(8,128)(2,1)S(1)} %cross.4.refs_1_.refs_3_, bf16[8,32,512]{2,1,0:T(8,128)(2,1)S(1)} %cross.5.refs_2_, ...), custom_call_target="tpu_custom_call" | custom-call | flops 268435456 | bytes 1048576 | tf_op jit(solution)/shard_map/part/pallas_call | solution.py:444
  20.8 0.2 collective-permute-done.5.rest_4_
  21.0 1.2 %lags.2.rest_0_ = bf16[8,64,512]{2,1,0:T(8,128)(2,1)} custom-call(bf16[512,512]{1,0:T(8,128)(2,1)S(1)} %inverse.1.table_ref, bf16[8,32,512]{2,1,0:T(8,128)(2,1)S(1)} %get-tuple-element.30.refs_0_.rest_0_, bf16[8,32,512]{2,1,0:T(8,128)(2,1)S(1)} %get-tuple-element.31.refs_1_.rest_1_, bf16[8,32,512]{2,1,0:T(8,128)(2,1)S(1)} %get-tuple-element.32.rest_2_, ...), custom_call_target="tpu_custom_call" | custom-call | flops 268435456 | bytes 1048576 | tf_op jit(solution)/shard_map/lags/pallas_call | solution.py:428
  22.2 2.5 %collective-permute-done.3.more_ref = bf16[8,32,512]{2,1,0:T(8,128)(2,1)S(1)} collective-permute-done((bf16[8,32,512]{2,1,0:T(8,128)(2,1)S(1)}, bf16[8,32,512]{2,1,0:T(8,128)(2,1)S(1)}, u32[]{:S(2)}, u32[]{:S(2)}) %collective-permute-start.3) | collective-permute-done | bytes 262176 | tf_op jit(solution)/shard_map/ppermute | solution.py:404
  24.7 1.0 %lags.3 = bf16[8,64,512]{2,1,0:T(8,128)(2,1)} custom-call(bf16[512,512]{1,0:T(8,128)(2,1)S(1)} %inverse.1.table_ref, f32[256,512]{1,0:T(8,128)S(1)} %part.1.rest_5_.part_ref, bf16[8,32,512]{2,1,0:T(8,128)(2,1)S(1)} %collective-permute-done.3.more_ref, bf16[8,64,512]{2,1,0:T(8,128)(2,1)} %lags.2.rest_0_), custom_call_target="tpu_custom_call", output_to_operand_aliasing={{}: (3, {})} | custom-call | flops 268435456 | bytes 1048576 | tf_op jit(solution)/shard_map/lags/pallas_call | solution.py:428
  (4 shorter events, 0.1 us)
Async XLA Ops:
  0.0 4.1 %copy-start = (bf16[64,8,512]{2,1,0:T(8,128)(2,1)S(1)}, bf16[64,8,512]{2,1,0:T(8,128)(2,1)}, u32[]{:S(2)}) copy-start(bf16[64,8,512]{2,1,0:T(8,128)(2,1)} %param.3) | copy-start | bytes 1572868
  1.5 7.8 %collective-permute-start = (bf16[32,4096]{1,0:T(8,128)(2,1)S(1)}, bf16[32,4096]{1,0:T(8,128)(2,1)S(1)}, u32[]{:S(2)}, u32[]{:S(2)}) collective-permute-start(bf16[32,4096]{1,0:T(8,128)(2,1)S(1)} %get-tuple-element.23.edge_ref), channel_id=1, source_target_pairs={{4,0},{8,4},{12,8},{16,12},{20,16},{24,20},{28,24},{5,1},{9,5},{13... | collective-permute-start | bytes 786440 | tf_op jit(solution)/shard_map/ppermute | solution.py:362
  4.2 9.2 %collective-permute-start.4 = (bf16[8,32,512]{2,1,0:T(8,128)(2,1)S(1)}, bf16[8,32,512]{2,1,0:T(8,128)(2,1)S(1)}, u32[]{:S(2)}, u32[]{:S(2)}) collective-permute-start(bf16[8,32,512]{2,1,0:T(8,128)(2,1)S(1)} %get-tuple-element.30.refs_0_.rest_0_), channel_id=1, source_target_pairs={{0,1},{1,0},{2,3},{4,6},{5,7},{8,9},{9,8},{10,11},{12,14},{13,15},... | collective-permute-start | bytes 786440 | tf_op jit(solution)/shard_map/ppermute | solution.py:404
  9.4 8.1 %collective-permute-start.1 = (bf16[8,32,512]{2,1,0:T(8,128)(2,1)S(1)}, bf16[8,32,512]{2,1,0:T(8,128)(2,1)S(1)}, u32[]{:S(2)}, u32[]{:S(2)}) collective-permute-start(bf16[8,32,512]{2,1,0:T(8,128)(2,1)S(1)} %cross.3._.after_ref.refs_0_.refs_3_), channel_id=1, source_target_pairs={{0,1},{1,0},{4,6},{5,7},{8,9},{9,8},{12,14},{13,15},{16,17},{17,16... | collective-permute-start | bytes 786440 | tf_op jit(solution)/shard_map/ppermute | solution.py:404
  10.7 9.7 %collective-permute-start.2 = (bf16[8,32,512]{2,1,0:T(8,128)(2,1)S(1)}, bf16[8,32,512]{2,1,0:T(8,128)(2,1)S(1)}, u32[]{:S(2)}, u32[]{:S(2)}) collective-permute-start(bf16[8,32,512]{2,1,0:T(8,128)(2,1)S(1)} %cross.3._.after_ref.refs_0_.refs_3_), channel_id=1, source_target_pairs={{2,3},{10,11},{18,19},{26,27}} | collective-permute-start | bytes 786440 | tf_op jit(solution)/shard_map/ppermute | solution.py:404
  13.6 7.5 %collective-permute-start.5 = (bf16[8,32,512]{2,1,0:T(8,128)(2,1)S(1)}, bf16[8,32,512]{2,1,0:T(8,128)(2,1)S(1)}, u32[]{:S(2)}, u32[]{:S(2)}) collective-permute-start(bf16[8,32,512]{2,1,0:T(8,128)(2,1)S(1)} %mix.3), channel_id=1, source_target_pairs={{0,2},{1,3},{4,5},{6,7},{7,6},{8,10},{9,11},{12,13},{14,15},{15,14... | collective-permute-start | bytes 786440 | tf_op jit(solution)/shard_map/ppermute | solution.py:404
  17.6 7.1 %collective-permute-start.3 = (bf16[8,32,512]{2,1,0:T(8,128)(2,1)S(1)}, bf16[8,32,512]{2,1,0:T(8,128)(2,1)S(1)}, u32[]{:S(2)}, u32[]{:S(2)}) collective-permute-start(bf16[8,32,512]{2,1,0:T(8,128)(2,1)S(1)} %mix.2.after_ref), channel_id=1, source_target_pairs={{0,2},{1,3},{4,5},{6,7},{7,6},{8,10},{9,11},{12,13},{14,15},{15,14... | collective-permute-start | bytes 786440 | tf_op jit(solution)/shard_map/ppermute | solution.py:404

commit v10 on v9

--- a/solution.py
+++ b/solution.py
@@ -359,11 +359,23 @@
     )(in_hbm(flat), in_hbm(valid.T), in_hbm(offsets))
 
     ring = lax.axis_size("chan")
-    edge = lax.ppermute(short_a, "chan", [(i, i - 1) for i in range(1, ring)])
+
+    def to_previous(odd, even):
+        moves = [
+            (c * groups + h, (c - 1) * groups + h)
+            for c in range(1, ring)
+            for h in (odd if c % 2 else even)
+        ]
+        return lax.ppermute(short_a, ("chan", "tm"), moves)
+
 
     columns = min(d for d in range(1, groups + 1) if groups % d == 0 and d * d >= groups)
     square = columns == 2 and groups == columns * columns
     limits = (2, 3) if square else (groups, groups)
+
+    ahead = 2 if square else groups
+    edge = to_previous(range(groups), range(ahead))
+    edge_late = to_previous([], range(ahead, groups)) if square else edge
 
     def tail(now, after):
         return pl.pallas_call(
@@ -377,7 +389,7 @@
             name="tail",
         )(flat, table, keep, pick, white_a, short_a, after)
 
-    def cross(now, white, short, after):
+    def cross(now, white, short, edge, after):
         return pl.pallas_call(
             functools.partial(cross_kernel, limits, now),
             out_shape=local_type,
@@ -390,9 +402,9 @@
         )(pick, white, short, edge, after)
 
     white_b, short_b, local_a = tail(0, table)
-    local_b = cross(0, white_b, short_b, table)
-    white_late, short_late, late_a = tail(1, local_b)
-    late_b = cross(1, white_late, short_late, local_b)
+    white_late, short_late, late_a = tail(1, local_a)
+    local_b = cross(0, white_b, short_b, edge, late_a)
+    late_b = cross(1, white_late, short_late, edge_late, local_b)
 
     power = [float(np.float32(factor) ** np.float32(d)) for d in range(groups)]
     def sent(value, even, odd):
@@ -481,10 +493,10 @@
 
     spread = two_hops if square else one_hop
     scale = bins**-0.5
-    _, terms_a, weights_a = spread(local_a, late_a, late_b, False)
+    _, terms_a, weights_a = spread(local_a, late_a, local_b, False)
     ahead, terms_b, weights_b = spread(local_b, late_b, local_b, True)
     white_last, short_last, last_a = tail(2, ahead)
-    last_b = cross(2, white_last, short_last, ahead)
+    last_b = cross(2, white_last, short_last, edge, ahead)
     terms_a = [local_a, late_a, last_a] + terms_a
     terms_b = [local_b, late_b, last_b] + terms_b
     before = part(terms_b[:-1], weights_b[:-1])

time: 25.9 us -> 26.8 us (1.035)
  the two profiles are of different devices: /device:TPU:5 before, /device:TPU:14 now
where the time goes in v10:
time: 26.8 us; the launch traced here: 26.5 us
  starting transfers between devices  10.2 us (38%)
  waiting for transfers between devices  9.19 us (34%)
  Pallas kernels  6.87 us (26%)
    ppermute x5, waiting for transfers between devices, sent(): return lax.ppermute(value, ('chan', 'tm'), moves)  9.18 us
    ppermute x5, starting transfers between devices, sent(): return lax.ppermute(value, ('chan', 'tm'), moves)  5.85 us
    ppermute x2, starting transfers between devices, to_previous(): return lax.ppermute(short_a, ('chan', 'tm'), moves)  4.4 us
    pallas_call x2, Pallas kernels, written(): pl.pallas_call(kernel, out_shape=jax.ShapeDtypeStruct((pairs, chans, leng...  2.18 us
    pallas_call x1, Pallas kernels, per_device(): pl.pallas_call(head_kernel, out_shape=(white_type, short_type, jax.ShapeD...  1.54 us
    pallas_call x3, Pallas kernels, tail(): pl.pallas_call(functools.partial(tail_kernel, limits, now), out_shape=(wh...  1.34 us
    pallas_call x3, Pallas kernels, cross(): pl.pallas_call(functools.partial(cross_kernel, limits, now), out_shape=lo...  0.83 us
  transfers between devices with their start and end apart: 7, of which 3 were waited for; matrix products, arithmetic and copies ran while one was open for 0% of the time, Pallas kernels for 16%

profile of v10, /device:TPU:14, one launch (start us, length us, event | category | flops | bytes accessed | tf_op | source)
XLA Modules:
  0.0 26.5 jit_solution(5498290488662688501)
XLA Ops:
  0.0 0.0 copy-start
  0.0 1.5 %head.1 = (f32[8,32,512]{2,1,0:T(8,128)S(1)}, bf16[32,4096]{1,0:T(8,128)(2,1)S(1)}, bf16[512,512]{1,0:T(8,128)(2,1)S(1)}, bf16[8,32,64]{2,1,0:T(8,128)(2,1)S(1)}, f32[64,1024]{1,0:T(8,128)S(1)}) custom-call(bf16[512,512]{1,0:T(8,128)(2,1)} %bitcast.3, s32[8,64]{1,0:T(8,128)} %bitcast.7, s32[8]{0:T(128)} %offsets_hbm.1), custom_call_target="tpu_custom_call" | custom-call | flops 134217728 | bytes 2097152 | tf_op jit(solution)/shard_map/head/pallas_call | solution.py:338
  1.6 1.3 %collective-permute-start = (bf16[32,4096]{1,0:T(8,128)(2,1)S(1)}, bf16[32,4096]{1,0:T(8,128)(2,1)S(1)}, u32[]{:S(2)}, u32[]{:S(2)}) collective-permute-start(bf16[32,4096]{1,0:T(8,128)(2,1)S(1)} %get-tuple-element.23.edge_ref), channel_id=1, source_target_pairs={{4,0},{5,1},{6,2},{7,3},{8,4},{9,5},{12,8},{13,9},{14,10},{15,11},... | collective-permute-start | bytes 786440 | tf_op jit(solution)/shard_map/ppermute | solution.py:369
  2.9 3.1 %collective-permute-start.1 = (bf16[32,4096]{1,0:T(8,128)(2,1)S(1)}, bf16[32,4096]{1,0:T(8,128)(2,1)S(1)}, u32[]{:S(2)}, u32[]{:S(2)}) collective-permute-start(bf16[32,4096]{1,0:T(8,128)(2,1)S(1)} %get-tuple-element.23.edge_ref), channel_id=1, source_target_pairs={{10,6},{11,7},{18,14},{19,15},{26,22},{27,23}} | collective-permute-start | bytes 786440 | tf_op jit(solution)/shard_map/ppermute | solution.py:369
  6.0 0.0 copy-done
  6.0 1.3 %collective-permute-start.5 = (bf16[8,32,512]{2,1,0:T(8,128)(2,1)S(1)}, bf16[8,32,512]{2,1,0:T(8,128)(2,1)S(1)}, u32[]{:S(2)}, u32[]{:S(2)}) collective-permute-start(bf16[8,32,512]{2,1,0:T(8,128)(2,1)S(1)} %get-tuple-element.26.after_ref.refs_0_.rest_0_), channel_id=1, source_target_pairs={{0,1},{1,0},{2,3},{4,6},{5,7},{8,9},{9,8},{10,11},{12,14},{13,15},... | collective-permute-start | bytes 786440 | tf_op jit(solution)/shard_map/ppermute | solution.py:416
  7.3 0.0 collective-permute-done.edge_ref
  7.4 0.7 %collective-permute-start.2 = (bf16[8,32,512]{2,1,0:T(8,128)(2,1)S(1)}, bf16[8,32,512]{2,1,0:T(8,128)(2,1)S(1)}, u32[]{:S(2)}, u32[]{:S(2)}) collective-permute-start(bf16[8,32,512]{2,1,0:T(8,128)(2,1)S(1)} %cross.3._.after_ref.refs_0_.refs_3_), channel_id=1, source_target_pairs={{0,1},{1,0},{4,6},{5,7},{8,9},{9,8},{12,14},{13,15},{16,17},{17,16... | collective-permute-start | bytes 786440 | tf_op jit(solution)/shard_map/ppermute | solution.py:416
  8.1 1.3 %collective-permute-start.3 = (bf16[8,32,512]{2,1,0:T(8,128)(2,1)S(1)}, bf16[8,32,512]{2,1,0:T(8,128)(2,1)S(1)}, u32[]{:S(2)}, u32[]{:S(2)}) collective-permute-start(bf16[8,32,512]{2,1,0:T(8,128)(2,1)S(1)} %cross.3._.after_ref.refs_0_.refs_3_), channel_id=1, source_target_pairs={{2,3},{10,11},{18,19},{26,27}} | collective-permute-start | bytes 786440 | tf_op jit(solution)/shard_map/ppermute | solution.py:416
  9.4 4.9 %collective-permute-done.5.refs_2_.rest_3_ = bf16[8,32,512]{2,1,0:T(8,128)(2,1)S(1)} collective-permute-done((bf16[8,32,512]{2,1,0:T(8,128)(2,1)S(1)}, bf16[8,32,512]{2,1,0:T(8,128)(2,1)S(1)}, u32[]{:S(2)}, u32[]{:S(2)}) %collective-permute-start.5) | collective-permute-done | bytes 262176 | tf_op jit(solution)/shard_map/ppermute | solution.py:416
  14.3 0.1 mix.3
  14.4 1.3 %collective-permute-start.6 = (bf16[8,32,512]{2,1,0:T(8,128)(2,1)S(1)}, bf16[8,32,512]{2,1,0:T(8,128)(2,1)S(1)}, u32[]{:S(2)}, u32[]{:S(2)}) collective-permute-start(bf16[8,32,512]{2,1,0:T(8,128)(2,1)S(1)} %mix.3), channel_id=1, source_target_pairs={{0,2},{1,3},{4,5},{6,7},{7,6},{8,10},{9,11},{12,13},{14,15},{15,14... | collective-permute-start | bytes 786440 | tf_op jit(solution)/shard_map/ppermute | solution.py:416
  15.7 0.0 collective-permute-done.1.edge_ref
  15.7 0.0 collective-permute-done.2.refs_2_.refs_3_
  15.8 0.1 mix.2.after_ref
  15.9 1.3 %collective-permute-start.4 = (bf16[8,32,512]{2,1,0:T(8,128)(2,1)S(1)}, bf16[8,32,512]{2,1,0:T(8,128)(2,1)S(1)}, u32[]{:S(2)}, u32[]{:S(2)}) collective-permute-start(bf16[8,32,512]{2,1,0:T(8,128)(2,1)S(1)} %mix.2.after_ref), channel_id=1, source_target_pairs={{0,2},{1,3},{4,5},{6,7},{7,6},{8,10},{9,11},{12,13},{14,15},{15,14... | collective-permute-start | bytes 786440 | tf_op jit(solution)/shard_map/ppermute | solution.py:416
  17.2 0.3 %inverse.1.table_ref = bf16[512,512]{1,0:T(8,128)(2,1)S(1)} custom-call(bf16[8,32,512]{2,1,0:T(8,128)(2,1)S(1)} %cross.3._.after_ref.refs_0_.refs_3_), custom_call_target="tpu_custom_call" | custom-call | flops 4194304 | bytes 524288 | tf_op jit(solution)/shard_map/inverse/pallas_call | solution.py:429
  17.5 1.3 %tail.5 = (f32[8,32,512]{2,1,0:T(8,128)S(1)}, bf16[32,4096]{1,0:T(8,128)(2,1)S(1)}, bf16[8,32,512]{2,1,0:T(8,128)(2,1)S(1)}) custom-call(bf16[512,512]{1,0:T(8,128)(2,1)S(1)} %bitcast.6, bf16[512,512]{1,0:T(8,128)(2,1)S(1)} %get-tuple-element.20.table_ref.after_ref, f32[64,1024]{1,0:T(8,128)S(1)} %get-tuple-element.21.keep_ref, ...), custom_call_target="tpu_custom_call" | custom-call | flops 268435456 | bytes 4194304 | tf_op jit(solution)/shard_map/tail/pallas_call | solution.py:381
  18.8 0.8 %cross.5.refs_2_ = bf16[8,32,512]{2,1,0:T(8,128)(2,1)S(1)} custom-call(bf16[8,32,64]{2,1,0:T(8,128)(2,1)S(1)} %get-tuple-element.19.pick_ref, f32[8,32,512]{2,1,0:T(8,128)S(1)} %get-tuple-element.30.white_ref, bf16[32,4096]{1,0:T(8,128)(2,1)S(1)} %get-tuple-element.31.short_ref, bf16[32,4096]{1,0:T(8,128)(2,1)S(1)} %collective-permute-done.edge_ref, ...), custom_call_target="tpu_custom_call" | custom-call | flops 4194304 | bytes 4194304 | tf_op jit(solution)/shard_map/cross/pallas_call | solution.py:393
  19.6 0.0 collective-permute-done.3.refs_4_
  19.6 0.4 %part.1.rest_5_.part_ref = f32[256,512]{1,0:T(8,128)S(1)} custom-call(bf16[512,512]{1,0:T(8,128)(2,1)S(1)} %inverse.1.table_ref, bf16[8,32,512]{2,1,0:T(8,128)(2,1)S(1)} %cross.3._.after_ref.refs_0_.refs_3_, bf16[8,32,512]{2,1,0:T(8,128)(2,1)S(1)} %cross.4.refs_1_, bf16[8,32,512]{2,1,0:T(8,128)(2,1)S(1)} %cross.5.refs_2_, ...), custom_call_target="tpu_custom_call" | custom-call | flops 268435456 | bytes 1048576 | tf_op jit(solution)/shard_map/part/pallas_call | solution.py:456
  20.0 2.6 %collective-permute-done.6.rest_4_ = bf16[8,32,512]{2,1,0:T(8,128)(2,1)S(1)} collective-permute-done((bf16[8,32,512]{2,1,0:T(8,128)(2,1)S(1)}, bf16[8,32,512]{2,1,0:T(8,128)(2,1)S(1)}, u32[]{:S(2)}, u32[]{:S(2)}) %collective-permute-start.6) | collective-permute-done | bytes 262176 | tf_op jit(solution)/shard_map/ppermute | solution.py:416
  22.7 1.2 %lags.2.rest_0_ = bf16[8,64,512]{2,1,0:T(8,128)(2,1)} custom-call(bf16[512,512]{1,0:T(8,128)(2,1)S(1)} %inverse.1.table_ref, bf16[8,32,512]{2,1,0:T(8,128)(2,1)S(1)} %get-tuple-element.26.after_ref.refs_0_.rest_0_, bf16[8,32,512]{2,1,0:T(8,128)(2,1)S(1)} %get-tuple-element.27.after_ref.refs_1_.rest_1_, bf16[8,32,512]{2,1,0:T(8,128)(2,1)S(1)} %get-tuple-element.32.rest_2_, ...), custom_call_target="tpu_custom_call" | custom-call | flops 268435456 | bytes 1048576 | tf_op jit(solution)/shard_map/lags/pallas_call | solution.py:440
  23.8 1.6 %collective-permute-done.4.more_ref = bf16[8,32,512]{2,1,0:T(8,128)(2,1)S(1)} collective-permute-done((bf16[8,32,512]{2,1,0:T(8,128)(2,1)S(1)}, bf16[8,32,512]{2,1,0:T(8,128)(2,1)S(1)}, u32[]{:S(2)}, u32[]{:S(2)}) %collective-permute-start.4) | collective-permute-done | bytes 262176 | tf_op jit(solution)/shard_map/ppermute | solution.py:416
  25.5 1.0 %lags.3 = bf16[8,64,512]{2,1,0:T(8,128)(2,1)} custom-call(bf16[512,512]{1,0:T(8,128)(2,1)S(1)} %inverse.1.table_ref, f32[256,512]{1,0:T(8,128)S(1)} %part.1.rest_5_.part_ref, bf16[8,32,512]{2,1,0:T(8,128)(2,1)S(1)} %collective-permute-done.4.more_ref, bf16[8,64,512]{2,1,0:T(8,128)(2,1)} %lags.2.rest_0_), custom_call_target="tpu_custom_call", output_to_operand_aliasing={{}: (3, {})} | custom-call | flops 268435456 | bytes 1048576 | tf_op jit(solution)/shard_map/lags/pallas_call | solution.py:440
  (4 shorter events, 0.1 us)
Async XLA Ops:
  0.0 6.0 %copy-start = (bf16[64,8,512]{2,1,0:T(8,128)(2,1)S(1)}, bf16[64,8,512]{2,1,0:T(8,128)(2,1)}, u32[]{:S(2)}) copy-start(bf16[64,8,512]{2,1,0:T(8,128)(2,1)} %param.3) | copy-start | bytes 1572868
  1.6 5.8 %collective-permute-start = (bf16[32,4096]{1,0:T(8,128)(2,1)S(1)}, bf16[32,4096]{1,0:T(8,128)(2,1)S(1)}, u32[]{:S(2)}, u32[]{:S(2)}) collective-permute-start(bf16[32,4096]{1,0:T(8,128)(2,1)S(1)} %get-tuple-element.23.edge_ref), channel_id=1, source_target_pairs={{4,0},{5,1},{6,2},{7,3},{8,4},{9,5},{12,8},{13,9},{14,10},{15,11},... | collective-permute-start | bytes 786440 | tf_op jit(solution)/shard_map/ppermute | solution.py:369
  2.9 12.9 %collective-permute-start.1 = (bf16[32,4096]{1,0:T(8,128)(2,1)S(1)}, bf16[32,4096]{1,0:T(8,128)(2,1)S(1)}, u32[]{:S(2)}, u32[]{:S(2)}) collective-permute-start(bf16[32,4096]{1,0:T(8,128)(2,1)S(1)} %get-tuple-element.23.edge_ref), channel_id=1, source_target_pairs={{10,6},{11,7},{18,14},{19,15},{26,22},{27,23}} | collective-permute-start | bytes 786440 | tf_op jit(solution)/shard_map/ppermute | solution.py:369
  6.0 8.3 %collective-permute-start.5 = (bf16[8,32,512]{2,1,0:T(8,128)(2,1)S(1)}, bf16[8,32,512]{2,1,0:T(8,128)(2,1)S(1)}, u32[]{:S(2)}, u32[]{:S(2)}) collective-permute-start(bf16[8,32,512]{2,1,0:T(8,128)(2,1)S(1)} %get-tuple-element.26.after_ref.refs_0_.rest_0_), channel_id=1, source_target_pairs={{0,1},{1,0},{2,3},{4,6},{5,7},{8,9},{9,8},{10,11},{12,14},{13,15},... | collective-permute-start | bytes 786440 | tf_op jit(solution)/shard_map/ppermute | solution.py:416
  7.4 8.4 %collective-permute-start.2 = (bf16[8,32,512]{2,1,0:T(8,128)(2,1)S(1)}, bf16[8,32,512]{2,1,0:T(8,128)(2,1)S(1)}, u32[]{:S(2)}, u32[]{:S(2)}) collective-permute-start(bf16[8,32,512]{2,1,0:T(8,128)(2,1)S(1)} %cross.3._.after_ref.refs_0_.refs_3_), channel_id=1, source_target_pairs={{0,1},{1,0},{4,6},{5,7},{8,9},{9,8},{12,14},{13,15},{16,17},{17,16... | collective-permute-start | bytes 786440 | tf_op jit(solution)/shard_map/ppermute | solution.py:416
  8.1 11.5 %collective-permute-start.3 = (bf16[8,32,512]{2,1,0:T(8,128)(2,1)S(1)}, bf16[8,32,512]{2,1,0:T(8,128)(2,1)S(1)}, u32[]{:S(2)}, u32[]{:S(2)}) collective-permute-start(bf16[8,32,512]{2,1,0:T(8,128)(2,1)S(1)} %cross.3._.after_ref.refs_0_.refs_3_), channel_id=1, source_target_pairs={{2,3},{10,11},{18,19},{26,27}} | collective-permute-start | bytes 786440 | tf_op jit(solution)/shard_map/ppermute | solution.py:416
  14.4 8.3 %collective-permute-start.6 = (bf16[8,32,512]{2,1,0:T(8,128)(2,1)S(1)}, bf16[8,32,512]{2,1,0:T(8,128)(2,1)S(1)}, u32[]{:S(2)}, u32[]{:S(2)}) collective-permute-start(bf16[8,32,512]{2,1,0:T(8,128)(2,1)S(1)} %mix.3), channel_id=1, source_target_pairs={{0,2},{1,3},{4,5},{6,7},{7,6},{8,10},{9,11},{12,13},{14,15},{15,14... | collective-permute-start | bytes 786440 | tf_op jit(solution)/shard_map/ppermute | solution.py:416
  15.9 9.6 %collective-permute-start.4 = (bf16[8,32,512]{2,1,0:T(8,128)(2,1)S(1)}, bf16[8,32,512]{2,1,0:T(8,128)(2,1)S(1)}, u32[]{:S(2)}, u32[]{:S(2)}) collective-permute-start(bf16[8,32,512]{2,1,0:T(8,128)(2,1)S(1)} %mix.2.after_ref), channel_id=1, source_target_pairs={{0,2},{1,3},{4,5},{6,7},{7,6},{8,10},{9,11},{12,13},{14,15},{15,14... | collective-permute-start | bytes 786440 | tf_op jit(solution)/shard_map/ppermute | solution.py:416

commit v11 on v10

--- a/solution.py
+++ b/solution.py
@@ -203,12 +203,16 @@
     white_ref,
     short_ref,
     out_ref,
+    again_ref,
     raw_ref,
     near_ref,
     *parts_refs,
 ):
     wins, span, length = white_ref.shape
     rows = slice(span * wins, 2 * span * wins)
+
+    if now == 0:
+        again_ref[...] = edge_ref[...]
 
     @pl.when(role(limits) == now)
     def _():
@@ -360,13 +364,13 @@
 
     ring = lax.axis_size("chan")
 
-    def to_previous(odd, even):
+    def to_previous(value, odd, even):
         moves = [
             (c * groups + h, (c - 1) * groups + h)
             for c in range(1, ring)
             for h in (odd if c % 2 else even)
         ]
-        return lax.ppermute(short_a, ("chan", "tm"), moves)
+        return lax.ppermute(value, ("chan", "tm"), moves)
 
 
     columns = min(d for d in range(1, groups + 1) if groups % d == 0 and d * d >= groups)
@@ -374,15 +378,14 @@
     limits = (2, 3) if square else (groups, groups)
 
     ahead = 2 if square else groups
-    edge = to_previous(range(groups), range(ahead))
-    edge_late = to_previous([], range(ahead, groups)) if square else edge
+    edge = to_previous(short_a, range(groups), range(ahead))
 
     def tail(now, after):
         return pl.pallas_call(
             functools.partial(tail_kernel, limits, now),
-            out_shape=(white_type, short_type, local_type),
+            out_shape=(white_type, short_type, local_type, short_type),
             in_specs=[whole()] * 6 + [whole(pl.ANY)],
-            out_specs=(whole(),) * 3,
+            out_specs=(whole(),) * 4,
             scratch_shapes=[raw_scratch, near_scratch] + parts_scratch,
             compiler_params=params,
             cost_estimate=cost(span * wins * length * length * 4, 4 * 1024 * 1024),
@@ -401,8 +404,9 @@
             name="cross",
         )(pick, white, short, edge, after)
 
-    white_b, short_b, local_a = tail(0, table)
-    white_late, short_late, late_a = tail(1, local_a)
+    white_b, short_b, local_a, again = tail(0, table)
+    edge_late = to_previous(again, [], range(ahead, groups)) if square else edge
+    white_late, short_late, late_a, _ = tail(1, local_a)
     local_b = cross(0, white_b, short_b, edge, late_a)
     late_b = cross(1, white_late, short_late, edge_late, local_b)
 
@@ -495,7 +499,7 @@
     scale = bins**-0.5
     _, terms_a, weights_a = spread(local_a, late_a, local_b, False)
     ahead, terms_b, weights_b = spread(local_b, late_b, local_b, True)
-    white_last, short_last, last_a = tail(2, ahead)
+    white_last, short_last, last_a, _ = tail(2, ahead)
     last_b = cross(2, white_last, short_last, edge, ahead)
     terms_a = [local_a, late_a, last_a] + terms_a
     terms_b = [local_b, late_b, last_b] + terms_b

time: 26.8 us -> 26.3 us (0.981)
  the two profiles are of different devices: /device:TPU:14 before, /device:TPU:28 now
where the time goes in v11:
time: 26.3 us; the launch traced here: 25.9 us
  starting transfers between devices  10.3 us (39%)
  Pallas kernels  8.23 us (31%)
  waiting for transfers between devices  7.2 us (27%)
    ppermute x5, starting transfers between devices, sent(): return lax.ppermute(value, ('chan', 'tm'), moves)  7.72 us
    ppermute x5, waiting for transfers between devices, sent(): return lax.ppermute(value, ('chan', 'tm'), moves)  7.19 us
    pallas_call x3, Pallas kernels, tail(): pl.pallas_call(functools.partial(tail_kernel, limits, now), out_shape=(wh...  2.74 us
    ppermute x2, starting transfers between devices, to_previous(): return lax.ppermute(value, ('chan', 'tm'), moves)  2.6 us
    pallas_call x2, Pallas kernels, written(): pl.pallas_call(kernel, out_shape=jax.ShapeDtypeStruct((pairs, chans, leng...  2.18 us
    pallas_call x1, Pallas kernels, per_device(): pl.pallas_call(head_kernel, out_shape=(white_type, short_type, jax.ShapeD...  1.54 us
    pallas_call x3, Pallas kernels, cross(): pl.pallas_call(functools.partial(cross_kernel, limits, now), out_shape=lo...  0.79 us
  transfers between devices with their start and end apart: 7, of which 3 were waited for; matrix products, arithmetic and copies ran while one was open for 0% of the time, Pallas kernels for 22%

profile of v11, /device:TPU:28, one launch (start us, length us, event | category | flops | bytes accessed | tf_op | source)
XLA Modules:
  0.0 25.9 jit_solution(12807306034595568595)
XLA Ops:
  0.0 0.0 copy-start
  0.0 1.5 %head.1 = (f32[8,32,512]{2,1,0:T(8,128)S(1)}, bf16[32,4096]{1,0:T(8,128)(2,1)S(1)}, bf16[512,512]{1,0:T(8,128)(2,1)S(1)}, bf16[8,32,64]{2,1,0:T(8,128)(2,1)S(1)}, f32[64,1024]{1,0:T(8,128)S(1)}) custom-call(bf16[512,512]{1,0:T(8,128)(2,1)} %bitcast.3, s32[8,64]{1,0:T(8,128)} %bitcast.7, s32[8]{0:T(128)} %offsets_hbm.1), custom_call_target="tpu_custom_call" | custom-call | flops 134217728 | bytes 2097152 | tf_op jit(solution)/shard_map/head/pallas_call | solution.py:342
  1.5 1.3 %collective-permute-start = (bf16[32,4096]{1,0:T(8,128)(2,1)S(1)}, bf16[32,4096]{1,0:T(8,128)(2,1)S(1)}, u32[]{:S(2)}, u32[]{:S(2)}) collective-permute-start(bf16[32,4096]{1,0:T(8,128)(2,1)S(1)} %get-tuple-element.24.edge_ref), channel_id=1, source_target_pairs={{4,0},{5,1},{6,2},{7,3},{8,4},{9,5},{12,8},{13,9},{14,10},{15,11},... | collective-permute-start | bytes 786440 | tf_op jit(solution)/shard_map/ppermute | solution.py:373
  2.8 0.0 copy-done
  2.9 1.3 %tail.3 = (f32[8,32,512]{2,1,0:T(8,128)S(1)}, bf16[32,4096]{1,0:T(8,128)(2,1)S(1)}, bf16[8,32,512]{2,1,0:T(8,128)(2,1)S(1)}, bf16[32,4096]{1,0:T(8,128)(2,1)S(1)}) custom-call(bf16[512,512]{1,0:T(8,128)(2,1)S(1)} %bitcast.4, bf16[512,512]{1,0:T(8,128)(2,1)S(1)} %get-tuple-element.21.table_ref.after_ref, f32[64,1024]{1,0:T(8,128)S(1)} %get-tuple-element.22.keep_ref, ...), custom_call_target="tpu_custom_call" | custom-call | flops 268435456 | bytes 4194304 | tf_op jit(solution)/shard_map/tail/pallas_call | solution.py:384
  4.2 2.1 %collective-permute-start.5 = (bf16[8,32,512]{2,1,0:T(8,128)(2,1)S(1)}, bf16[8,32,512]{2,1,0:T(8,128)(2,1)S(1)}, u32[]{:S(2)}, u32[]{:S(2)}) collective-permute-start(bf16[8,32,512]{2,1,0:T(8,128)(2,1)S(1)} %get-tuple-element.27.after_ref.refs_0_.rest_0_), channel_id=1, source_target_pairs={{0,1},{1,0},{2,3},{4,6},{5,7},{8,9},{9,8},{10,11},{12,14},{13,15},... | collective-permute-start | bytes 786440 | tf_op jit(solution)/shard_map/ppermute | solution.py:420
  6.3 1.3 %collective-permute-start.1 = (bf16[32,4096]{1,0:T(8,128)(2,1)S(1)}, bf16[32,4096]{1,0:T(8,128)(2,1)S(1)}, u32[]{:S(2)}, u32[]{:S(2)}) collective-permute-start(bf16[32,4096]{1,0:T(8,128)(2,1)S(1)} %get-tuple-element.31), channel_id=1, source_target_pairs={{10,6},{11,7},{18,14},{19,15},{26,22},{27,23}} | collective-permute-start | bytes 786440 | tf_op jit(solution)/shard_map/ppermute | solution.py:373
  7.6 0.7 %tail.4 = (f32[8,32,512]{2,1,0:T(8,128)S(1)}, bf16[32,4096]{1,0:T(8,128)(2,1)S(1)}, bf16[8,32,512]{2,1,0:T(8,128)(2,1)S(1)}, bf16[32,4096]{1,0:T(8,128)(2,1)}) custom-call(bf16[512,512]{1,0:T(8,128)(2,1)S(1)} %bitcast.5, bf16[512,512]{1,0:T(8,128)(2,1)S(1)} %get-tuple-element.21.table_ref.after_ref, f32[64,1024]{1,0:T(8,128)S(1)} %get-tuple-element.22.keep_ref, ...), custom_call_target="tpu_custom_call" | custom-call | flops 268435456 | bytes 4194304 | tf_op jit(solution)/shard_map/tail/pallas_call | solution.py:384
  8.4 0.0 collective-permute-done.edge_ref
  8.4 0.8 %cross.3._.after_ref.refs_0_.refs_3_ = bf16[8,32,512]{2,1,0:T(8,128)(2,1)S(1)} custom-call(bf16[8,32,64]{2,1,0:T(8,128)(2,1)S(1)} %get-tuple-element.20.pick_ref, f32[8,32,512]{2,1,0:T(8,128)S(1)} %get-tuple-element.25.white_ref, bf16[32,4096]{1,0:T(8,128)(2,1)S(1)} %get-tuple-element.26.short_ref, bf16[32,4096]{1,0:T(8,128)(2,1)S(1)} %collective-permute-done.edge_ref, ...), custom_call_target="tpu_custom_call" | custom-call | flops 4194304 | bytes 4194304 | tf_op jit(solution)/shard_map/cross/pallas_call | solution.py:396
  9.1 0.7 %collective-permute-start.2 = (bf16[8,32,512]{2,1,0:T(8,128)(2,1)S(1)}, bf16[8,32,512]{2,1,0:T(8,128)(2,1)S(1)}, u32[]{:S(2)}, u32[]{:S(2)}) collective-permute-start(bf16[8,32,512]{2,1,0:T(8,128)(2,1)S(1)} %cross.3._.after_ref.refs_0_.refs_3_), channel_id=1, source_target_pairs={{0,1},{1,0},{4,6},{5,7},{8,9},{9,8},{12,14},{13,15},{16,17},{17,16... | collective-permute-start | bytes 786440 | tf_op jit(solution)/shard_map/ppermute | solution.py:420
  9.8 2.3 %collective-permute-start.3 = (bf16[8,32,512]{2,1,0:T(8,128)(2,1)S(1)}, bf16[8,32,512]{2,1,0:T(8,128)(2,1)S(1)}, u32[]{:S(2)}, u32[]{:S(2)}) collective-permute-start(bf16[8,32,512]{2,1,0:T(8,128)(2,1)S(1)} %cross.3._.after_ref.refs_0_.refs_3_), channel_id=1, source_target_pairs={{2,3},{10,11},{18,19},{26,27}} | collective-permute-start | bytes 786440 | tf_op jit(solution)/shard_map/ppermute | solution.py:420
  12.1 0.0 collective-permute-done.5.refs_2_.rest_3_
  12.1 0.1 mix.3
  12.3 1.3 %collective-permute-start.6 = (bf16[8,32,512]{2,1,0:T(8,128)(2,1)S(1)}, bf16[8,32,512]{2,1,0:T(8,128)(2,1)S(1)}, u32[]{:S(2)}, u32[]{:S(2)}) collective-permute-start(bf16[8,32,512]{2,1,0:T(8,128)(2,1)S(1)} %mix.3), channel_id=1, source_target_pairs={{0,2},{1,3},{4,5},{6,7},{7,6},{8,10},{9,11},{12,13},{14,15},{15,14... | collective-permute-start | bytes 786440 | tf_op jit(solution)/shard_map/ppermute | solution.py:420
  13.6 0.0 collective-permute-done.1.edge_ref
  13.6 0.0 collective-permute-done.2.refs_2_.refs_3_
  13.6 0.1 mix.2.after_ref
  13.8 1.3 %collective-permute-start.4 = (bf16[8,32,512]{2,1,0:T(8,128)(2,1)S(1)}, bf16[8,32,512]{2,1,0:T(8,128)(2,1)S(1)}, u32[]{:S(2)}, u32[]{:S(2)}) collective-permute-start(bf16[8,32,512]{2,1,0:T(8,128)(2,1)S(1)} %mix.2.after_ref), channel_id=1, source_target_pairs={{0,2},{1,3},{4,5},{6,7},{7,6},{8,10},{9,11},{12,13},{14,15},{15,14... | collective-permute-start | bytes 786440 | tf_op jit(solution)/shard_map/ppermute | solution.py:420
  15.1 0.3 %inverse.1.table_ref = bf16[512,512]{1,0:T(8,128)(2,1)S(1)} custom-call(bf16[8,32,512]{2,1,0:T(8,128)(2,1)S(1)} %cross.3._.after_ref.refs_0_.refs_3_), custom_call_target="tpu_custom_call" | custom-call | flops 4194304 | bytes 524288 | tf_op jit(solution)/shard_map/inverse/pallas_call | solution.py:433
  15.4 0.7 %tail.5 = (f32[8,32,512]{2,1,0:T(8,128)S(1)}, bf16[32,4096]{1,0:T(8,128)(2,1)S(1)}, bf16[8,32,512]{2,1,0:T(8,128)(2,1)S(1)}, bf16[32,4096]{1,0:T(8,128)(2,1)}) custom-call(bf16[512,512]{1,0:T(8,128)(2,1)S(1)} %bitcast.6, bf16[512,512]{1,0:T(8,128)(2,1)S(1)} %get-tuple-element.21.table_ref.after_ref, f32[64,1024]{1,0:T(8,128)S(1)} %get-tuple-element.22.keep_ref, ...), custom_call_target="tpu_custom_call" | custom-call | flops 268435456 | bytes 4194304 | tf_op jit(solution)/shard_map/tail/pallas_call | solution.py:384
  16.1 0.9 %collective-permute-done.3.refs_4_ = bf16[8,32,512]{2,1,0:T(8,128)(2,1)S(1)} collective-permute-done((bf16[8,32,512]{2,1,0:T(8,128)(2,1)S(1)}, bf16[8,32,512]{2,1,0:T(8,128)(2,1)S(1)}, u32[]{:S(2)}, u32[]{:S(2)}) %collective-permute-start.3) | collective-permute-done | bytes 262176 | tf_op jit(solution)/shard_map/ppermute | solution.py:420
  17.0 0.4 %part.1.rest_5_.part_ref = f32[256,512]{1,0:T(8,128)S(1)} custom-call(bf16[512,512]{1,0:T(8,128)(2,1)S(1)} %inverse.1.table_ref, bf16[8,32,512]{2,1,0:T(8,128)(2,1)S(1)} %cross.3._.after_ref.refs_0_.refs_3_, bf16[8,32,512]{2,1,0:T(8,128)(2,1)S(1)} %cross.4.refs_1_, bf16[8,32,512]{2,1,0:T(8,128)(2,1)S(1)} %cross.5.refs_2_, ...), custom_call_target="tpu_custom_call" | custom-call | flops 268435456 | bytes 1048576 | tf_op jit(solution)/shard_map/part/pallas_call | solution.py:460
  17.5 3.1 %collective-permute-done.6.rest_4_ = bf16[8,32,512]{2,1,0:T(8,128)(2,1)S(1)} collective-permute-done((bf16[8,32,512]{2,1,0:T(8,128)(2,1)S(1)}, bf16[8,32,512]{2,1,0:T(8,128)(2,1)S(1)}, u32[]{:S(2)}, u32[]{:S(2)}) %collective-permute-start.6) | collective-permute-done | bytes 262176 | tf_op jit(solution)/shard_map/ppermute | solution.py:420
  20.5 1.2 %lags.2.rest_0_ = bf16[8,64,512]{2,1,0:T(8,128)(2,1)} custom-call(bf16[512,512]{1,0:T(8,128)(2,1)S(1)} %inverse.1.table_ref, bf16[8,32,512]{2,1,0:T(8,128)(2,1)S(1)} %get-tuple-element.27.after_ref.refs_0_.rest_0_, bf16[8,32,512]{2,1,0:T(8,128)(2,1)S(1)} %get-tuple-element.28.after_ref.refs_1_.rest_1_, bf16[8,32,512]{2,1,0:T(8,128)(2,1)S(1)} %get-tuple-element.34.rest_2_, ...), custom_call_target="tpu_custom_call" | custom-call | flops 268435456 | bytes 1048576 | tf_op jit(solution)/shard_map/lags/pallas_call | solution.py:444
  21.7 3.2 %collective-permute-done.4.more_ref = bf16[8,32,512]{2,1,0:T(8,128)(2,1)S(1)} collective-permute-done((bf16[8,32,512]{2,1,0:T(8,128)(2,1)S(1)}, bf16[8,32,512]{2,1,0:T(8,128)(2,1)S(1)}, u32[]{:S(2)}, u32[]{:S(2)}) %collective-permute-start.4) | collective-permute-done | bytes 262176 | tf_op jit(solution)/shard_map/ppermute | solution.py:420
  24.9 1.0 %lags.3 = bf16[8,64,512]{2,1,0:T(8,128)(2,1)} custom-call(bf16[512,512]{1,0:T(8,128)(2,1)S(1)} %inverse.1.table_ref, f32[256,512]{1,0:T(8,128)S(1)} %part.1.rest_5_.part_ref, bf16[8,32,512]{2,1,0:T(8,128)(2,1)S(1)} %collective-permute-done.4.more_ref, bf16[8,64,512]{2,1,0:T(8,128)(2,1)} %lags.2.rest_0_), custom_call_target="tpu_custom_call", output_to_operand_aliasing={{}: (3, {})} | custom-call | flops 268435456 | bytes 1048576 | tf_op jit(solution)/shard_map/lags/pallas_call | solution.py:444
  (2 shorter events, 0.0 us)
Async XLA Ops:
  0.0 2.9 %copy-start = (bf16[64,8,512]{2,1,0:T(8,128)(2,1)S(1)}, bf16[64,8,512]{2,1,0:T(8,128)(2,1)}, u32[]{:S(2)}) copy-start(bf16[64,8,512]{2,1,0:T(8,128)(2,1)} %param.3) | copy-start | bytes 1572868
  1.5 6.8 %collective-permute-start = (bf16[32,4096]{1,0:T(8,128)(2,1)S(1)}, bf16[32,4096]{1,0:T(8,128)(2,1)S(1)}, u32[]{:S(2)}, u32[]{:S(2)}) collective-permute-start(bf16[32,4096]{1,0:T(8,128)(2,1)S(1)} %get-tuple-element.24.edge_ref), channel_id=1, source_target_pairs={{4,0},{5,1},{6,2},{7,3},{8,4},{9,5},{12,8},{13,9},{14,10},{15,11},... | collective-permute-start | bytes 786440 | tf_op jit(solution)/shard_map/ppermute | solution.py:373
  4.2 8.0 %collective-permute-start.5 = (bf16[8,32,512]{2,1,0:T(8,128)(2,1)S(1)}, bf16[8,32,512]{2,1,0:T(8,128)(2,1)S(1)}, u32[]{:S(2)}, u32[]{:S(2)}) collective-permute-start(bf16[8,32,512]{2,1,0:T(8,128)(2,1)S(1)} %get-tuple-element.27.after_ref.refs_0_.rest_0_), channel_id=1, source_target_pairs={{0,1},{1,0},{2,3},{4,6},{5,7},{8,9},{9,8},{10,11},{12,14},{13,15},... | collective-permute-start | bytes 786440 | tf_op jit(solution)/shard_map/ppermute | solution.py:420
  6.3 7.3 %collective-permute-start.1 = (bf16[32,4096]{1,0:T(8,128)(2,1)S(1)}, bf16[32,4096]{1,0:T(8,128)(2,1)S(1)}, u32[]{:S(2)}, u32[]{:S(2)}) collective-permute-start(bf16[32,4096]{1,0:T(8,128)(2,1)S(1)} %get-tuple-element.31), channel_id=1, source_target_pairs={{10,6},{11,7},{18,14},{19,15},{26,22},{27,23}} | collective-permute-start | bytes 786440 | tf_op jit(solution)/shard_map/ppermute | solution.py:373
  9.1 4.5 %collective-permute-start.2 = (bf16[8,32,512]{2,1,0:T(8,128)(2,1)S(1)}, bf16[8,32,512]{2,1,0:T(8,128)(2,1)S(1)}, u32[]{:S(2)}, u32[]{:S(2)}) collective-permute-start(bf16[8,32,512]{2,1,0:T(8,128)(2,1)S(1)} %cross.3._.after_ref.refs_0_.refs_3_), channel_id=1, source_target_pairs={{0,1},{1,0},{4,6},{5,7},{8,9},{9,8},{12,14},{13,15},{16,17},{17,16... | collective-permute-start | bytes 786440 | tf_op jit(solution)/shard_map/ppermute | solution.py:420
  9.8 7.2 %collective-permute-start.3 = (bf16[8,32,512]{2,1,0:T(8,128)(2,1)S(1)}, bf16[8,32,512]{2,1,0:T(8,128)(2,1)S(1)}, u32[]{:S(2)}, u32[]{:S(2)}) collective-permute-start(bf16[8,32,512]{2,1,0:T(8,128)(2,1)S(1)} %cross.3._.after_ref.refs_0_.refs_3_), channel_id=1, source_target_pairs={{2,3},{10,11},{18,19},{26,27}} | collective-permute-start | bytes 786440 | tf_op jit(solution)/shard_map/ppermute | solution.py:420
  12.3 8.3 %collective-permute-start.6 = (bf16[8,32,512]{2,1,0:T(8,128)(2,1)S(1)}, bf16[8,32,512]{2,1,0:T(8,128)(2,1)S(1)}, u32[]{:S(2)}, u32[]{:S(2)}) collective-permute-start(bf16[8,32,512]{2,1,0:T(8,128)(2,1)S(1)} %mix.3), channel_id=1, source_target_pairs={{0,2},{1,3},{4,5},{6,7},{7,6},{8,10},{9,11},{12,13},{14,15},{15,14... | collective-permute-start | bytes 786440 | tf_op jit(solution)/shard_map/ppermute | solution.py:420
  13.8 11.1 %collective-permute-start.4 = (bf16[8,32,512]{2,1,0:T(8,128)(2,1)S(1)}, bf16[8,32,512]{2,1,0:T(8,128)(2,1)S(1)}, u32[]{:S(2)}, u32[]{:S(2)}) collective-permute-start(bf16[8,32,512]{2,1,0:T(8,128)(2,1)S(1)} %mix.2.after_ref), channel_id=1, source_target_pairs={{0,2},{1,3},{4,5},{6,7},{7,6},{8,10},{9,11},{12,13},{14,15},{15,14... | collective-permute-start | bytes 786440 | tf_op jit(solution)/shard_map/ppermute | solution.py:420

commit v12 on v11

--- a/solution.py
+++ b/solution.py
@@ -203,16 +203,15 @@
     white_ref,
     short_ref,
     out_ref,
-    again_ref,
-    raw_ref,
-    near_ref,
-    *parts_refs,
+    *rest,
 ):
     wins, span, length = white_ref.shape
     rows = slice(span * wins, 2 * span * wins)
 
     if now == 0:
-        again_ref[...] = edge_ref[...]
+        rest[0][...] = edge_ref[...]
+        rest = rest[1:]
+    raw_ref, near_ref, *parts_refs = rest
 
     @pl.when(role(limits) == now)
     def _():
@@ -383,9 +382,9 @@
     def tail(now, after):
         return pl.pallas_call(
             functools.partial(tail_kernel, limits, now),
-            out_shape=(white_type, short_type, local_type, short_type),
+            out_shape=(white_type, short_type, local_type) + (short_type,) * (now == 0),
             in_specs=[whole()] * 6 + [whole(pl.ANY)],
-            out_specs=(whole(),) * 4,
+            out_specs=(whole(),) * (3 + (now == 0)),
             scratch_shapes=[raw_scratch, near_scratch] + parts_scratch,
             compiler_params=params,
             cost_estimate=cost(span * wins * length * length * 4, 4 * 1024 * 1024),
@@ -406,7 +405,7 @@
 
     white_b, short_b, local_a, again = tail(0, table)
     edge_late = to_previous(again, [], range(ahead, groups)) if square else edge
-    white_late, short_late, late_a, _ = tail(1, local_a)
+    white_late, short_late, late_a = tail(1, local_a)
     local_b = cross(0, white_b, short_b, edge, late_a)
     late_b = cross(1, white_late, short_late, edge_late, local_b)
 
@@ -499,7 +498,7 @@
     scale = bins**-0.5
     _, terms_a, weights_a = spread(local_a, late_a, local_b, False)
     ahead, terms_b, weights_b = spread(local_b, late_b, local_b, True)
-    white_last, short_last, last_a, _ = tail(2, ahead)
+    white_last, short_last, last_a = tail(2, ahead)
     last_b = cross(2, white_last, short_last, edge, ahead)
     terms_a = [local_a, late_a, last_a] + terms_a
     terms_b = [local_b, late_b, last_b] + terms_b

time: 26.3 us -> 25.6 us (0.973)
  Pallas kernels: 8.23 us -> 6.86 us
  waiting for transfers between devices: 7.2 us -> 7.83 us
    pallas_call x3, Pallas kernels: 2.74 us -> 1.34 us  [tail(): pl.pallas_call(functools.partial(tail_kernel, limits, now), out_shape=(wh...]
    ppermute x5, waiting for transfers between devices: 7.19 us -> 7.82 us  [sent(): return lax.ppermute(value, ('chan', 'tm'), moves)]
  transfers between devices with their start and end apart: 7 -> 7, of which waited for: 3 -> 3; matrix products, arithmetic and copies ran while one was open for 0% -> 0% of each run, Pallas kernels for 22% -> 17%
where the time goes in v12:
time: 25.6 us; the launch traced here: 25.2 us
  starting transfers between devices  10.4 us (41%)
  waiting for transfers between devices  7.83 us (31%)
  Pallas kernels  6.86 us (27%)
    ppermute x5, waiting for transfers between devices, sent(): return lax.ppermute(value, ('chan', 'tm'), moves)  7.82 us
    ppermute x5, starting transfers between devices, sent(): return lax.ppermute(value, ('chan', 'tm'), moves)  7.76 us
    ppermute x2, starting transfers between devices, to_previous(): return lax.ppermute(value, ('chan', 'tm'), moves)  2.6 us
    pallas_call x2, Pallas kernels, written(): pl.pallas_call(kernel, out_shape=jax.ShapeDtypeStruct((pairs, chans, leng...  2.18 us
    pallas_call x1, Pallas kernels, per_device(): pl.pallas_call(head_kernel, out_shape=(white_type, short_type, jax.ShapeD...  1.54 us
    pallas_call x3, Pallas kernels, tail(): pl.pallas_call(functools.partial(tail_kernel, limits, now), out_shape=(wh...  1.34 us
    pallas_call x3, Pallas kernels, cross(): pl.pallas_call(functools.partial(cross_kernel, limits, now), out_shape=lo...  0.82 us
  transfers between devices with their start and end apart: 7, of which 3 were waited for; matrix products, arithmetic and copies ran while one was open for 0% of the time, Pallas kernels for 17%

profile of v12, /device:TPU:28, one launch (start us, length us, event | category | flops | bytes accessed | tf_op | source)
XLA Modules:
  0.0 25.2 jit_solution(8037768142347818594)
XLA Ops:
  0.0 0.0 copy-start
  0.0 1.5 %head.1 = (f32[8,32,512]{2,1,0:T(8,128)S(1)}, bf16[32,4096]{1,0:T(8,128)(2,1)S(1)}, bf16[512,512]{1,0:T(8,128)(2,1)S(1)}, bf16[8,32,64]{2,1,0:T(8,128)(2,1)S(1)}, f32[64,1024]{1,0:T(8,128)S(1)}) custom-call(bf16[512,512]{1,0:T(8,128)(2,1)} %bitcast.3, s32[8,64]{1,0:T(8,128)} %bitcast.7, s32[8]{0:T(128)} %offsets_hbm.1), custom_call_target="tpu_custom_call" | custom-call | flops 134217728 | bytes 2097152 | tf_op jit(solution)/shard_map/head/pallas_call | solution.py:341
  1.5 1.3 %collective-permute-start = (bf16[32,4096]{1,0:T(8,128)(2,1)S(1)}, bf16[32,4096]{1,0:T(8,128)(2,1)S(1)}, u32[]{:S(2)}, u32[]{:S(2)}) collective-permute-start(bf16[32,4096]{1,0:T(8,128)(2,1)S(1)} %get-tuple-element.24.edge_ref), channel_id=1, source_target_pairs={{4,0},{5,1},{6,2},{7,3},{8,4},{9,5},{12,8},{13,9},{14,10},{15,11},... | collective-permute-start | bytes 786440 | tf_op jit(solution)/shard_map/ppermute | solution.py:372
  2.8 0.0 copy-done
  2.9 1.3 %tail.3 = (f32[8,32,512]{2,1,0:T(8,128)S(1)}, bf16[32,4096]{1,0:T(8,128)(2,1)S(1)}, bf16[8,32,512]{2,1,0:T(8,128)(2,1)S(1)}, bf16[32,4096]{1,0:T(8,128)(2,1)S(1)}) custom-call(bf16[512,512]{1,0:T(8,128)(2,1)S(1)} %bitcast.4, bf16[512,512]{1,0:T(8,128)(2,1)S(1)} %get-tuple-element.21.table_ref.after_ref, f32[64,1024]{1,0:T(8,128)S(1)} %get-tuple-element.22.keep_ref, ...), custom_call_target="tpu_custom_call" | custom-call | flops 268435456 | bytes 4194304 | tf_op jit(solution)/shard_map/tail/pallas_call | solution.py:383
  4.2 2.1 %collective-permute-start.5 = (bf16[8,32,512]{2,1,0:T(8,128)(2,1)S(1)}, bf16[8,32,512]{2,1,0:T(8,128)(2,1)S(1)}, u32[]{:S(2)}, u32[]{:S(2)}) collective-permute-start(bf16[8,32,512]{2,1,0:T(8,128)(2,1)S(1)} %get-tuple-element.27.after_ref.refs_0_.rest_0_), channel_id=1, source_target_pairs={{0,1},{1,0},{2,3},{4,6},{5,7},{8,9},{9,8},{10,11},{12,14},{13,15},... | collective-permute-start | bytes 786440 | tf_op jit(solution)/shard_map/ppermute | solution.py:419
  6.3 1.3 %collective-permute-start.1 = (bf16[32,4096]{1,0:T(8,128)(2,1)S(1)}, bf16[32,4096]{1,0:T(8,128)(2,1)S(1)}, u32[]{:S(2)}, u32[]{:S(2)}) collective-permute-start(bf16[32,4096]{1,0:T(8,128)(2,1)S(1)} %get-tuple-element.31), channel_id=1, source_target_pairs={{10,6},{11,7},{18,14},{19,15},{26,22},{27,23}} | collective-permute-start | bytes 786440 | tf_op jit(solution)/shard_map/ppermute | solution.py:372
  7.7 0.0 collective-permute-done.edge_ref
  7.7 0.8 %cross.3._.after_ref.refs_0_.refs_3_ = bf16[8,32,512]{2,1,0:T(8,128)(2,1)S(1)} custom-call(bf16[8,32,64]{2,1,0:T(8,128)(2,1)S(1)} %get-tuple-element.20.pick_ref, f32[8,32,512]{2,1,0:T(8,128)S(1)} %get-tuple-element.25.white_ref, bf16[32,4096]{1,0:T(8,128)(2,1)S(1)} %get-tuple-element.26.short_ref, bf16[32,4096]{1,0:T(8,128)(2,1)S(1)} %collective-permute-done.edge_ref, ...), custom_call_target="tpu_custom_call" | custom-call | flops 4194304 | bytes 4194304 | tf_op jit(solution)/shard_map/cross/pallas_call | solution.py:395
  8.4 0.7 %collective-permute-start.2 = (bf16[8,32,512]{2,1,0:T(8,128)(2,1)S(1)}, bf16[8,32,512]{2,1,0:T(8,128)(2,1)S(1)}, u32[]{:S(2)}, u32[]{:S(2)}) collective-permute-start(bf16[8,32,512]{2,1,0:T(8,128)(2,1)S(1)} %cross.3._.after_ref.refs_0_.refs_3_), channel_id=1, source_target_pairs={{0,1},{1,0},{4,6},{5,7},{8,9},{9,8},{12,14},{13,15},{16,17},{17,16... | collective-permute-start | bytes 786440 | tf_op jit(solution)/shard_map/ppermute | solution.py:419
  9.1 2.4 %collective-permute-start.3 = (bf16[8,32,512]{2,1,0:T(8,128)(2,1)S(1)}, bf16[8,32,512]{2,1,0:T(8,128)(2,1)S(1)}, u32[]{:S(2)}, u32[]{:S(2)}) collective-permute-start(bf16[8,32,512]{2,1,0:T(8,128)(2,1)S(1)} %cross.3._.after_ref.refs_0_.refs_3_), channel_id=1, source_target_pairs={{2,3},{10,11},{18,19},{26,27}} | collective-permute-start | bytes 786440 | tf_op jit(solution)/shard_map/ppermute | solution.py:419
  11.5 0.0 collective-permute-done.5.refs_2_.rest_3_
  11.5 0.1 mix.3
  11.6 1.3 %collective-permute-start.6 = (bf16[8,32,512]{2,1,0:T(8,128)(2,1)S(1)}, bf16[8,32,512]{2,1,0:T(8,128)(2,1)S(1)}, u32[]{:S(2)}, u32[]{:S(2)}) collective-permute-start(bf16[8,32,512]{2,1,0:T(8,128)(2,1)S(1)} %mix.3), channel_id=1, source_target_pairs={{0,2},{1,3},{4,5},{6,7},{7,6},{8,10},{9,11},{12,13},{14,15},{15,14... | collective-permute-start | bytes 786440 | tf_op jit(solution)/shard_map/ppermute | solution.py:419
  12.9 0.0 collective-permute-done.1.edge_ref
  13.0 0.0 collective-permute-done.2.refs_2_.refs_3_
  13.0 0.1 mix.2.after_ref
  13.1 1.3 %collective-permute-start.4 = (bf16[8,32,512]{2,1,0:T(8,128)(2,1)S(1)}, bf16[8,32,512]{2,1,0:T(8,128)(2,1)S(1)}, u32[]{:S(2)}, u32[]{:S(2)}) collective-permute-start(bf16[8,32,512]{2,1,0:T(8,128)(2,1)S(1)} %mix.2.after_ref), channel_id=1, source_target_pairs={{0,2},{1,3},{4,5},{6,7},{7,6},{8,10},{9,11},{12,13},{14,15},{15,14... | collective-permute-start | bytes 786440 | tf_op jit(solution)/shard_map/ppermute | solution.py:419
  14.4 0.3 %inverse.1.table_ref = bf16[512,512]{1,0:T(8,128)(2,1)S(1)} custom-call(bf16[8,32,512]{2,1,0:T(8,128)(2,1)S(1)} %cross.3._.after_ref.refs_0_.refs_3_), custom_call_target="tpu_custom_call" | custom-call | flops 4194304 | bytes 524288 | tf_op jit(solution)/shard_map/inverse/pallas_call | solution.py:432
  14.8 0.9 %collective-permute-done.3.refs_4_ = bf16[8,32,512]{2,1,0:T(8,128)(2,1)S(1)} collective-permute-done((bf16[8,32,512]{2,1,0:T(8,128)(2,1)S(1)}, bf16[8,32,512]{2,1,0:T(8,128)(2,1)S(1)}, u32[]{:S(2)}, u32[]{:S(2)}) %collective-permute-start.3) | collective-permute-done | bytes 262176 | tf_op jit(solution)/shard_map/ppermute | solution.py:419
  15.7 0.4 %part.1.rest_5_.part_ref = f32[256,512]{1,0:T(8,128)S(1)} custom-call(bf16[512,512]{1,0:T(8,128)(2,1)S(1)} %inverse.1.table_ref, bf16[8,32,512]{2,1,0:T(8,128)(2,1)S(1)} %cross.3._.after_ref.refs_0_.refs_3_, bf16[8,32,512]{2,1,0:T(8,128)(2,1)S(1)} %cross.4.refs_1_, bf16[8,32,512]{2,1,0:T(8,128)(2,1)S(1)} %cross.5.refs_2_, ...), custom_call_target="tpu_custom_call" | custom-call | flops 268435456 | bytes 1048576 | tf_op jit(solution)/shard_map/part/pallas_call | solution.py:459
  16.2 3.7 %collective-permute-done.6.rest_4_ = bf16[8,32,512]{2,1,0:T(8,128)(2,1)S(1)} collective-permute-done((bf16[8,32,512]{2,1,0:T(8,128)(2,1)S(1)}, bf16[8,32,512]{2,1,0:T(8,128)(2,1)S(1)}, u32[]{:S(2)}, u32[]{:S(2)}) %collective-permute-start.6) | collective-permute-done | bytes 262176 | tf_op jit(solution)/shard_map/ppermute | solution.py:419
  19.9 1.2 %lags.2.rest_0_ = bf16[8,64,512]{2,1,0:T(8,128)(2,1)} custom-call(bf16[512,512]{1,0:T(8,128)(2,1)S(1)} %inverse.1.table_ref, bf16[8,32,512]{2,1,0:T(8,128)(2,1)S(1)} %get-tuple-element.27.after_ref.refs_0_.rest_0_, bf16[8,32,512]{2,1,0:T(8,128)(2,1)S(1)} %get-tuple-element.28.after_ref.refs_1_.rest_1_, bf16[8,32,512]{2,1,0:T(8,128)(2,1)S(1)} %get-tuple-element.34.rest_2_, ...), custom_call_target="tpu_custom_call" | custom-call | flops 268435456 | bytes 1048576 | tf_op jit(solution)/shard_map/lags/pallas_call | solution.py:443
  21.1 3.1 %collective-permute-done.4.more_ref = bf16[8,32,512]{2,1,0:T(8,128)(2,1)S(1)} collective-permute-done((bf16[8,32,512]{2,1,0:T(8,128)(2,1)S(1)}, bf16[8,32,512]{2,1,0:T(8,128)(2,1)S(1)}, u32[]{:S(2)}, u32[]{:S(2)}) %collective-permute-start.4) | collective-permute-done | bytes 262176 | tf_op jit(solution)/shard_map/ppermute | solution.py:419
  24.2 1.0 %lags.3 = bf16[8,64,512]{2,1,0:T(8,128)(2,1)} custom-call(bf16[512,512]{1,0:T(8,128)(2,1)S(1)} %inverse.1.table_ref, f32[256,512]{1,0:T(8,128)S(1)} %part.1.rest_5_.part_ref, bf16[8,32,512]{2,1,0:T(8,128)(2,1)S(1)} %collective-permute-done.4.more_ref, bf16[8,64,512]{2,1,0:T(8,128)(2,1)} %lags.2.rest_0_), custom_call_target="tpu_custom_call", output_to_operand_aliasing={{}: (3, {})} | custom-call | flops 268435456 | bytes 1048576 | tf_op jit(solution)/shard_map/lags/pallas_call | solution.py:443
  (4 shorter events, 0.1 us)
Async XLA Ops:
  0.0 2.9 %copy-start = (bf16[64,8,512]{2,1,0:T(8,128)(2,1)S(1)}, bf16[64,8,512]{2,1,0:T(8,128)(2,1)}, u32[]{:S(2)}) copy-start(bf16[64,8,512]{2,1,0:T(8,128)(2,1)} %param.3) | copy-start | bytes 1572868
  1.5 6.1 %collective-permute-start = (bf16[32,4096]{1,0:T(8,128)(2,1)S(1)}, bf16[32,4096]{1,0:T(8,128)(2,1)S(1)}, u32[]{:S(2)}, u32[]{:S(2)}) collective-permute-start(bf16[32,4096]{1,0:T(8,128)(2,1)S(1)} %get-tuple-element.24.edge_ref), channel_id=1, source_target_pairs={{4,0},{5,1},{6,2},{7,3},{8,4},{9,5},{12,8},{13,9},{14,10},{15,11},... | collective-permute-start | bytes 786440 | tf_op jit(solution)/shard_map/ppermute | solution.py:372
  4.2 7.3 %collective-permute-start.5 = (bf16[8,32,512]{2,1,0:T(8,128)(2,1)S(1)}, bf16[8,32,512]{2,1,0:T(8,128)(2,1)S(1)}, u32[]{:S(2)}, u32[]{:S(2)}) collective-permute-start(bf16[8,32,512]{2,1,0:T(8,128)(2,1)S(1)} %get-tuple-element.27.after_ref.refs_0_.rest_0_), channel_id=1, source_target_pairs={{0,1},{1,0},{2,3},{4,6},{5,7},{8,9},{9,8},{10,11},{12,14},{13,15},... | collective-permute-start | bytes 786440 | tf_op jit(solution)/shard_map/ppermute | solution.py:419
  6.3 6.6 %collective-permute-start.1 = (bf16[32,4096]{1,0:T(8,128)(2,1)S(1)}, bf16[32,4096]{1,0:T(8,128)(2,1)S(1)}, u32[]{:S(2)}, u32[]{:S(2)}) collective-permute-start(bf16[32,4096]{1,0:T(8,128)(2,1)S(1)} %get-tuple-element.31), channel_id=1, source_target_pairs={{10,6},{11,7},{18,14},{19,15},{26,22},{27,23}} | collective-permute-start | bytes 786440 | tf_op jit(solution)/shard_map/ppermute | solution.py:372
  8.4 4.5 %collective-permute-start.2 = (bf16[8,32,512]{2,1,0:T(8,128)(2,1)S(1)}, bf16[8,32,512]{2,1,0:T(8,128)(2,1)S(1)}, u32[]{:S(2)}, u32[]{:S(2)}) collective-permute-start(bf16[8,32,512]{2,1,0:T(8,128)(2,1)S(1)} %cross.3._.after_ref.refs_0_.refs_3_), channel_id=1, source_target_pairs={{0,1},{1,0},{4,6},{5,7},{8,9},{9,8},{12,14},{13,15},{16,17},{17,16... | collective-permute-start | bytes 786440 | tf_op jit(solution)/shard_map/ppermute | solution.py:419
  9.1 6.6 %collective-permute-start.3 = (bf16[8,32,512]{2,1,0:T(8,128)(2,1)S(1)}, bf16[8,32,512]{2,1,0:T(8,128)(2,1)S(1)}, u32[]{:S(2)}, u32[]{:S(2)}) collective-permute-start(bf16[8,32,512]{2,1,0:T(8,128)(2,1)S(1)} %cross.3._.after_ref.refs_0_.refs_3_), channel_id=1, source_target_pairs={{2,3},{10,11},{18,19},{26,27}} | collective-permute-start | bytes 786440 | tf_op jit(solution)/shard_map/ppermute | solution.py:419
  11.6 8.3 %collective-permute-start.6 = (bf16[8,32,512]{2,1,0:T(8,128)(2,1)S(1)}, bf16[8,32,512]{2,1,0:T(8,128)(2,1)S(1)}, u32[]{:S(2)}, u32[]{:S(2)}) collective-permute-start(bf16[8,32,512]{2,1,0:T(8,128)(2,1)S(1)} %mix.3), channel_id=1, source_target_pairs={{0,2},{1,3},{4,5},{6,7},{7,6},{8,10},{9,11},{12,13},{14,15},{15,14... | collective-permute-start | bytes 786440 | tf_op jit(solution)/shard_map/ppermute | solution.py:419
  13.1 11.1 %collective-permute-start.4 = (bf16[8,32,512]{2,1,0:T(8,128)(2,1)S(1)}, bf16[8,32,512]{2,1,0:T(8,128)(2,1)S(1)}, u32[]{:S(2)}, u32[]{:S(2)}) collective-permute-start(bf16[8,32,512]{2,1,0:T(8,128)(2,1)S(1)} %mix.2.after_ref), channel_id=1, source_target_pairs={{0,2},{1,3},{4,5},{6,7},{7,6},{8,10},{9,11},{12,13},{14,15},{15,14... | collective-permute-start | bytes 786440 | tf_op jit(solution)/shard_map/ppermute | solution.py:419

commit v13 on v12

--- a/solution.py
+++ b/solution.py
@@ -209,8 +209,12 @@
     rows = slice(span * wins, 2 * span * wins)
 
     if now == 0:
-        rest[0][...] = edge_ref[...]
-        rest = rest[1:]
+        again_ref, *rest = rest
+
+        @pl.when(lax.axis_index("tm") >= min(limits))
+        def _():
+            again_ref[...] = edge_ref[...]
+
     raw_ref, near_ref, *parts_refs = rest
 
     @pl.when(role(limits) == now)
@@ -283,29 +287,37 @@
 
 
 def lag_kernel(limits, scale, first, weights, table_ref, *rest):
-    out_hbm, stage_ref, sem = rest[-3:]
+    out_hbm, stage_ref, sems = rest[-3:]
     place = whereabouts(len(weights[0]) // 2)
     pairs, rows, length = stage_ref.shape
     stack = weighted(limits, rest[: len(weights) + 2], weights, place)
     stack = stack.reshape(pairs * rows, length)
     lagged = to_lags(stack, table_ref[...]) * scale
     stage_ref[...] = lagged.astype(stage_ref.dtype).reshape(pairs, rows, length)
-    copy = pltpu.make_async_copy(stage_ref, out_hbm.at[:, pl.ds(first, rows)], sem)
+    copy = pltpu.make_async_copy(stage_ref, out_hbm.at[:, pl.ds(first, rows)], sems.at[0])
     copy.start()
     copy.wait()
 
 
 def last_kernel(scale, first, weights, table_ref, part_ref, more_ref, *rest):
-    out_hbm, stage_ref, sem = rest[-3:]
+    out_hbm, stage_ref, sems = rest[-3:]
     place = whereabouts(len(weights) // 2)
     pairs, rows, length = stage_ref.shape
     more = more_ref[...].reshape(pairs * rows, length)
     lagged = jnp.dot(more, table_ref[...], preferred_element_type=jnp.float32)
-    lagged = (part_ref[...] + lagged * chosen(weights, place)) * scale
-    stage_ref[...] = lagged.astype(stage_ref.dtype).reshape(pairs, rows, length)
-    copy = pltpu.make_async_copy(stage_ref, out_hbm.at[:, pl.ds(first, rows)], sem)
-    copy.start()
-    copy.wait()
+    weight = chosen(weights, place)
+    size = pairs // 2
+    copies = []
+    for piece in range(2):
+        here = slice(piece * size * rows, (piece + 1) * size * rows)
+        value = (part_ref[here] + lagged[here] * weight) * scale
+        there = pl.ds(piece * size, size)
+        stage_ref[there] = value.astype(stage_ref.dtype).reshape(size, rows, length)
+        target = out_hbm.at[there, pl.ds(first, rows)]
+        copies.append(pltpu.make_async_copy(stage_ref.at[there], target, sems.at[piece]))
+        copies[-1].start()
+    for copy in copies:
+        copy.wait()
 
 
 def cost(flops, moved):
@@ -447,7 +459,7 @@
             out_specs=whole(pl.ANY),
             scratch_shapes=[
                 pltpu.VMEM((pairs, span, length), jnp.bfloat16),
-                pltpu.SemaphoreType.DMA,
+                pltpu.SemaphoreType.DMA((2,)),
             ],
             input_output_aliases={1 + len(terms) + len(later): 0} if so_far else {},
             compiler_params=params,

time: 25.6 us -> 25.6 us (level)
  no operation moved by 1% of the time
where the time goes in v13:
time: 25.6 us; the launch traced here: 25.2 us
  starting transfers between devices  10.4 us (41%)
  waiting for transfers between devices  7.82 us (31%)
  Pallas kernels  6.86 us (27%)
    ppermute x5, waiting for transfers between devices, sent(): return lax.ppermute(value, ('chan', 'tm'), moves)  7.82 us
    ppermute x5, starting transfers between devices, sent(): return lax.ppermute(value, ('chan', 'tm'), moves)  7.76 us
    ppermute x2, starting transfers between devices, to_previous(): return lax.ppermute(value, ('chan', 'tm'), moves)  2.6 us
    pallas_call x2, Pallas kernels, written(): pl.pallas_call(kernel, out_shape=jax.ShapeDtypeStruct((pairs, chans, leng...  2.16 us
    pallas_call x1, Pallas kernels, per_device(): pl.pallas_call(head_kernel, out_shape=(white_type, short_type, jax.ShapeD...  1.54 us
    pallas_call x3, Pallas kernels, tail(): pl.pallas_call(functools.partial(tail_kernel, limits, now), out_shape=(wh...  1.36 us
    pallas_call x3, Pallas kernels, cross(): pl.pallas_call(functools.partial(cross_kernel, limits, now), out_shape=lo...  0.82 us
  transfers between devices with their start and end apart: 7, of which 3 were waited for; matrix products, arithmetic and copies ran while one was open for 0% of the time, Pallas kernels for 17%

profile of v13, /device:TPU:28, one launch (start us, length us, event | category | flops | bytes accessed | tf_op | source)
XLA Modules:
  0.0 25.2 jit_solution(2838451344162244089)
XLA Ops:
  0.0 0.0 copy-start
  0.0 1.5 %head.1 = (f32[8,32,512]{2,1,0:T(8,128)S(1)}, bf16[32,4096]{1,0:T(8,128)(2,1)S(1)}, bf16[512,512]{1,0:T(8,128)(2,1)S(1)}, bf16[8,32,64]{2,1,0:T(8,128)(2,1)S(1)}, f32[64,1024]{1,0:T(8,128)S(1)}) custom-call(bf16[512,512]{1,0:T(8,128)(2,1)} %bitcast.3, s32[8,64]{1,0:T(8,128)} %bitcast.7, s32[8]{0:T(128)} %offsets_hbm.1), custom_call_target="tpu_custom_call" | custom-call | flops 134217728 | bytes 2097152 | tf_op jit(solution)/shard_map/head/pallas_call | solution.py:353
  1.5 1.3 %collective-permute-start = (bf16[32,4096]{1,0:T(8,128)(2,1)S(1)}, bf16[32,4096]{1,0:T(8,128)(2,1)S(1)}, u32[]{:S(2)}, u32[]{:S(2)}) collective-permute-start(bf16[32,4096]{1,0:T(8,128)(2,1)S(1)} %get-tuple-element.24.edge_ref), channel_id=1, source_target_pairs={{4,0},{5,1},{6,2},{7,3},{8,4},{9,5},{12,8},{13,9},{14,10},{15,11},... | collective-permute-start | bytes 786440 | tf_op jit(solution)/shard_map/ppermute | solution.py:384
  2.8 0.0 copy-done
  2.9 1.3 %tail.3 = (f32[8,32,512]{2,1,0:T(8,128)S(1)}, bf16[32,4096]{1,0:T(8,128)(2,1)S(1)}, bf16[8,32,512]{2,1,0:T(8,128)(2,1)S(1)}, bf16[32,4096]{1,0:T(8,128)(2,1)S(1)}) custom-call(bf16[512,512]{1,0:T(8,128)(2,1)S(1)} %bitcast.4, bf16[512,512]{1,0:T(8,128)(2,1)S(1)} %get-tuple-element.21.table_ref.after_ref, f32[64,1024]{1,0:T(8,128)S(1)} %get-tuple-element.22.keep_ref, ...), custom_call_target="tpu_custom_call" | custom-call | flops 268435456 | bytes 4194304 | tf_op jit(solution)/shard_map/tail/pallas_call | solution.py:395
  4.2 2.1 %collective-permute-start.5 = (bf16[8,32,512]{2,1,0:T(8,128)(2,1)S(1)}, bf16[8,32,512]{2,1,0:T(8,128)(2,1)S(1)}, u32[]{:S(2)}, u32[]{:S(2)}) collective-permute-start(bf16[8,32,512]{2,1,0:T(8,128)(2,1)S(1)} %get-tuple-element.27.after_ref.refs_0_.rest_0_), channel_id=1, source_target_pairs={{0,1},{1,0},{2,3},{4,6},{5,7},{8,9},{9,8},{10,11},{12,14},{13,15},... | collective-permute-start | bytes 786440 | tf_op jit(solution)/shard_map/ppermute | solution.py:431
  6.3 1.3 %collective-permute-start.1 = (bf16[32,4096]{1,0:T(8,128)(2,1)S(1)}, bf16[32,4096]{1,0:T(8,128)(2,1)S(1)}, u32[]{:S(2)}, u32[]{:S(2)}) collective-permute-start(bf16[32,4096]{1,0:T(8,128)(2,1)S(1)} %get-tuple-element.31), channel_id=1, source_target_pairs={{10,6},{11,7},{18,14},{19,15},{26,22},{27,23}} | collective-permute-start | bytes 786440 | tf_op jit(solution)/shard_map/ppermute | solution.py:384
  7.7 0.0 collective-permute-done.edge_ref
  7.7 0.8 %cross.3._.after_ref.refs_0_.refs_3_ = bf16[8,32,512]{2,1,0:T(8,128)(2,1)S(1)} custom-call(bf16[8,32,64]{2,1,0:T(8,128)(2,1)S(1)} %get-tuple-element.20.pick_ref, f32[8,32,512]{2,1,0:T(8,128)S(1)} %get-tuple-element.25.white_ref, bf16[32,4096]{1,0:T(8,128)(2,1)S(1)} %get-tuple-element.26.short_ref, bf16[32,4096]{1,0:T(8,128)(2,1)S(1)} %collective-permute-done.edge_ref, ...), custom_call_target="tpu_custom_call" | custom-call | flops 4194304 | bytes 4194304 | tf_op jit(solution)/shard_map/cross/pallas_call | solution.py:407
  8.5 0.7 %collective-permute-start.2 = (bf16[8,32,512]{2,1,0:T(8,128)(2,1)S(1)}, bf16[8,32,512]{2,1,0:T(8,128)(2,1)S(1)}, u32[]{:S(2)}, u32[]{:S(2)}) collective-permute-start(bf16[8,32,512]{2,1,0:T(8,128)(2,1)S(1)} %cross.3._.after_ref.refs_0_.refs_3_), channel_id=1, source_target_pairs={{0,1},{1,0},{4,6},{5,7},{8,9},{9,8},{12,14},{13,15},{16,17},{17,16... | collective-permute-start | bytes 786440 | tf_op jit(solution)/shard_map/ppermute | solution.py:431
  9.2 2.4 %collective-permute-start.3 = (bf16[8,32,512]{2,1,0:T(8,128)(2,1)S(1)}, bf16[8,32,512]{2,1,0:T(8,128)(2,1)S(1)}, u32[]{:S(2)}, u32[]{:S(2)}) collective-permute-start(bf16[8,32,512]{2,1,0:T(8,128)(2,1)S(1)} %cross.3._.after_ref.refs_0_.refs_3_), channel_id=1, source_target_pairs={{2,3},{10,11},{18,19},{26,27}} | collective-permute-start | bytes 786440 | tf_op jit(solution)/shard_map/ppermute | solution.py:431
  11.5 0.0 collective-permute-done.5.refs_2_.rest_3_
  11.5 0.1 mix.3
  11.7 1.3 %collective-permute-start.6 = (bf16[8,32,512]{2,1,0:T(8,128)(2,1)S(1)}, bf16[8,32,512]{2,1,0:T(8,128)(2,1)S(1)}, u32[]{:S(2)}, u32[]{:S(2)}) collective-permute-start(bf16[8,32,512]{2,1,0:T(8,128)(2,1)S(1)} %mix.3), channel_id=1, source_target_pairs={{0,2},{1,3},{4,5},{6,7},{7,6},{8,10},{9,11},{12,13},{14,15},{15,14... | collective-permute-start | bytes 786440 | tf_op jit(solution)/shard_map/ppermute | solution.py:431
  13.0 0.0 collective-permute-done.1.edge_ref
  13.0 0.0 collective-permute-done.2.refs_2_.refs_3_
  13.0 0.1 mix.2.after_ref
  13.1 1.3 %collective-permute-start.4 = (bf16[8,32,512]{2,1,0:T(8,128)(2,1)S(1)}, bf16[8,32,512]{2,1,0:T(8,128)(2,1)S(1)}, u32[]{:S(2)}, u32[]{:S(2)}) collective-permute-start(bf16[8,32,512]{2,1,0:T(8,128)(2,1)S(1)} %mix.2.after_ref), channel_id=1, source_target_pairs={{0,2},{1,3},{4,5},{6,7},{7,6},{8,10},{9,11},{12,13},{14,15},{15,14... | collective-permute-start | bytes 786440 | tf_op jit(solution)/shard_map/ppermute | solution.py:431
  14.4 0.3 %inverse.1.table_ref = bf16[512,512]{1,0:T(8,128)(2,1)S(1)} custom-call(bf16[8,32,512]{2,1,0:T(8,128)(2,1)S(1)} %cross.3._.after_ref.refs_0_.refs_3_), custom_call_target="tpu_custom_call" | custom-call | flops 4194304 | bytes 524288 | tf_op jit(solution)/shard_map/inverse/pallas_call | solution.py:444
  14.8 0.9 %collective-permute-done.3.refs_4_ = bf16[8,32,512]{2,1,0:T(8,128)(2,1)S(1)} collective-permute-done((bf16[8,32,512]{2,1,0:T(8,128)(2,1)S(1)}, bf16[8,32,512]{2,1,0:T(8,128)(2,1)S(1)}, u32[]{:S(2)}, u32[]{:S(2)}) %collective-permute-start.3) | collective-permute-done | bytes 262176 | tf_op jit(solution)/shard_map/ppermute | solution.py:431
  15.7 0.4 %part.1.rest_5_.part_ref = f32[256,512]{1,0:T(8,128)S(1)} custom-call(bf16[512,512]{1,0:T(8,128)(2,1)S(1)} %inverse.1.table_ref, bf16[8,32,512]{2,1,0:T(8,128)(2,1)S(1)} %cross.3._.after_ref.refs_0_.refs_3_, bf16[8,32,512]{2,1,0:T(8,128)(2,1)S(1)} %cross.4.refs_1_, bf16[8,32,512]{2,1,0:T(8,128)(2,1)S(1)} %cross.5.refs_2_, ...), custom_call_target="tpu_custom_call" | custom-call | flops 268435456 | bytes 1048576 | tf_op jit(solution)/shard_map/part/pallas_call | solution.py:471
  16.2 3.7 %collective-permute-done.6.rest_4_ = bf16[8,32,512]{2,1,0:T(8,128)(2,1)S(1)} collective-permute-done((bf16[8,32,512]{2,1,0:T(8,128)(2,1)S(1)}, bf16[8,32,512]{2,1,0:T(8,128)(2,1)S(1)}, u32[]{:S(2)}, u32[]{:S(2)}) %collective-permute-start.6) | collective-permute-done | bytes 262176 | tf_op jit(solution)/shard_map/ppermute | solution.py:431
  19.9 1.2 %lags.2.rest_0_ = bf16[8,64,512]{2,1,0:T(8,128)(2,1)} custom-call(bf16[512,512]{1,0:T(8,128)(2,1)S(1)} %inverse.1.table_ref, bf16[8,32,512]{2,1,0:T(8,128)(2,1)S(1)} %get-tuple-element.27.after_ref.refs_0_.rest_0_, bf16[8,32,512]{2,1,0:T(8,128)(2,1)S(1)} %get-tuple-element.28.after_ref.refs_1_.rest_1_, bf16[8,32,512]{2,1,0:T(8,128)(2,1)S(1)} %get-tuple-element.34.rest_2_, ...), custom_call_target="tpu_custom_call" | custom-call | flops 268435456 | bytes 1048576 | tf_op jit(solution)/shard_map/lags/pallas_call | solution.py:455
  21.1 3.1 %collective-permute-done.4.more_ref = bf16[8,32,512]{2,1,0:T(8,128)(2,1)S(1)} collective-permute-done((bf16[8,32,512]{2,1,0:T(8,128)(2,1)S(1)}, bf16[8,32,512]{2,1,0:T(8,128)(2,1)S(1)}, u32[]{:S(2)}, u32[]{:S(2)}) %collective-permute-start.4) | collective-permute-done | bytes 262176 | tf_op jit(solution)/shard_map/ppermute | solution.py:431
  24.2 1.0 %lags.3 = bf16[8,64,512]{2,1,0:T(8,128)(2,1)} custom-call(bf16[512,512]{1,0:T(8,128)(2,1)S(1)} %inverse.1.table_ref, f32[256,512]{1,0:T(8,128)S(1)} %part.1.rest_5_.part_ref, bf16[8,32,512]{2,1,0:T(8,128)(2,1)S(1)} %collective-permute-done.4.more_ref, bf16[8,64,512]{2,1,0:T(8,128)(2,1)} %lags.2.rest_0_), custom_call_target="tpu_custom_call", output_to_operand_aliasing={{}: (3, {})} | custom-call | flops 268435456 | bytes 1048576 | tf_op jit(solution)/shard_map/lags/pallas_call | solution.py:455
  (4 shorter events, 0.1 us)
Async XLA Ops:
  0.0 2.9 %copy-start = (bf16[64,8,512]{2,1,0:T(8,128)(2,1)S(1)}, bf16[64,8,512]{2,1,0:T(8,128)(2,1)}, u32[]{:S(2)}) copy-start(bf16[64,8,512]{2,1,0:T(8,128)(2,1)} %param.3) | copy-start | bytes 1572868
  1.5 6.1 %collective-permute-start = (bf16[32,4096]{1,0:T(8,128)(2,1)S(1)}, bf16[32,4096]{1,0:T(8,128)(2,1)S(1)}, u32[]{:S(2)}, u32[]{:S(2)}) collective-permute-start(bf16[32,4096]{1,0:T(8,128)(2,1)S(1)} %get-tuple-element.24.edge_ref), channel_id=1, source_target_pairs={{4,0},{5,1},{6,2},{7,3},{8,4},{9,5},{12,8},{13,9},{14,10},{15,11},... | collective-permute-start | bytes 786440 | tf_op jit(solution)/shard_map/ppermute | solution.py:384
  4.2 7.3 %collective-permute-start.5 = (bf16[8,32,512]{2,1,0:T(8,128)(2,1)S(1)}, bf16[8,32,512]{2,1,0:T(8,128)(2,1)S(1)}, u32[]{:S(2)}, u32[]{:S(2)}) collective-permute-start(bf16[8,32,512]{2,1,0:T(8,128)(2,1)S(1)} %get-tuple-element.27.after_ref.refs_0_.rest_0_), channel_id=1, source_target_pairs={{0,1},{1,0},{2,3},{4,6},{5,7},{8,9},{9,8},{10,11},{12,14},{13,15},... | collective-permute-start | bytes 786440 | tf_op jit(solution)/shard_map/ppermute | solution.py:431
  6.3 6.6 %collective-permute-start.1 = (bf16[32,4096]{1,0:T(8,128)(2,1)S(1)}, bf16[32,4096]{1,0:T(8,128)(2,1)S(1)}, u32[]{:S(2)}, u32[]{:S(2)}) collective-permute-start(bf16[32,4096]{1,0:T(8,128)(2,1)S(1)} %get-tuple-element.31), channel_id=1, source_target_pairs={{10,6},{11,7},{18,14},{19,15},{26,22},{27,23}} | collective-permute-start | bytes 786440 | tf_op jit(solution)/shard_map/ppermute | solution.py:384
  8.5 4.5 %collective-permute-start.2 = (bf16[8,32,512]{2,1,0:T(8,128)(2,1)S(1)}, bf16[8,32,512]{2,1,0:T(8,128)(2,1)S(1)}, u32[]{:S(2)}, u32[]{:S(2)}) collective-permute-start(bf16[8,32,512]{2,1,0:T(8,128)(2,1)S(1)} %cross.3._.after_ref.refs_0_.refs_3_), channel_id=1, source_target_pairs={{0,1},{1,0},{4,6},{5,7},{8,9},{9,8},{12,14},{13,15},{16,17},{17,16... | collective-permute-start | bytes 786440 | tf_op jit(solution)/shard_map/ppermute | solution.py:431
  9.2 6.6 %collective-permute-start.3 = (bf16[8,32,512]{2,1,0:T(8,128)(2,1)S(1)}, bf16[8,32,512]{2,1,0:T(8,128)(2,1)S(1)}, u32[]{:S(2)}, u32[]{:S(2)}) collective-permute-start(bf16[8,32,512]{2,1,0:T(8,128)(2,1)S(1)} %cross.3._.after_ref.refs_0_.refs_3_), channel_id=1, source_target_pairs={{2,3},{10,11},{18,19},{26,27}} | collective-permute-start | bytes 786440 | tf_op jit(solution)/shard_map/ppermute | solution.py:431
  11.7 8.3 %collective-permute-start.6 = (bf16[8,32,512]{2,1,0:T(8,128)(2,1)S(1)}, bf16[8,32,512]{2,1,0:T(8,128)(2,1)S(1)}, u32[]{:S(2)}, u32[]{:S(2)}) collective-permute-start(bf16[8,32,512]{2,1,0:T(8,128)(2,1)S(1)} %mix.3), channel_id=1, source_target_pairs={{0,2},{1,3},{4,5},{6,7},{7,6},{8,10},{9,11},{12,13},{14,15},{15,14... | collective-permute-start | bytes 786440 | tf_op jit(solution)/shard_map/ppermute | solution.py:431
  13.1 11.1 %collective-permute-start.4 = (bf16[8,32,512]{2,1,0:T(8,128)(2,1)S(1)}, bf16[8,32,512]{2,1,0:T(8,128)(2,1)S(1)}, u32[]{:S(2)}, u32[]{:S(2)}) collective-permute-start(bf16[8,32,512]{2,1,0:T(8,128)(2,1)S(1)} %mix.2.after_ref), channel_id=1, source_target_pairs={{0,2},{1,3},{4,5},{6,7},{7,6},{8,10},{9,11},{12,13},{14,15},{15,14... | collective-permute-start | bytes 786440 | tf_op jit(solution)/shard_map/ppermute | solution.py:431
